TPU v7x, 128 devices: a whole 4x4x4 slice. The times are simulated.
128 devices in a mesh: dp: 8 (over z_lo, x), seq: 16 (over y, z_hi, core).
Axes of the slice: x: 4, y: 4, z: 4 (z_hi: 2, z_lo: 2; z = z_hi * 2 + z_lo), core: 2. Of those that a mesh axis runs over, the one named last changes fastest.
Arguments:
- item_table: float32 [4096, 512], P('dp'), may hold values from -40 to 40
- serve_lists: int32 [8, 8, 16, 128], P('dp', None, 'seq'), may hold values from 0 to 511, as said below
- event_slots: int32 [8, 2, 4096], P('dp', None, 'seq'), may hold values from 0 to 1023, as said below
- session_tiles: int32 [8, 32, 32], P('dp', 'seq'), may hold values from 0 to 1, as said below
- w_query: float32 [512, 512], replicated, may hold values from -1 to 1
- w_key: float32 [512, 512], replicated, may hold values from -1 to 1
- w_value: float32 [512, 512], replicated, may hold values from -0.25 to 0.25
- w_out: float32 [512, 512], replicated, may hold values from -0.25 to 0.25
- grad_attended: float32 [8, 4096, 512], P('dp', 'seq'), may hold values from -6 to 6
Outputs:
- attended: float32 [8, 4096, 512], P('dp', 'seq')
- grad_query_w: float32 [512, 512], replicated
- grad_key_w: float32 [512, 512], replicated
- grad_value_w: float32 [512, 512], replicated
- grad_out_w: float32 [512, 512], replicated
- grad_table: float32 [4096, 512], P(('dp', 'seq'))
Inputs may be any that keep to these rules, and one draw needn't show every extreme that they name: `serve_lists`: within each list of 128 the entries are distinct rows of the owner's shard. `event_slots`: A slot s names entry s % 128 of the list that shard s // 128 serves to the event's device. On every device, for some shard, all 128 entries of its list are named by events. `session_tiles`: tile (i, i) is 1 for every i.
All inputs are finite; a program needn't handle non-finite values.
Results may differ from a plain program's by a relative error of at most 0.0003.
Values sent between devices are 32-bit elements; how exact they have to be, the bound alone decides.
No kernel may reach another device: no remote copies, remote signals or barrier semaphores. Data moves between devices by JAX's collectives and lax.ppermute only.
A program may use at most 192 MiB of HBM per device.

v0:
```python
import math

import jax
import jax.numpy as jnp
from jax import lax
from jax.sharding import PartitionSpec as P

HEADS = 8
HEAD_DIM = 64
TILE = 128


HIGH = lax.Precision.HIGHEST
NEGATIVE = -1e30


def product(left, right):
    return jnp.dot(left, right, precision=HIGH, preferred_element_type=jnp.float32)


def block_mask(tile_rows, index, span_tiles):
    picked = lax.dynamic_slice_in_dim(tile_rows, index * span_tiles, span_tiles, 1)
    query_tiles = tile_rows.shape[0]
    spread = jnp.broadcast_to(picked[:, None, :, None], (query_tiles, TILE, span_tiles, TILE))
    return (picked, spread.reshape(query_tiles * TILE, span_tiles * TILE) > 0)


def on_device(
    item_table,
    serve_lists,
    event_slots,
    session_tiles,
    w_query,
    w_key,
    w_value,
    w_out,
    grad_attended,
):
    width = item_table.shape[1]
    lists = serve_lists[0, :, 0, :]
    served = item_table[lists]
    arrived = lax.all_to_all(served, "dp", split_axis=0, concat_axis=0, tiled=True)
    slot_rows = arrived.reshape(-1, width)
    slots = event_slots[0]
    inputs = slot_rows[slots[0]] + slot_rows[slots[1]]
    rows_here = inputs.shape[0]
    scale = HEAD_DIM ** (-0.5)
    queries = product(inputs, w_query)
    keys_here = product(inputs, w_key)
    values_here = product(inputs, w_value)
    keys_all, values_all = (
        lax.all_gather(keys_here, "seq", axis=0, tiled=True),
        lax.all_gather(values_here, "seq", axis=0, tiled=True),
    )
    history = keys_all.shape[0]
    span_tiles = math.gcd(history // TILE, max(1, 512 // TILE))
    span = span_tiles * TILE
    block_count = history // span
    tiles = session_tiles[0]
    query_heads = queries.reshape(rows_here, HEADS, HEAD_DIM)
    indices = jnp.arange(block_count, dtype=jnp.int32)

    def scores_for(index):
        picked, mask = block_mask(tiles, index, span_tiles)
        block_keys = lax.dynamic_slice_in_dim(keys_all, index * span, span, 0).reshape(
            span, HEADS, HEAD_DIM
        )
        block_values = lax.dynamic_slice_in_dim(values_all, index * span, span, 0).reshape(
            span, HEADS, HEAD_DIM
        )
        scores = jnp.einsum("qhd,khd->hqk", query_heads, block_keys, precision=HIGH) * scale
        return (mask, block_keys, block_values, jnp.where(mask[None], scores, NEGATIVE))

    def forward_step(carry, index):
        peak, total, accum = carry
        mask, block_keys, block_values, scores = scores_for(index)
        raised = jnp.maximum(peak, jnp.max(scores, axis=2))
        factor = jnp.exp(peak - raised)
        weights = jnp.exp(scores - raised[:, :, None]) * mask[None]
        total = total * factor + jnp.sum(weights, axis=2)
        accum = accum * factor[:, :, None] + jnp.einsum(
            "hqk,khd->hqd", weights, block_values, precision=HIGH
        )
        state = (raised, total, accum)
        return (state, None)

    start_state = (
        jnp.full((HEADS, rows_here), NEGATIVE, jnp.float32),
        jnp.zeros((HEADS, rows_here), jnp.float32),
        jnp.zeros((HEADS, rows_here, HEAD_DIM), jnp.float32),
    )
    (peak, total, accum), _ = lax.scan(forward_step, start_state, indices)
    log_total = peak + jnp.log(total)
    context_heads = (accum / total[:, :, None]).transpose(1, 0, 2)
    context = context_heads.reshape(rows_here, width)
    attended = product(context, w_out)
    cotangent = grad_attended[0]
    grad_out_w = product(context.T, cotangent)
    grad_context = product(cotangent, w_out.T).reshape(rows_here, HEADS, HEAD_DIM)
    delta = jnp.sum(grad_context * context_heads, axis=2).T

    def backward_step(carry, index):
        grad_queries = carry
        mask, block_keys, block_values, scores = scores_for(index)
        probs = jnp.exp(scores - log_total[:, :, None]) * mask[None]
        grad_values = jnp.einsum("hqk,qhd->khd", probs, grad_context, precision=HIGH)
        grad_probs = jnp.einsum("qhd,khd->hqk", grad_context, block_values, precision=HIGH)
        grad_scores = probs * (grad_probs - delta[:, :, None])
        grad_queries = (
            grad_queries
            + jnp.einsum("hqk,khd->qhd", grad_scores, block_keys, precision=HIGH) * scale
        )
        grad_keys = jnp.einsum("hqk,qhd->khd", grad_scores, query_heads, precision=HIGH) * scale
        terms = jnp.concatenate(
            [grad_keys.reshape(span, width), grad_values.reshape(span, width)], axis=1
        )
        return (grad_queries, terms)

    grad_queries, key_terms = lax.scan(
        backward_step, jnp.zeros((rows_here, HEADS, HEAD_DIM), jnp.float32), indices
    )
    key_terms = key_terms.reshape(history, 2 * width)
    grad_queries = grad_queries.reshape(rows_here, width)
    grad_query_w = product(inputs.T, grad_queries)
    summed = lax.psum_scatter(key_terms, "seq", scatter_dimension=0, tiled=True)
    grad_keys = summed[:, :width]
    grad_values = summed[:, width:]
    grad_key_w = product(inputs.T, grad_keys)
    grad_value_w = product(inputs.T, grad_values)
    grad_inputs = (
        product(grad_queries, w_query.T)
        + product(grad_keys, w_key.T)
        + product(grad_values, w_value.T)
    )
    doubled = jnp.concatenate([grad_inputs, grad_inputs], axis=0)
    slot_grads = jax.ops.segment_sum(
        doubled, jnp.concatenate([slots[0], slots[1]]), num_segments=slot_rows.shape[0]
    )
    returned = lax.all_to_all(
        slot_grads.reshape(arrived.shape), "dp", split_axis=0, concat_axis=0, tiled=True
    )
    table_terms = jax.ops.segment_sum(
        returned.reshape(-1, width), lists.reshape(-1), num_segments=item_table.shape[0]
    )
    grad_table = lax.psum_scatter(table_terms, "seq", scatter_dimension=0, tiled=True)
    grad_query_w, grad_key_w, grad_value_w, grad_out_w = lax.psum(
        (grad_query_w, grad_key_w, grad_value_w, grad_out_w), ("dp", "seq")
    )
    return (attended[None], grad_query_w, grad_key_w, grad_value_w, grad_out_w, grad_table)


def solution(mesh):
    return jax.shard_map(
        on_device,
        mesh=mesh,
        in_specs=(
            P("dp", None),
            P("dp", None, "seq", None),
            P("dp", None, "seq"),
            P("dp", "seq", None),
            P(),
            P(),
            P(),
            P(),
            P("dp", "seq", None),
        ),
        out_specs=(P("dp", "seq", None), P(), P(), P(), P(), P(("dp", "seq"), None)),
        check_vma=False,
    )
```

profile of v0, /device:TPU:1, one launch (start us, length us, event | category | flops | bytes accessed | tf_op | source)
XLA Modules:
  0.0 1108.4 jit_solution(8127208061247333426)
XLA Ops:
  8.0 6.5 gather_fusion
  14.5 6.3 all-to-all-start
  20.9 26.9 %all-to-all-done = f32[8,128,512]{2,1,0:T(8,128)S(1)} async-done(((f32[8,128,512]{2,1,0:T(8,128)}), f32[8,128,512]{2,1,0:T(8,128)S(1)}, u32[]{:S(2)}, u32[]{:S(2)}) %all-to-all-start) | async-done | bytes 2097184 | tf_op jit(solution)/shard_map/all_to_all | solution.py:42
  62.4 69.8 %all-gather.3.cloned.1.call-done = f32[4096,512]{1,0:T(8,128)} async-done(((f32[256,512]{1,0:T(8,128)}), f32[4096,512]{1,0:T(8,128)}) %all-gather.3.cloned.1.call-update) | async-done | bytes 8388624 | tf_op jit(solution)/shard_map/all_gather | solution.py:52
  132.2 8.9 copy.36
  141.1 64.5 %all-gather.5.cloned.1.call-done = f32[4096,512]{1,0:T(8,128)} async-done(((f32[256,512]{1,0:T(8,128)}), f32[4096,512]{1,0:T(8,128)}) %all-gather.5.cloned.1.call-update) | async-done | bytes 8388624 | tf_op jit(solution)/shard_map/all_gather | solution.py:53
  205.6 8.9 copy.37
  214.5 152.9 %while.28 = (s32[]{:T(128)}, f32[8,256]{1,0:T(8,128)S(1)}, f32[8,256]{1,0:T(8,128)S(1)}, f32[8,256,64]{1,2,0:T(8,128)}, s32[8]{0:T(128)S(1)}, /*index=5*/s32[2,3...) while((s32[]{:T(128)}, f32[8,256]{1,0:T(8,128)S(1)}, ...), condition=%wide.region_3.4_spmd.clone, body=%wide.region_0.3_spmd.clone.sunk | while | flops 1623730176 | bytes 45220244 | solution.py:92
  218.7 6.5 fusion.110
  237.9 6.5 fusion.110
  257.0 6.5 fusion.110
  276.1 6.5 fusion.110
  295.2 6.5 fusion.110
  314.3 6.5 fusion.110
  333.4 6.5 fusion.110
  352.6 6.5 fusion.110
  370.6 338.3 %while.29 = (s32[]{:T(128)}, f32[256,8,64]{0,2,1:T(8,128)}, f32[8,512,1024]{2,1,0:T(8,128)}, s32[8]{0:T(128)S(1)}, f32[4096,512]{0,1:T(8,128)}, /*index=5*/s32[2...) while((s32[]{:T(128)}, f32[256,8,64]{0,2,1:T(8,128)}, ...), condition=%wide.region_6.7_spmd.clone, body=%wide.region_5.6_spmd.clone.sunk | while | flops 4038328320 | bytes 91644352 | solution.py:119
  373.7 6.2 fusion.124
  384.0 7.9 bitcast_multiply_fusion.3
  391.9 5.8 fusion.125
  402.8 5.2 convolution_multiply_fusion.3
  415.9 6.2 fusion.124
  426.1 7.9 bitcast_multiply_fusion.3
  434.0 5.9 fusion.125
  458.1 6.2 fusion.124
  468.4 7.9 bitcast_multiply_fusion.3
  476.2 5.9 fusion.125
  500.4 6.2 fusion.124
  510.6 7.9 bitcast_multiply_fusion.3
  518.5 5.9 fusion.125
  542.7 6.2 fusion.124
  553.0 7.9 bitcast_multiply_fusion.3
  560.8 5.9 fusion.125
  571.9 5.2 convolution_multiply_fusion.3
  585.0 6.2 fusion.124
  595.3 7.9 bitcast_multiply_fusion.3
  603.2 5.9 fusion.125
  627.3 6.2 fusion.124
  637.5 7.9 bitcast_multiply_fusion.3
  645.4 5.9 fusion.125
  669.5 6.2 fusion.124
  679.8 7.9 bitcast_multiply_fusion.3
  687.7 5.9 fusion.125
  718.9 134.1 %reduce-scatter.3.cloned.1.call-done = f32[256,1024]{1,0:T(8,128)} async-done(((f32[4096,1024]{1,0:T(8,128)}), f32[256,1024]{1,0:T(8,128)}) %reduce-scatter.3.cloned.1.call-update) | async-done | bytes 1048592 | tf_op jit(solution)/shard_map/reduce_scatter | solution.py:125
  869.2 34.5 %all_to_all.10 = f32[8,128,512]{2,1,0:T(8,128)} all-to-all(f32[8,128,512]{2,1,0:T(8,128)S(1)} %bitcast.210), channel_id=1, replica_groups=mesh['dp'=8,'seq'=16] {'dp'}, dimensions={0} | all-to-all | bytes 4194304 | tf_op jit(solution)/shard_map/all_to_all | solution.py:139
  903.8 8.3 scatter_custom_fusion.1
  914.9 112.0 %all-reduce.3.cloned.1.call-done = (f32[512,512]{1,0:T(8,128)}, f32[512,512]{1,0:T(8,128)}, f32[512,512]{1,0:T(8,128)}, f32[512,512]{1,0:T(8,128)}) async-done(((f32[512,512]{1,0:T(8,128)}, f32[512,512]{1,0:T(8,128)}, f32[512,512]{1,0:T(8,128)}, f32[512,512]{1,0:T(8,128)}), (f32[512,512]{1,0:T(8,128)}, f32[512,512]{1,0:T(8,128)}, f32[512,512]{1,0:T(8,128)}, ...) | async-done | bytes 4194320 | tf_op jit(solution)/shard_map/psum | solution.py:146
  1026.9 68.1 %reduce-scatter.5.cloned.1.call-done = f32[32,512]{1,0:T(8,128)} async-done(((f32[512,512]{1,0:T(8,128)}), f32[32,512]{1,0:T(8,128)}) %reduce-scatter.5.cloned.1.call-update) | async-done | bytes 65552 | tf_op jit(solution)/shard_map/reduce_scatter | solution.py:145
  (372 shorter events, 300.3 us)
Async XLA Ops:
  7.2 360.3 %copy-start = (f32[512,512]{1,0:T(8,128)S(1)}, f32[512,512]{1,0:T(8,128)}, u32[]{:S(2)}) copy-start(f32[512,512]{1,0:T(8,128)} %param.20) | copy-start | bytes 3145732
  14.5 6.4 copy-start.19
  14.5 33.4 %all-to-all-start = ((f32[8,128,512]{2,1,0:T(8,128)}), f32[8,128,512]{2,1,0:T(8,128)S(1)}, u32[]{:S(2)}, u32[]{:S(2)}) async-start(f32[8,128,512]{2,1,0:T(8,128)} %bitcast.209), calls=%async_computation | async-start | bytes 4194304 | tf_op jit(solution)/shard_map/all_to_all | solution.py:42
  20.8 111.4 %all-gather.3.cloned.1.call-start = ((), (), s32[]{:S(2)}) async-start(), calls=%async_computation.4 | async-start | bytes 8912896 | tf_op jit(solution)/shard_map/all_gather | solution.py:52
  51.4 8.4 copy-start.10
  52.7 88.4 %copy-start.6 = (f32[256,512]{1,0:T(8,128)}, f32[256,512]{1,0:T(8,128)S(1)}, u32[]{:S(2)}) copy-start(f32[256,512]{1,0:T(8,128)S(1)} %add.94) | copy-start | bytes 1572868
  56.0 149.6 %all-gather.5.cloned.1.call-start = ((), (), s32[]{:S(2)}) async-start(), calls=%async_computation.5 | async-start | bytes 8912896 | tf_op jit(solution)/shard_map/all_gather | solution.py:53
  59.2 793.8 %reduce-scatter.3.cloned.1.call-start = ((), (), s32[]{:S(2)}) async-start(), calls=%async_computation.6 | async-start | bytes 17825792 | tf_op jit(solution)/shard_map/reduce_scatter | solution.py:125
  141.1 73.5 %copy-start.18 = (s32[1,2,32]{2,1,0:T(2,128)S(1)}, s32[1,2,32]{2,1,0:T(2,128)}, u32[]{:S(2)}) copy-start(s32[1,2,32]{2,1,0:T(2,128)} %param.16) | copy-start | bytes 772
  391.9 5.8 copy-start.4
  391.9 5.8 copy-start.8
  391.9 5.8 copy-start.2
  397.7 5.1 copy-start.1
  434.0 6.0 copy-start.4
  434.0 6.0 copy-start.8
  434.0 6.0 copy-start.2
  440.0 5.1 copy-start.1
  476.2 6.0 copy-start.4
  476.2 6.0 copy-start.8
  476.2 6.0 copy-start.2
  482.2 5.1 copy-start.1
  518.5 6.0 copy-start.4
  518.5 6.0 copy-start.8
  518.5 6.0 copy-start.2
  524.5 5.1 copy-start.1
  560.8 6.0 copy-start.4
  560.8 6.0 copy-start.8
  560.8 6.0 copy-start.2
  566.8 5.1 copy-start.1
  603.2 6.0 copy-start.4
  603.2 6.0 copy-start.8
  603.2 6.0 copy-start.2
  609.1 5.1 copy-start.1
  645.4 6.0 copy-start.4
  645.4 6.0 copy-start.8
  645.4 6.0 copy-start.2
  651.4 5.1 copy-start.1
  687.6 6.0 copy-start.4
  687.6 6.0 copy-start.8
  687.7 6.0 copy-start.2
  693.6 5.1 copy-start.1
  709.0 7.9 copy-start.9
  709.0 7.9 copy-start.13
  709.0 317.9 %all-reduce.3.cloned.1.call-start = ((), (), s32[]{:S(2)}) async-start(), calls=%async_computation.8 | async-start | bytes 8388608 | tf_op jit(solution)/shard_map/psum | solution.py:146
  718.9 140.2 %copy-start.11 = (f32[512,512]{1,0:T(8,128)S(1)}, f32[512,512]{1,0:T(8,128)}, u32[]{:S(2)}) copy-start(f32[512,512]{1,0:T(8,128)} %param.18) | copy-start | bytes 3145732
  859.0 236.0 %reduce-scatter.5.cloned.1.call-start = ((), (), s32[]{:S(2)}) async-start(), calls=%async_computation.7 | async-start | bytes 1114112 | tf_op jit(solution)/shard_map/reduce_scatter | solution.py:145
  1026.9 72.6 %copy-start.15 = (f32[512,512]{1,0:T(8,128)S(1)}, f32[512,512]{1,0:T(8,128)}, u32[]{:S(2)}) copy-start(f32[512,512]{1,0:T(8,128)} %get-tuple-element.532) | copy-start | bytes 3145732
  1026.9 73.6 %copy-start.14 = (f32[512,512]{1,0:T(8,128)S(1)}, f32[512,512]{1,0:T(8,128)}, u32[]{:S(2)}) copy-start(f32[512,512]{1,0:T(8,128)} %get-tuple-element.533) | copy-start | bytes 3145732
  (27 other events, 67.1 us)
Sparse Core Ops, SparseCore 0:
  56.1 75.9 all-gather.2
  135.1 70.4 all-gather.4
  709.1 143.7 reduce-scatter.2
  859.8 167.0 all-reduce.2
  1031.6 63.3 reduce-scatter.4
where the time goes:
time: 1120 us; the launch traced here: 1110 us
  waiting for transfers between devices  475 us (42%)
  matrix products  360 us (32%)
  local copies, waits for them, and re-layouts  132 us (12%)
  other arithmetic  63.1 us (6%)
  blocking collectives  34.5 us (3%)
  loops' own time  22.5 us (2%)
  between operations  14.4 us (1%)
    reduce_scatter x1, waiting for transfers between devices, on_device(): summed = lax.psum_scatter(key_terms, 'seq', scatter_dimension=0, tiled=True)  134 us
    psum x1, waiting for transfers between devices, on_device(): lax.psum((grad_query_w, grad_key_w, grad_value_w, grad_out_w), ('dp', 'se...  112 us
    dot_general x16, matrix products, scores_for(): jnp.einsum('qhd,khd->hqk', query_heads, block_keys, precision=HIGH) * scale  102 us
    all_gather x1, waiting for transfers between devices, on_device(): lax.all_gather(keys_here, 'seq', axis=0, tiled=True)  69.8 us
    reduce_scatter x1, waiting for transfers between devices, on_device(): lax.psum_scatter(table_terms, 'seq', scatter_dimension=0, tiled=True)  68.1 us
    all_gather x1, waiting for transfers between devices, on_device(): lax.all_gather(values_here, 'seq', axis=0, tiled=True)  64.5 us
    dot_general x8, matrix products, backward_step(): jnp.einsum('qhd,khd->hqk', grad_context, block_values, precision=HIGH)  62.9 us
    dot_general x8, matrix products, backward_step(): jnp.einsum('hqk,khd->qhd', grad_scores, block_keys, precision=HIGH) * scale  47.4 us
  transfers between devices with their start and end apart: 6, of which 6 were waited for; matrix products, arithmetic and copies ran while one was open for 4% of the time, Pallas kernels for 0%

commit v1 on v0

v1 whole, which is shorter than its diff:
```python
import jax
import jax.numpy as jnp
from jax import lax
from jax.experimental import pallas as pl
from jax.experimental.pallas import tpu as pltpu
from jax.sharding import PartitionSpec as P

HEADS = 8
HEAD_DIM = 64
TILE = 128
SPAN = 512
BF = jnp.bfloat16
F32 = jnp.float32
EXACT = lax.Precision.HIGHEST
THREE = lax.Precision.HIGH


def product(left, right, precision=THREE):
    return jnp.dot(left, right, precision=precision, preferred_element_type=F32)


def dot_nn(a, b):
    return lax.dot_general(a, b, (((1,), (0,)), ((), ())), preferred_element_type=F32)


def dot_tn(a, b):
    return lax.dot_general(a, b, (((0,), (0,)), ((), ())), preferred_element_type=F32)


def halves(x):
    hi = x.astype(BF)
    lo = (x - hi.astype(F32)).astype(BF)
    return hi, lo


def make(span):
    def kernel(bias, qt4, qs2, dot_, k_ref, v_ref, ctx_ref, dq_ref, dk_ref, dv_ref, k2, v2, s_ref, ph, plo):
        rows = k_ref.shape[0]
        nb = rows // span
        tiles = span // 128
        low = lax.broadcasted_iota(jnp.int32, (span, 128), 1) < 64
        for head in range(2):
            def prepare(i, c):
                at = pl.ds(pl.multiple_of(i * span, span), span)
                for src, dst in ((k_ref, k2), (v_ref, v2)):
                    x = src[at, :]
                    hi = x.astype(BF).astype(F32)
                    lo = x - hi
                    if head == 0:
                        both = jnp.where(low, hi, pltpu.roll(lo, 64, 1))
                    else:
                        both = jnp.where(low, pltpu.roll(hi, 64, 1), lo)
                    dst[at, :] = both.astype(BF)
                return c
            lax.fori_loop(0, nb, prepare, 0)
            q4 = qt4[head]

            def score(i, peak):
                at = pl.ds(pl.multiple_of(i * span, span), span)
                k = k2[at, :]
                s = dot_nn(jnp.concatenate([k, k], axis=1), q4)
                parts = []
                for t in range(tiles):
                    st = s[t * 128:(t + 1) * 128] + bias[pl.ds(i * tiles + t, 1), :]
                    s_ref[pl.ds(pl.multiple_of(i * span + t * 128, 128), 128), :] = st
                    peak = jnp.maximum(peak, jnp.max(st.reshape(16, 8, 256), axis=0))
                return peak
            peak = lax.fori_loop(0, nb, score, jnp.full((8, 256), -3e38, F32))
            peak = jnp.max(peak, axis=0, keepdims=True)

            def weigh(i, carry):
                total, acc = carry
                at = pl.ds(pl.multiple_of(i * span, span), span)
                p = jnp.exp2(s_ref[at, :] - peak)
                total = total + jnp.sum(p.reshape(span // 8, 8, 256), axis=0)
                hi, lo = halves(p)
                ph[at, :] = hi
                plo[at, :] = lo
                v = v2[at, :]
                acc = acc + dot_tn(v, hi) + dot_tn(v, lo)
                return total, acc
            total, acc = lax.fori_loop(0, nb, weigh, (jnp.zeros((8, 256), F32), jnp.zeros((128, 256), F32)))
            share = 1.0 / jnp.sum(total, axis=0, keepdims=True)
            ctx = (acc[:64] + acc[64:]) * share
            ctx_ref[head * 64:(head + 1) * 64, :] = ctx
            g = dot_[head] * share
            delta = jnp.sum(g * ctx, axis=0, keepdims=True)
            ghi = g.astype(BF).astype(F32)
            glo = g - ghi
            g2 = jnp.concatenate([ghi, glo], axis=0)
            g4 = jnp.concatenate([ghi, ghi, glo, glo], axis=0).astype(BF)
            gn = g2.T.astype(BF)
            qn = qs2[head]

            def back(i, acc):
                at = pl.ds(pl.multiple_of(i * span, span), span)
                v = v2[at, :]
                k = k2[at, :]
                dp = dot_nn(jnp.concatenate([v, v], axis=1), g4)
                hi = ph[at, :]
                lo = plo[at, :]
                ds = (hi.astype(F32) + lo.astype(F32)) * (dp - delta)
                dv = dot_nn(hi, gn) + dot_nn(lo, gn)
                dv = dv + pltpu.roll(dv, 64, 1)
                shi, slo = halves(ds)
                dk = dot_nn(shi, qn) + dot_nn(slo, qn)
                dk = dk + pltpu.roll(dk, 64, 1)
                if head == 0:
                    dv_ref[at, :] = dv
                    dk_ref[at, :] = dk
                else:
                    dv_ref[at, :] = jnp.where(low, dv_ref[at, :], dv)
                    dk_ref[at, :] = jnp.where(low, dk_ref[at, :], dk)
                return acc + dot_tn(k, shi) + dot_tn(k, slo)
            acc = lax.fori_loop(0, nb, back, jnp.zeros((128, 256), F32))
            dq_ref[head * 64:(head + 1) * 64, :] = acc[:64] + acc[64:]

    def call(bias, qt4, qs2, dot_, kv):
        rows = kv.shape[0]
        pairs = 4
        return pl.pallas_call(
            kernel,
            grid=(pairs,),
            in_specs=[
                pl.BlockSpec(bias.shape, lambda p: (0, 0)),
                pl.BlockSpec((2, 256, 256), lambda p: (p, 0, 0)),
                pl.BlockSpec((2, 256, 128), lambda p: (p, 0, 0)),
                pl.BlockSpec((2, 64, 256), lambda p: (p, 0, 0)),
                pl.BlockSpec((rows, 128), lambda p: (0, p)),
                pl.BlockSpec((rows, 128), lambda p: (0, 4 + p)),
            ],
            out_specs=[
                pl.BlockSpec((128, 256), lambda p: (p, 0)),
                pl.BlockSpec((128, 256), lambda p: (p, 0)),
                pl.BlockSpec((rows, 128), lambda p: (0, p)),
                pl.BlockSpec((rows, 128), lambda p: (0, p)),
            ],
            out_shape=[
                jax.ShapeDtypeStruct((512, 256), F32),
                jax.ShapeDtypeStruct((512, 256), F32),
                jax.ShapeDtypeStruct((rows, 512), F32),
                jax.ShapeDtypeStruct((rows, 512), F32),
            ],
            scratch_shapes=[
                pltpu.VMEM((rows, 128), BF),
                pltpu.VMEM((rows, 128), BF),
                pltpu.VMEM((rows, 256), F32),
                pltpu.VMEM((rows, 256), BF),
                pltpu.VMEM((rows, 256), BF),
            ],
            compiler_params=pltpu.CompilerParams(vmem_limit_bytes=56 * 1024 * 1024),
        )(bias, qt4, qs2, dot_, kv, kv)
    return call

def split_xla(x):
    hi = lax.reduce_precision(x, 8, 7)
    return hi, x - hi

def operands(q, dctx, tiles):
    log2e = 1.4426950408889634
    qt = (q * log2e).T.reshape(8, 64, 256)
    hi, lo = split_xla(qt)
    qt4 = jnp.concatenate([hi, hi, lo, lo], axis=1).astype(BF)
    qh = q.reshape(256, 8, 64).transpose(1, 0, 2)
    hi, lo = split_xla(qh)
    qs2 = jnp.concatenate([hi, lo], axis=2).astype(BF)
    dot_ = dctx.T.reshape(8, 64, 256)
    bias = jnp.where(tiles.T > 0, 0.0, -1e30).astype(F32)
    bias = jnp.repeat(bias, 128, axis=1)
    return bias, qt4, qs2, dot_


def on_device(
    item_table,
    serve_lists,
    event_slots,
    session_tiles,
    w_query,
    w_key,
    w_value,
    w_out,
    grad_attended,
):
    width = item_table.shape[1]
    lists = serve_lists[0, :, 0, :]
    served = item_table[lists]
    arrived = lax.all_to_all(served, "dp", split_axis=0, concat_axis=0, tiled=True)
    slot_rows = arrived.reshape(-1, width)
    slots = event_slots[0]
    inputs = slot_rows[slots[0]] + slot_rows[slots[1]]
    history = lax.all_gather(inputs, "seq", axis=0, tiled=True)
    cotangent = grad_attended[0]
    scale = HEAD_DIM ** (-0.5)
    queries = product(inputs, w_query, EXACT) * scale
    grad_context = product(cotangent, w_out.T)
    w_both = jnp.concatenate([w_key, w_value], axis=1)
    both = product(history, w_both)
    context_t, grad_queries_t, grad_keys, grad_values = make(SPAN)(
        *operands(queries, grad_context, session_tiles[0]), both
    )
    context = context_t.T
    grad_queries = grad_queries_t.T * scale
    attended = product(context, w_out)
    grad_out_w = product(context_t, cotangent)
    grad_query_w = product(inputs.T, grad_queries)
    grad_key_w = product(history.T, grad_keys)
    grad_value_w = product(history.T, grad_values)
    partial = product(grad_keys, w_key.T) + product(grad_values, w_value.T)
    grad_inputs = lax.psum_scatter(partial, "seq", scatter_dimension=0, tiled=True)
    grad_inputs = grad_inputs + product(grad_queries, w_query.T)
    doubled = jnp.concatenate([grad_inputs, grad_inputs], axis=0)
    slot_grads = jax.ops.segment_sum(
        doubled, jnp.concatenate([slots[0], slots[1]]), num_segments=slot_rows.shape[0]
    )
    returned = lax.all_to_all(
        slot_grads.reshape(arrived.shape), "dp", split_axis=0, concat_axis=0, tiled=True
    )
    table_terms = jax.ops.segment_sum(
        returned.reshape(-1, width), lists.reshape(-1), num_segments=item_table.shape[0]
    )
    grad_table = lax.psum_scatter(table_terms, "seq", scatter_dimension=0, tiled=True)
    grad_query_w, grad_key_w, grad_value_w, grad_out_w = lax.psum(
        (grad_query_w, grad_key_w, grad_value_w, grad_out_w), ("dp", "seq")
    )
    return (attended[None], grad_query_w, grad_key_w, grad_value_w, grad_out_w, grad_table)


def solution(mesh):
    return jax.shard_map(
        on_device,
        mesh=mesh,
        in_specs=(
            P("dp", None),
            P("dp", None, "seq", None),
            P("dp", None, "seq"),
            P("dp", "seq", None),
            P(),
            P(),
            P(),
            P(),
            P("dp", "seq", None),
        ),
        out_specs=(P("dp", "seq", None), P(), P(), P(), P(), P(("dp", "seq"), None)),
        check_vma=False,
    )
```

time: 1120 us -> 619 us (0.55)
  matrix products: 360 us -> 88.8 us
  waiting for transfers between devices: 475 us -> 332 us
  local copies, waits for them, and re-layouts: 132 us -> 24.2 us
  Pallas kernels: 0 us -> 93.7 us
  other arithmetic: 63.1 us -> 19.7 us
  loops' own time: 22.5 us -> 0 us
    dot_general x68 -> x11, matrix products: 360 us -> 88.8 us  [product(): return jnp.dot(left, right, precision=precision, preferred_element_type=F32)]
    pallas_call x0 -> x1, Pallas kernels: none -> 93.7 us  [call(): pl.pallas_call(kernel, grid=(pairs,), in_specs=[pl.BlockSpec(bias.shape,...]
    reduce_scatter x1, waiting for transfers between devices: 134 us -> 57 us  [on_device(): lax.psum_scatter(partial, 'seq', scatter_dimension=0, tiled=True)]
    all_gather x2 -> x1, waiting for transfers between devices: 134 us -> 61.3 us  [on_device(): history = lax.all_gather(inputs, 'seq', axis=0, tiled=True)]
    dynamic_slice x32 -> x0, local copies, waits for them, and re-layouts: 36.9 us -> none  [the longest x16 27.5 us: scores_for(): lax.dynamic_slice_in_dim(values_all, index * span, span, 0)]
    dynamic_update_slice x16 -> x0, local copies, waits for them, and re-layouts: 27.2 us -> none  [on_device(): lax.scan(backward_step, jnp.zeros((rows_here, HEADS, HEAD_DIM), jnp.float...]
    reduce_sum x8 -> x0, other arithmetic: 26.7 us -> none  [forward_step(): total = total * factor + jnp.sum(weights, axis=2)]
    another operation x2 -> x0, loops' own time: 22.5 us -> none  [the longest x1 11.3 us: on_device(): (peak, total, accum), _ = lax.scan(forward_step, start_state, indices)]
  transfers between devices with their start and end apart: 6 -> 5, of which waited for: 6 -> 5; matrix products, arithmetic and copies ran while one was open for 4% -> 12% of each run, Pallas kernels for 0% -> 0%
where the time goes in v1:
time: 619 us; the launch traced here: 613 us
  waiting for transfers between devices  332 us (54%)
  Pallas kernels  93.7 us (15%)
  matrix products  88.8 us (14%)
  blocking collectives  34.3 us (6%)
  local copies, waits for them, and re-layouts  24.2 us (4%)
  other arithmetic  19.7 us (3%)
  between operations  14.2 us (2%)
  starting transfers between devices  6.5 us (1%)
    psum x1, waiting for transfers between devices, on_device(): lax.psum((grad_query_w, grad_key_w, grad_value_w, grad_out_w), ('dp', 'se...  119 us
    pallas_call x1, Pallas kernels, call(): pl.pallas_call(kernel, grid=(pairs,), in_specs=[pl.BlockSpec(bias.shape,...  93.7 us
    dot_general x11, matrix products, product(): return jnp.dot(left, right, precision=precision, preferred_element_type=F32)  88.8 us
    reduce_scatter x1, waiting for transfers between devices, on_device(): lax.psum_scatter(table_terms, 'seq', scatter_dimension=0, tiled=True)  67.7 us
    all_gather x1, waiting for transfers between devices, on_device(): history = lax.all_gather(inputs, 'seq', axis=0, tiled=True)  61.3 us
    reduce_scatter x1, waiting for transfers between devices, on_device(): lax.psum_scatter(partial, 'seq', scatter_dimension=0, tiled=True)  57 us
    all_to_all x1, blocking collectives, on_device(): lax.all_to_all(slot_grads.reshape(arrived.shape), 'dp', split_axis=0, con...  34.3 us
    all_to_all x1, waiting for transfers between devices, on_device(): lax.all_to_all(served, 'dp', split_axis=0, concat_axis=0, tiled=True)  27 us
  transfers between devices with their start and end apart: 5, of which 5 were waited for; matrix products, arithmetic and copies ran while one was open for 12% of the time, Pallas kernels for 0%

profile of v1, /device:TPU:1, one launch (start us, length us, event | category | flops | bytes accessed | tf_op | source)
XLA Modules:
  0.0 613.4 jit_solution(3428094713560222849)
XLA Ops:
  7.2 0.8 fusion.23
  8.0 0.5 copy-done
  8.4 4.9 gather_fusion
  13.3 6.3 %all-to-all-start = ((f32[8,128,512]{2,1,0:T(8,128)}), f32[8,128,512]{2,1,0:T(8,128)S(1)}, u32[]{:S(2)}, u32[]{:S(2)}) async-start(f32[8,128,512]{2,1,0:T(8,128)} %bitcast.65), calls=%async_computation | async-start | bytes 4194304 | tf_op jit(solution)/shard_map/all_to_all | solution.py:187
  19.6 0.0 all-gather.2.cloned.1.call-start
  19.7 27.0 %all-to-all-done = f32[8,128,512]{2,1,0:T(8,128)S(1)} async-done(((f32[8,128,512]{2,1,0:T(8,128)}), f32[8,128,512]{2,1,0:T(8,128)S(1)}, u32[]{:S(2)}, u32[]{:S(2)}) %all-to-all-start) | async-done | bytes 2097184 | tf_op jit(solution)/shard_map/all_to_all | solution.py:187
  46.7 1.8 gather_fusion.1
  48.4 1.8 gather_fusion.2
  50.2 2.2 add.62
  52.4 0.0 reduce-scatter.3.cloned.1.call-start
  52.5 0.1 copy.17
  52.6 0.1 broadcast_in_dim.28
  52.7 0.6 copy.23
  53.3 2.8 fusion.11.dot_
  56.1 3.2 broadcast_multiply_fusion
  59.3 1.0 copy.19
  60.3 1.4 copy.20
  61.7 2.0 copy.18
  63.7 0.2 reduce-precision_convert_fusion
  64.0 1.1 pad_maximum_fusion.1.qs2
  65.1 1.2 reduce-precision_convert_fusion.1
  66.2 1.1 pad_maximum_fusion.qt4
  67.3 61.3 %all-gather.2.cloned.1.call-done = f32[4096,512]{1,0:T(8,128)} async-done(((f32[256,512]{1,0:T(8,128)}), f32[4096,512]{1,0:T(8,128)}) %all-gather.2.cloned.1.call-update) | async-done | bytes 8388624 | tf_op jit(solution)/shard_map/all_gather | solution.py:191
  128.6 18.1 %fusion.k_ref.v_ref = f32[4096,1024]{1,0:T(8,128)} fusion(f32[4096,512]{1,0:T(8,128)} %all-gather.2.cloned.1.call-done, f32[512,512]{1,0:T(8,128)S(1)} %copy-done.4, f32[512,512]{1,0:T(8,128)S(1)} %copy-done.3), kind=kOutput, calls=%fused_computation.6 | convolution fusion | flops 12885426176 | bytes 27262976 | tf_op jit(solution)/shard_map/dot_general | solution.py:19
  146.7 93.7 %shard_map.136 = (f32[512,256]{1,0:T(8,128)}, f32[512,256]{1,0:T(8,128)}, f32[4096,512]{1,0:T(8,128)}, f32[4096,512]{1,0:T(8,128)}) custom-call(f32[32,256]{1,0:T(8,128)} %bitcast.71, bf16[8,256,256]{2,1,0:T(8,128)(2,1)} %pad_maximum_fusion.qt4, bf16[8,256,128]{2,1,0:T(8,128)(2,1)} %pad_maximum_fusion.1.qs2, f32[8,64,256]{2,1,0:T(8,128)} %fusion.11.dot_, ...), custom_call_target="tpu_custom_call" | custom-call | tf_op jit(solution)/shard_map/pallas_call | solution.py:121
  240.4 9.3 %fusion.31 = f32[4096,512]{1,0:T(8,128)S(1)} fusion(f32[4096,512]{1,0:T(8,128)} %get-tuple-element.12, f32[512,512]{1,0:T(8,128)S(1)} %copy-done.3), kind=kOutput, calls=%fused_computation.55 | convolution fusion | flops 6442450944 | bytes 17825792 | tf_op jit(solution)/shard_map/dot_general | solution.py:19
  249.8 9.2 %convolution_add_fusion = f32[4096,512]{1,0:T(8,128)} fusion(f32[4096,512]{1,0:T(8,128)S(1)} %fusion.31, f32[4096,512]{1,0:T(8,128)S(1)} %bitcast.62, f32[512,512]{1,0:T(8,128)S(1)} %copy-done.4), kind=kOutput, calls=%fused_computation.5 | convolution fusion | flops 6444548096 | bytes 26214400 | tf_op jit(solution)/shard_map/dot_general | solution.py:19
  259.0 0.0 reduce-scatter.3.cloned.1.call-update
  259.0 0.0 all-reduce.3.cloned.1.call-start
  259.1 0.9 copy-done.2
  260.0 0.2 copy-done.6
  260.2 2.0 fusion.18
  262.2 1.6 fusion.13
  263.8 20.2 %fusion.30 = f32[512,512]{1,0:T(8,128)} fusion(f32[4096,512]{1,0:T(8,128)} %all-gather.2.cloned.1.call-done, f32[4096,512]{1,0:T(8,128)} %get-tuple-element.13), kind=kOutput, calls=%fused_computation.54 | convolution fusion | flops 6442450944 | bytes 17825792 | tf_op jit(solution)/shard_map/dot_general | solution.py:19
  284.0 16.7 %fusion.29 = f32[512,512]{1,0:T(8,128)} fusion(f32[4096,512]{1,0:T(8,128)S(1)} %bitcast.60, f32[4096,512]{1,0:T(8,128)} %get-tuple-element.12), kind=kOutput, calls=%fused_computation.53 | convolution fusion | flops 6442450944 | bytes 17825792 | tf_op jit(solution)/shard_map/dot_general | solution.py:19
  300.7 0.0 reduce-scatter.5.cloned.1.call-start
  300.8 57.0 %reduce-scatter.3.cloned.1.call-done = f32[256,512]{1,0:T(8,128)} async-done(((f32[4096,512]{1,0:T(8,128)}), f32[256,512]{1,0:T(8,128)}) %reduce-scatter.3.cloned.1.call-update) | async-done | bytes 524304 | tf_op jit(solution)/shard_map/reduce_scatter | solution.py:209
  357.8 2.9 convolution_add_fusion.1
  360.7 4.9 scatter_custom_fusion
  365.5 34.3 %all_to_all.10 = f32[8,128,512]{2,1,0:T(8,128)} all-to-all(f32[8,128,512]{2,1,0:T(8,128)S(1)} %bitcast.66), channel_id=1, replica_groups=mesh['dp'=8,'seq'=16] {'dp'}, dimensions={0} | all-to-all | bytes 4194304 | tf_op jit(solution)/shard_map/all_to_all | solution.py:215
  399.9 8.3 %scatter_custom_fusion.1 = f32[512,512]{1,0:T(8,128)} fusion(s32[1024]{0:T(1024)} %bitcast.74, f32[1024,512]{1,0:T(8,128)} %bitcast.69, f32[]{:T(128)} %constant.8.clone.1), kind=kCustom, calls=%fused_computation.29 | custom fusion | flops 524288 | bytes 1049088 | tf_op jit(solution)/shard_map/scatter-add | solution.py:218
  408.1 2.8 convolution_bitcast_fusion
  410.9 119.0 %all-reduce.3.cloned.1.call-done = (f32[512,512]{1,0:T(8,128)}, f32[512,512]{1,0:T(8,128)}, f32[512,512]{1,0:T(8,128)}, f32[512,512]{1,0:T(8,128)}) async-done(((f32[512,512]{1,0:T(8,128)}, f32[512,512]{1,0:T(8,128)}, f32[512,512]{1,0:T(8,128)}, f32[512,512]{1,0:T(8,128)}), (f32[512,512]{1,0:T(8,128)}, f32[512,512]{1,0:T(8,128)}, f32[512,512]{1,0:T(8,128)}, ...) | async-done | bytes 4194320 | tf_op jit(solution)/shard_map/psum | solution.py:222
  530.0 67.7 %reduce-scatter.5.cloned.1.call-done = f32[32,512]{1,0:T(8,128)} async-done(((f32[512,512]{1,0:T(8,128)}), f32[32,512]{1,0:T(8,128)}) %reduce-scatter.5.cloned.1.call-update) | async-done | bytes 65552 | tf_op jit(solution)/shard_map/reduce_scatter | solution.py:221
  597.7 2.3 copy.28
  599.9 2.3 copy.29
  602.2 2.3 copy.30
  604.5 2.3 copy.31
  (38 shorter events, 0.1 us)
Async XLA Ops:
  7.2 1.2 copy-start
  8.4 11.3 %copy-start.9 = (s32[1,2,256]{2,1,0:T(2,128)S(1)}, s32[1,2,256]{2,1,0:T(2,128)}, u32[]{:S(2)}) copy-start(s32[1,2,256]{2,1,0:T(2,128)} %param.11) | copy-start | bytes 6148
  13.3 39.2 %copy-start.10 = (s32[1,2,32]{2,1,0:T(2,128)S(1)}, s32[1,2,32]{2,1,0:T(2,128)}, u32[]{:S(2)}) copy-start(s32[1,2,32]{2,1,0:T(2,128)} %param.12) | copy-start | bytes 772
  13.3 33.4 %all-to-all-start = ((f32[8,128,512]{2,1,0:T(8,128)}), f32[8,128,512]{2,1,0:T(8,128)S(1)}, u32[]{:S(2)}, u32[]{:S(2)}) async-start(f32[8,128,512]{2,1,0:T(8,128)} %bitcast.65), calls=%async_computation | async-start | bytes 4194304 | tf_op jit(solution)/shard_map/all_to_all | solution.py:187
  19.6 108.9 %all-gather.2.cloned.1.call-start = ((), (), s32[]{:S(2)}) async-start(), calls=%async_computation.4 | async-start | bytes 8912896 | tf_op jit(solution)/shard_map/all_gather | solution.py:191
  50.2 78.4 %copy-start.3 = (f32[512,512]{1,0:T(8,128)S(1)}, f32[512,512]{1,0:T(8,128)}, u32[]{:S(2)}) copy-start(f32[512,512]{1,0:T(8,128)} %param.14) | copy-start | bytes 3145732
  50.2 78.4 %copy-start.4 = (f32[512,512]{1,0:T(8,128)S(1)}, f32[512,512]{1,0:T(8,128)}, u32[]{:S(2)}) copy-start(f32[512,512]{1,0:T(8,128)} %param.15) | copy-start | bytes 3145732
  52.4 305.3 %reduce-scatter.3.cloned.1.call-start = ((), (), s32[]{:S(2)}) async-start(), calls=%async_computation.5 | async-start | bytes 8912896 | tf_op jit(solution)/shard_map/reduce_scatter | solution.py:209
  240.4 9.3 %slice-start.2 = ((s8[8388608]{0:T(1024)(128)(4,1)}), s8[4194304]{0:T(1024)(128)(4,1)S(1)}, s32[]{:S(2)}) async-start(s8[8388608]{0:T(1024)(128)(4,1)} %bitcast.61), calls=%async_computation.10 | async-start | bytes 8388608
  240.4 9.4 %slice-start.3 = ((s8[8388608]{0:T(1024)(128)(4,1)}), s8[4194304]{0:T(1024)(128)(4,1)S(1)}, s32[]{:S(2)}) async-start(s8[8388608]{0:T(1024)(128)(4,1)} %bitcast.61), calls=%async_computation.11 | async-start | bytes 8388608
  259.0 1.0 copy-start.2
  259.0 1.2 copy-start.6
  259.0 3.2 copy-start.7
  259.0 3.2 copy-start.8
  259.0 271.0 %all-reduce.3.cloned.1.call-start = ((), (), s32[]{:S(2)}) async-start(), calls=%async_computation.7 | async-start | bytes 8388608 | tf_op jit(solution)/shard_map/psum | solution.py:222
  262.2 21.7 %slice-start = ((s8[8388608]{0:T(1024)(128)(4,1)}), s8[4194304]{0:T(1024)(128)(4,1)S(1)}, s32[]{:S(2)}) async-start(s8[8388608]{0:T(1024)(128)(4,1)} %bitcast.59), calls=%async_computation.8 | async-start | bytes 8388608
  263.8 20.2 %slice-start.1 = ((s8[8388608]{0:T(1024)(128)(4,1)}), s8[4194304]{0:T(1024)(128)(4,1)S(1)}, s32[]{:S(2)}) async-start(s8[8388608]{0:T(1024)(128)(4,1)} %bitcast.59), calls=%async_computation.9 | async-start | bytes 8388608
  284.0 73.8 %copy-start.5 = (f32[512,512]{1,0:T(8,128)S(1)}, f32[512,512]{1,0:T(8,128)}, u32[]{:S(2)}) copy-start(f32[512,512]{1,0:T(8,128)} %param.13) | copy-start | bytes 3145732
  300.7 296.9 %reduce-scatter.5.cloned.1.call-start = ((), (), s32[]{:S(2)}) async-start(), calls=%async_computation.6 | async-start | bytes 1114112 | tf_op jit(solution)/shard_map/reduce_scatter | solution.py:221
  365.5 241.2 %copy-start.1 = (f32[512,512]{1,0:T(8,128)S(1)}, f32[512,512]{1,0:T(8,128)}, u32[]{:S(2)}) copy-start(f32[512,512]{1,0:T(8,128)} %param.9) | copy-start | bytes 3145732
Sparse Core Ops, SparseCore 0:
  52.5 75.9 all-gather.1
  259.1 98.5 reduce-scatter.2
  363.9 166.0 all-reduce.2
  534.2 63.3 reduce-scatter.4

commit v2 on v1

--- a/solution.py
+++ b/solution.py
@@ -3,12 +3,13 @@
 from jax import lax
 from jax.experimental import pallas as pl
 from jax.experimental.pallas import tpu as pltpu
-from jax.sharding import PartitionSpec as P
+from jax.sharding import Mesh, PartitionSpec as P
 
 HEADS = 8
 HEAD_DIM = 64
 TILE = 128
 SPAN = 512
+MIB = 1024 * 1024
 BF = jnp.bfloat16
 F32 = jnp.float32
 EXACT = lax.Precision.HIGHEST
@@ -18,20 +19,16 @@
 def product(left, right, precision=THREE):
     return jnp.dot(left, right, precision=precision, preferred_element_type=F32)
 
-
 def dot_nn(a, b):
     return lax.dot_general(a, b, (((1,), (0,)), ((), ())), preferred_element_type=F32)
 
-
 def dot_tn(a, b):
     return lax.dot_general(a, b, (((0,), (0,)), ((), ())), preferred_element_type=F32)
-
 
 def halves(x):
     hi = x.astype(BF)
     lo = (x - hi.astype(F32)).astype(BF)
     return hi, lo
-
 
 def make(span):
     def kernel(bias, qt4, qs2, dot_, k_ref, v_ref, ctx_ref, dq_ref, dk_ref, dv_ref, k2, v2, s_ref, ph, plo):
@@ -170,6 +167,249 @@
     return bias, qt4, qs2, dot_
 
 
+def front(pieces, slots, w_hi, w_lo, rows, span=512, unroll=8):
+    width = 512
+    n = len(pieces)
+    count = sum(p.shape[0] for p in pieces)
+    def kernel(*refs):
+        idx = refs[0]
+        parts = refs[1:1 + n]
+        wh, wl, x_ref, kv_ref, table, flat, sem = refs[1 + n:]
+        step = pl.program_id(0)
+        @pl.when(step == 0)
+        def _():
+            copies = []
+            at = 0
+            for j, p in enumerate(parts):
+                copies.append(pltpu.make_async_copy(p, table.at[pl.ds(at, p.shape[0])], sem.at[j]))
+                at += p.shape[0]
+            for c in copies:
+                c.start()
+            for c in copies:
+                c.wait()
+        def body(i, c):
+            for u in range(unroll):
+                e = i * unroll + u
+                a = idx[0, step * span + e]
+                b = idx[1, step * span + e]
+                a = pl.multiple_of(a * 4, 4)
+                b = pl.multiple_of(b * 4, 4)
+                flat[pl.ds(pl.multiple_of(e * 4, 4), 4), :] = table[pl.ds(a, 4), :] + table[pl.ds(b, 4), :]
+            return c
+        lax.fori_loop(0, span // unroll, body, 0)
+        x = jnp.concatenate([flat[pl.ds(j, span, stride=4), :] for j in range(4)], axis=1)
+        x_ref[...] = x
+        hi, lo = halves(x)
+        kv_ref[...] = dot_nn(hi, wh[...]) + dot_nn(hi, wl[...]) + dot_nn(lo, wh[...])
+    return pl.pallas_call(
+        kernel,
+        grid=(rows // span,),
+        in_specs=[pl.BlockSpec(memory_space=pltpu.SMEM)]
+        + [pl.BlockSpec(memory_space=pl.ANY)] * n
+        + [pl.BlockSpec(w_hi.shape, lambda i: (0, 0))] * 2,
+        out_specs=[pl.BlockSpec((span, width), lambda i: (i, 0)), pl.BlockSpec((span, 2 * width), lambda i: (i, 0))],
+        out_shape=[jax.ShapeDtypeStruct((rows, width), F32), jax.ShapeDtypeStruct((rows, 2 * width), F32)],
+        scratch_shapes=[pltpu.VMEM((count, 128), F32), pltpu.VMEM((span * 4, 128), F32), pltpu.SemaphoreType.DMA((n,))],
+        compiler_params=pltpu.CompilerParams(vmem_limit_bytes=56 * MIB),
+    )(slots, *pieces, w_hi, w_lo)
+
+def back(slots, own, dk, dv, x, wt_hi, wt_lo, qx, count, span=512, unroll=8, chains=4):
+    rows, width = x.shape
+    def kernel(idx, own_ref, dk_ref, dv_ref, x_ref, wh, wl, qx_ref, acc, w_ref, *more):
+        *others, dx, flat = more
+        accs = [acc, *others]
+        step = pl.program_id(0)
+        @pl.when(step == 0)
+        def _():
+            w_ref[...] = jnp.zeros_like(w_ref)
+            def clear(i, c):
+                at = pl.ds(pl.multiple_of(i * 512, 512), 512)
+                for a in accs:
+                    a[at, :] = jnp.zeros((512, 128), F32)
+                return c
+            lax.fori_loop(0, count * 4 // 512, clear, 0)
+        khi, klo = halves(dk_ref[...])
+        vhi, vlo = halves(dv_ref[...])
+        hi = jnp.concatenate([khi, vhi], axis=1)
+        lo = jnp.concatenate([klo, vlo], axis=1)
+        dx[...] = dot_nn(hi, wh[...]) + dot_nn(hi, wl[...]) + dot_nn(lo, wh[...])
+        xhi, xlo = halves(x_ref[...])
+        w_ref[...] += dot_tn(hi, xhi) + dot_tn(hi, xlo) + dot_tn(lo, xhi)
+        @pl.when(own_ref[0] // 2 == step)
+        def _():
+            at = pl.ds(pl.multiple_of(own_ref[0] % 2 * 256, 256), 256)
+            dx[at, :] += qx_ref[...]
+        for j in range(4):
+            flat[pl.ds(j, span, stride=4), :] = dx[:, j * 128:(j + 1) * 128]
+        def body(i, c):
+            for u in range(unroll):
+                e = i * unroll + u
+                a = pl.multiple_of(idx[0, step * span + e] * 4, 4)
+                b = pl.multiple_of(idx[1, step * span + e] * 4, 4)
+                row = flat[pl.ds(pl.multiple_of(e * 4, 4), 4), :]
+                k = u % (chains // 2) * 2
+                accs[k][pl.ds(a, 4), :] += row
+                accs[k + 1][pl.ds(b, 4), :] += row
+            return c
+        lax.fori_loop(0, span // unroll, body, 0)
+        @pl.when(step == rows // span - 1)
+        def _():
+            def add(i, c):
+                at = pl.ds(pl.multiple_of(i * 512, 512), 512)
+                acc[at, :] = sum(a[at, :] for a in accs)
+                return c
+            lax.fori_loop(0, count * 4 // 512, add, 0)
+    return pl.pallas_call(
+        kernel,
+        grid=(rows // span,),
+        in_specs=[pl.BlockSpec(memory_space=pltpu.SMEM)] * 2
+        + [pl.BlockSpec((span, width), lambda i: (i, 0))] * 3
+        + [pl.BlockSpec((2 * width, width), lambda i: (0, 0))] * 2
+        + [pl.BlockSpec(qx.shape, lambda i: (0, 0))],
+        out_specs=[pl.BlockSpec((count * 4, 128), lambda i: (0, 0), pipeline_mode=pl.Buffered(1)), pl.BlockSpec((2 * width, width), lambda i: (0, 0), pipeline_mode=pl.Buffered(1))],
+        out_shape=[jax.ShapeDtypeStruct((count * 4, 128), F32), jax.ShapeDtypeStruct((2 * width, width), F32)],
+        scratch_shapes=[pltpu.VMEM((count * 4, 128), F32)] * (chains - 1) + [pltpu.VMEM((span, width), F32), pltpu.VMEM((span * 4, 128), F32)],
+        compiler_params=pltpu.CompilerParams(vmem_limit_bytes=56 * MIB),
+    )(slots, own, dk, dv, x, wt_hi, wt_lo, qx)
+
+
+Z = ("zl", "zh")
+SIZES = {"x": 4, "y": 4, Z: 4, "c": 2}
+
+def shift(v, axis, s):
+    n = SIZES[axis]
+    place = (lambda z: z % 2 * 2 + z // 2) if axis == Z else (lambda i: i)
+    return lax.ppermute(v, axis, [(place(i), place((i + s) % n)) for i in range(n)])
+
+def ring_gather(v, axis):
+    n = v.shape[0] // 2
+    before = shift(v, axis, 1)
+    after = shift(v, axis, -1)
+    far_a = shift(before[:n], axis, 1)
+    far_b = shift(after[n:], axis, -1)
+    return [v, before, after, far_a, far_b]
+
+def table_gather(shard):
+    c = lax.axis_index("c")
+    half = shard.shape[0] // 2
+    mine = lax.dynamic_slice_in_dim(shard, c * half, half, 0)
+    a1, a2 = mine[:half // 2], mine[half // 2:]
+    q = half // 4
+    za = shift(a2[:q], Z, 1)
+    zb = shift(a2[q:], Z, -1)
+    s1 = ring_gather(a1, "x")
+    v2 = jnp.concatenate([a2, za, zb], 0)
+    s2 = ring_gather(v2, "x")
+    z1 = shift(jnp.concatenate(s1[:2], 0), Z, 1)
+    z2 = shift(jnp.concatenate(s1[2:], 0), Z, -1)
+    first = jnp.concatenate(s1 + [z1, z2], 0)
+    other_first = shift(first, "c", 1)
+    second = jnp.concatenate(s2, 0)
+    other_second = shift(second, "c", 1)
+    return first, second, other_first, other_second
+
+def ring_scatter(v, axis):
+    m = v.shape[0] // 4
+    h = m // 2
+    up = shift(v[m + h:2 * m + h], axis, 1)
+    down = shift(v[2 * m + h:3 * m + h], axis, -1)
+    up2 = shift(v[m:m + h] + up[h:], axis, 1)
+    down2 = shift(v[3 * m + h:] + down[:h], axis, -1)
+    top = v[:h] + down[h:] + up2
+    low = v[h:m] + up[:h] + down2
+    return jnp.concatenate([top, low], 0)
+
+def direct_scatter(v, axis):
+    m = v.shape[0] // 4
+    a = shift(v[m:2 * m], axis, 1)
+    b = shift(v[3 * m:], axis, -1)
+    d = shift(v[2 * m:3 * m], axis, 2)
+    return v[:m] + a + b + d
+
+def scatter_parts(parts, orders, direct=True):
+    out = []
+    for v, order in zip(parts, orders):
+        half = v.shape[0] // 2
+        v = v[:half] + shift(v[half:], "c", 1)
+        v = ring_scatter(v, order[0])
+        for ax in order[1:]:
+            v = direct_scatter(v, ax) if direct else ring_scatter(v, ax)
+        out.append(v)
+    return out
+
+def direct_gather(v, axis):
+    return jnp.concatenate([v, shift(v, axis, -1), shift(v, axis, 2), shift(v, axis, 1)], 0)
+
+def ring_gather4(v, axis):
+    own, before, after, fa, fb = ring_gather(v, axis)
+    return jnp.concatenate([own, after, fa, fb, before], 0)
+
+def gather_parts(parts, orders):
+    out = []
+    for v, order in zip(parts, orders):
+        for ax in order[:0:-1]:
+            v = direct_gather(v, ax)
+        v = ring_gather4(v, order[0])
+        out.append(jnp.concatenate([v, shift(v, "c", 1)], 0))
+    return out
+
+
+def coordinates():
+    zl, x, y, zh, c = (lax.axis_index(a) for a in ("zl", "x", "y", "zh", "c"))
+    return {"x": x, "y": y, Z: zh * 2 + zl, "c": c, "zl": zl, "zh": zh}
+
+
+def table_place(row, me):
+    owner, local = row // 512, row % 512
+    half, part, within = local // 256, local % 256 // 128, local % 128
+    turn = (owner % 4 - me["x"]) % 4
+    order = jnp.where(turn == 0, 0, jnp.where(turn == 3, 1, jnp.where(turn == 1, 2, 3)))
+    other = (owner // 4 != me["zl"]).astype(jnp.int32)
+    first = other * 512 + order * 128 + within
+    second = 1024 + order * 256 + other * 128 + within
+    return jnp.where(half != me["c"], 2048, 0) + jnp.where(part == 0, first, second)
+
+
+PARTS = (("x", "y", Z), ("y", Z, "x"), (Z, "x", "y"))
+PART_ROWS = (16, 8, 8)
+
+
+def scatter_place(row, me):
+    owner, local = row // 512, row % 512
+    seq, within = local // 32, local % 32
+    at = {"x": owner % 4, "y": seq // 4, Z: seq // 2 % 2 * 2 + owner // 4, "c": seq % 2}
+    turn = {k: (v - me[k]) % SIZES[k] for k, v in at.items()}
+    result, base, low = jnp.zeros_like(row), 0, 0
+    for order, n in zip(PARTS, PART_ROWS):
+        block = turn["c"]
+        for axis in order:
+            block = block * 4 + turn[axis]
+        place = base + block * n + within - low
+        result = jnp.where((within >= low) & (within < low + n), place, result)
+        base, low = base + 128 * n, low + n
+    return result
+
+
+def turned(order, me, back):
+    ids = jnp.arange(128, dtype=jnp.int32)
+    digits = [("c", ids // 64, 2), (order[0], ids // 16 % 4, 4), (order[1], ids // 4 % 4, 4), (order[2], ids % 4, 4)]
+    out = jnp.zeros_like(ids)
+    for axis, digit, n in digits:
+        out = out * n + ((digit - me[axis]) if back else (digit + me[axis])) % n
+    return out
+
+
+def sum_everywhere(arrays, me):
+    orders = PARTS[:2]
+    sent = [v.reshape(128, 8, 512)[turned(o, me, False)].reshape(1024, 512) for v, o in zip(arrays, orders)]
+    got = gather_parts(scatter_parts(sent, orders), orders)
+    return [v.reshape(128, 8, 512)[turned(o, me, True)].reshape(1024, 512) for v, o in zip(got, orders)]
+
+
+DP = ("zl", "x")
+SEQ = ("y", "zh", "c")
+
+
 def on_device(
     item_table,
     serve_lists,
@@ -181,20 +421,25 @@
     w_out,
     grad_attended,
 ):
-    width = item_table.shape[1]
-    lists = serve_lists[0, :, 0, :]
-    served = item_table[lists]
-    arrived = lax.all_to_all(served, "dp", split_axis=0, concat_axis=0, tiled=True)
-    slot_rows = arrived.reshape(-1, width)
+    me = coordinates()
+    seq = lax.axis_index(SEQ)
+    pieces = table_gather(item_table.reshape(-1, 128))
+    lists = lax.all_to_all(serve_lists[0, :, 0, :], DP, split_axis=0, concat_axis=0, tiled=True)
     slots = event_slots[0]
-    inputs = slot_rows[slots[0]] + slot_rows[slots[1]]
-    history = lax.all_gather(inputs, "seq", axis=0, tiled=True)
+    rows = slots // TILE * 512 + lists.reshape(-1)[slots]
+    rows = lax.all_to_all(
+        jnp.broadcast_to(rows.reshape(1, 4, 128), (16, 4, 128)), SEQ, split_axis=0, concat_axis=0, tiled=True
+    )
+    rows = rows.reshape(16, 2, 256).transpose(1, 0, 2).reshape(2, 4096)
+    w_both = jnp.concatenate([w_key, w_value], axis=1)
+    w_hi, w_lo = split_xla(w_both)
+    w_hi, w_lo = w_hi.astype(BF), w_lo.astype(BF)
+    history, both = front(pieces, table_place(rows, me), w_hi, w_lo, 4096)
+    inputs = lax.dynamic_slice_in_dim(history, seq * 256, 256, 0)
     cotangent = grad_attended[0]
     scale = HEAD_DIM ** (-0.5)
     queries = product(inputs, w_query, EXACT) * scale
     grad_context = product(cotangent, w_out.T)
-    w_both = jnp.concatenate([w_key, w_value], axis=1)
-    both = product(history, w_both)
     context_t, grad_queries_t, grad_keys, grad_values = make(SPAN)(
         *operands(queries, grad_context, session_tiles[0]), both
     )
@@ -203,43 +448,37 @@
     attended = product(context, w_out)
     grad_out_w = product(context_t, cotangent)
     grad_query_w = product(inputs.T, grad_queries)
-    grad_key_w = product(history.T, grad_keys)
-    grad_value_w = product(history.T, grad_values)
-    partial = product(grad_keys, w_key.T) + product(grad_values, w_value.T)
-    grad_inputs = lax.psum_scatter(partial, "seq", scatter_dimension=0, tiled=True)
-    grad_inputs = grad_inputs + product(grad_queries, w_query.T)
-    doubled = jnp.concatenate([grad_inputs, grad_inputs], axis=0)
-    slot_grads = jax.ops.segment_sum(
-        doubled, jnp.concatenate([slots[0], slots[1]]), num_segments=slot_rows.shape[0]
+    query_terms = product(grad_queries, w_query.T)
+    terms, grad_both_w = back(
+        scatter_place(rows, me), seq.reshape(1), grad_keys, grad_values, history, w_hi.T, w_lo.T, query_terms, 4096
     )
-    returned = lax.all_to_all(
-        slot_grads.reshape(arrived.shape), "dp", split_axis=0, concat_axis=0, tiled=True
-    )
-    table_terms = jax.ops.segment_sum(
-        returned.reshape(-1, width), lists.reshape(-1), num_segments=item_table.shape[0]
-    )
-    grad_table = lax.psum_scatter(table_terms, "seq", scatter_dimension=0, tiled=True)
-    grad_query_w, grad_key_w, grad_value_w, grad_out_w = lax.psum(
-        (grad_query_w, grad_key_w, grad_value_w, grad_out_w), ("dp", "seq")
-    )
+    sums = sum_everywhere([grad_both_w, jnp.concatenate([grad_query_w, grad_out_w], axis=0)], me)
+    grad_key_w, grad_value_w = sums[0][:512].T, sums[0][512:].T
+    grad_query_w, grad_out_w = sums[1][:512], sums[1][512:]
+    cuts, at = [], 0
+    for n in PART_ROWS:
+        cuts.append(terms[at * 512:(at + n) * 512])
+        at += n
+    grad_table = jnp.concatenate(scatter_parts(cuts, PARTS), axis=0).reshape(32, 512)
     return (attended[None], grad_query_w, grad_key_w, grad_value_w, grad_out_w, grad_table)
 
 
 def solution(mesh):
+    fine = Mesh(mesh.devices.reshape(2, 4, 4, 2, 2), ("zl", "x", "y", "zh", "c"))
     return jax.shard_map(
         on_device,
-        mesh=mesh,
+        mesh=fine,
         in_specs=(
-            P("dp", None),
-            P("dp", None, "seq", None),
-            P("dp", None, "seq"),
-            P("dp", "seq", None),
+            P(DP, None),
+            P(DP, None, SEQ, None),
+            P(DP, None, SEQ),
+            P(DP, SEQ, None),
             P(),
             P(),
             P(),
             P(),
-            P("dp", "seq", None),
+            P(DP, SEQ, None),
         ),
-        out_specs=(P("dp", "seq", None), P(), P(), P(), P(), P(("dp", "seq"), None)),
+        out_specs=(P(DP, SEQ, None), P(), P(), P(), P(), P(DP + SEQ, None)),
         check_vma=False,
     )

time: 619 us -> 497 us (0.80)
  waiting for transfers between devices: 332 us -> 58.3 us
  starting transfers between devices: 6.5 us -> 131 us
  Pallas kernels: 93.7 us -> 190 us
  matrix products: 88.8 us -> 11.3 us
  local copies, waits for them, and re-layouts: 24.2 us -> 68.6 us
  blocking collectives: 34.3 us -> 0 us
  between operations: 14.2 us -> 1.93 us
  other arithmetic: 19.7 us -> 27 us
    reduce_scatter x2 -> x0, waiting for transfers between devices: 125 us -> none  [the longest x1 67.7 us: on_device(): lax.psum_scatter(table_terms, 'seq', scatter_dimension=0, tiled=True)]
    ppermute x0 -> x91, starting transfers between devices: none -> 122 us  [shift(): lax.ppermute(v, axis, [(place(i), place((i + s) % n)) for i in range(n)])]
    psum x1 -> x0, waiting for transfers between devices: 119 us -> none  [on_device(): lax.psum((grad_query_w, grad_key_w, grad_value_w, grad_out_w), ('dp', 'se...]
    pallas_call x0 -> x2, Pallas kernels: none -> 96.6 us  [the longest x1 57.2 us: back(): pl.pallas_call(kernel, grid=(rows // span,), in_specs=[pl.BlockSpec(memor...]
    dot_general x11 -> x6, matrix products: 88.8 us -> 11.3 us  [product(): return jnp.dot(left, right, precision=precision, preferred_element_type=F32)]
    all_gather x1 -> x0, waiting for transfers between devices: 61.3 us -> none  [on_device(): history = lax.all_gather(inputs, 'seq', axis=0, tiled=True)]
    ppermute x0 -> x91, waiting for transfers between devices: none -> 55.1 us  [shift(): lax.ppermute(v, axis, [(place(i), place((i + s) % n)) for i in range(n)])]
    all_to_all x1 -> x0, blocking collectives: 34.3 us -> none  [on_device(): lax.all_to_all(slot_grads.reshape(arrived.shape), 'dp', split_axis=0, con...]
  transfers between devices with their start and end apart: 5 -> 93, of which waited for: 5 -> 32; matrix products, arithmetic and copies ran while one was open for 12% -> 16% of each run, Pallas kernels for 0% -> 0%
where the time goes in v2:
time: 497 us; the launch traced here: 489 us
  Pallas kernels  190 us (38%)
  starting transfers between devices  131 us (26%)
  local copies, waits for them, and re-layouts  68.6 us (14%)
  waiting for transfers between devices  58.3 us (12%)
  other arithmetic  27 us (5%)
  matrix products  11.3 us (2%)
    ppermute x91, starting transfers between devices, shift(): lax.ppermute(v, axis, [(place(i), place((i + s) % n)) for i in range(n)])  122 us
    pallas_call x1, Pallas kernels, call(): pl.pallas_call(kernel, grid=(pairs,), in_specs=[pl.BlockSpec(bias.shape,...  93.8 us
    pallas_call x1, Pallas kernels, back(): pl.pallas_call(kernel, grid=(rows // span,), in_specs=[pl.BlockSpec(memor...  57.2 us
    ppermute x91, waiting for transfers between devices, shift(): lax.ppermute(v, axis, [(place(i), place((i + s) % n)) for i in range(n)])  55.1 us
    pallas_call x1, Pallas kernels, front(): pl.pallas_call(kernel, grid=(rows // span,), in_specs=[pl.BlockSpec(memor...  39.5 us
    unnamed x91, local copies, waits for them, and re-layouts  27.6 us
    dot_general x6, matrix products, product(): return jnp.dot(left, right, precision=precision, preferred_element_type=F32)  11.3 us
  transfers between devices with their start and end apart: 93, of which 32 were waited for; matrix products, arithmetic and copies ran while one was open for 16% of the time, Pallas kernels for 0%

profile of v2, /device:TPU:1, one launch (start us, length us, event | category | flops | bytes accessed | tf_op | source)
XLA Modules:
  0.0 488.9 jit_solution(7985216353246631728)
XLA Ops:
  3.1 2.0 collective-permute-start
  9.0 2.1 collective-permute-start.7
  11.1 3.3 all-to-all-start
  24.0 2.3 gather_fusion
  33.5 2.6 collective-permute-start.3
  41.0 2.4 collective-permute-done.2
  54.1 4.7 collective-permute-start.13
  60.3 6.0 %all-to-all-start.1 = ((s32[16,4,128]{2,1,0:T(4,128)}), s32[16,4,128]{2,1,0:T(4,128)S(1)}, u32[]{:S(2)}, u32[]{:S(2)}) async-start(s32[16,4,128]{2,1,0:T(4,128)} %broadcast_in_dim.38), calls=%async_computation.1 | async-start | bytes 65536 | tf_op jit(solution)/shard_map/all_to_all | solution.py:430
  70.4 3.2 all-to-all-done.1
  76.1 39.5 %shard_map.136 = (f32[4096,512]{1,0:T(8,128)}, f32[4096,1024]{1,0:T(8,128)}) custom-call(s32[2,4096]{1,0:T(2,128)} %fusion.38.refs_0_, f32[4096,128]{1,0:T(8,128)} %constant_dynamic-update-slice_fusion.refs_1_, f32[4096,128]{1,0:T(8,128)} %constant_dynamic-update-slice_fusion.7.refs_2_, f32[4096,128]{1,0:T(8,128)} %collective-permute-done.12.refs_3_, ...), custom_call_target="tpu_custom_call" | custom-call | tf_op jit(solution)/shard_map/pallas_call | solution.py:204
  115.6 2.9 broadcast_multiply_fusion
  122.1 2.1 copy.36
  127.5 93.8 %shard_map.137 = (f32[512,256]{1,0:T(8,128)}, f32[512,256]{1,0:T(8,128)}, f32[4096,512]{1,0:T(8,128)}, f32[4096,512]{1,0:T(8,128)}) custom-call(f32[32,256]{1,0:T(8,128)} %bitcast.94, bf16[8,256,256]{2,1,0:T(8,128)(2,1)} %pad_maximum_fusion.1.qt4, bf16[8,256,128]{2,1,0:T(8,128)(2,1)} %pad_maximum_fusion.5.qs2, f32[8,64,256]{2,1,0:T(8,128)} %fusion.5.dot_, ...), custom_call_target="tpu_custom_call" | custom-call | tf_op jit(solution)/shard_map/pallas_call | solution.py:118
  221.3 2.9 fusion.9.qx_ref
  224.2 57.2 %shard_map.138 = (f32[16384,128]{1,0:T(8,128)}, f32[1024,512]{1,0:T(8,128)}) custom-call(s32[2,4096]{1,0:T(2,128)} %get-tuple-element.36.idx, s32[1]{0:T(128)} %bitcast.24.own_ref, f32[4096,512]{1,0:T(8,128)} %get-tuple-element.18.dk_ref, f32[4096,512]{1,0:T(8,128)} %get-tuple-element.19.dv_ref, f32[4096,512]{1,0:T(8,128)} %get-tuple-element.14.x_ref, ...), custom_call_target="tpu_custom_call" | custom-call | tf_op jit(solution)/shard_map/pallas_call | solution.py:262
  281.4 3.0 slice.448
  284.4 2.3 slice.468
  287.5 2.4 gather_fusion.3
  291.4 2.1 fusion.11
  295.6 3.7 gather_fusion.1
  303.2 2.4 collective-permute-start.70
  308.9 2.8 collective-permute-done.71
  311.7 5.4 %collective-permute-done.38 = f32[128,512]{1,0:T(8,128)S(1)} collective-permute-done((f32[128,512]{1,0:T(8,128)S(1)}, f32[128,512]{1,0:T(8,128)S(1)}, u32[]{:S(2)}, u32[]{:S(2)}) %collective-permute-start.38) | collective-permute-done | bytes 262176 | tf_op jit(solution)/shard_map/ppermute | solution.py:282
  319.5 2.7 collective-permute-start.15
  322.2 2.2 collective-permute-done.72
  325.2 4.3 collective-permute-done.39
  336.2 2.2 collective-permute-done.19
  338.9 2.7 collective-permute-start.42
  353.8 2.7 collective-permute-start.23
  357.6 2.2 collective-permute-start.47
  368.0 2.2 collective-permute-start.50
  372.1 2.1 collective-permute-start.52
  385.4 2.3 collective-permute-start.79
  393.6 4.4 collective-permute-done.32
  399.0 2.7 collective-permute-start.34
  403.9 2.4 slice_add_fusion
  407.4 2.4 collective-permute-done.82
  411.5 3.6 collective-permute-done.81
  415.1 2.6 collective-permute-start.59
  417.8 23.4 %collective-permute-start.57 = (f32[512,512]{1,0:T(8,128)S(1)}, f32[512,512]{1,0:T(8,128)S(1)}, u32[]{:S(2)}, u32[]{:S(2)}) collective-permute-start(f32[512,512]{1,0:T(8,128)S(1)} %get-tuple-element.85), channel_id=1, source_target_pairs={{0,1},{1,0},{2,3},{3,2},{4,5},{5,4},{6,7},{7,6},{8,9},{9,8},{10,11... | collective-permute-start | bytes 3145736 | tf_op jit(solution)/shard_map/ppermute | solution.py:282
  444.2 2.2 collective-permute-done.85
  451.4 2.7 collective-permute-start.89
  454.0 3.1 collective-permute-done.61
  458.0 2.4 collective-permute-start.35
  467.6 2.4 gather_fusion.4
  475.0 2.4 gather_fusion.2
  479.2 2.7 collective-permute-start.67
  484.0 2.6 copy.39
  (351 shorter events, 148.3 us)
Async XLA Ops:
  3.1 29.3 %collective-permute-start = (f32[512,128]{1,0:T(8,128)}, f32[512,128]{1,0:T(8,128)}, u32[]{:S(2)}, u32[]{:S(2)}) collective-permute-start(f32[512,128]{1,0:T(8,128)} %get-tuple-element.78), channel_id=1, source_target_pairs={{0,16},{16,32},{32,48},{48,0},{1,17},{17,33},{33,49},{49,1},{2,18}... | collective-permute-start | bytes 786440 | tf_op jit(solution)/shard_map/ppermute | solution.py:282
  5.2 28.4 %collective-permute-start.1 = (f32[512,128]{1,0:T(8,128)}, f32[512,128]{1,0:T(8,128)S(1)}, u32[]{:S(2)}, u32[]{:S(2)}) collective-permute-start(f32[512,128]{1,0:T(8,128)} %get-tuple-element.78), channel_id=1, source_target_pairs={{0,48},{16,0},{32,16},{48,32},{1,49},{17,1},{33,17},{49,33},{2,50}... | collective-permute-start | bytes 786440 | tf_op jit(solution)/shard_map/ppermute | solution.py:282
  7.2 19.2 %collective-permute-start.6 = (f32[256,128]{1,0:T(8,128)}, f32[256,128]{1,0:T(8,128)S(1)}, u32[]{:S(2)}, u32[]{:S(2)}) collective-permute-start(f32[256,128]{1,0:T(8,128)} %get-tuple-element.76), channel_id=1, source_target_pairs={{0,64},{64,2},{2,66},{66,0},{1,65},{65,3},{3,67},{67,1},{4,68},{68... | collective-permute-start | bytes 393224 | tf_op jit(solution)/shard_map/ppermute | solution.py:282
  9.0 17.3 %collective-permute-start.7 = (f32[256,128]{1,0:T(8,128)}, f32[256,128]{1,0:T(8,128)}, u32[]{:S(2)}, u32[]{:S(2)}) collective-permute-start(f32[256,128]{1,0:T(8,128)} %get-tuple-element.75), channel_id=1, source_target_pairs={{0,66},{64,0},{2,64},{66,2},{1,67},{65,1},{3,65},{67,3},{4,70},{68... | collective-permute-start | bytes 393224 | tf_op jit(solution)/shard_map/ppermute | solution.py:282
  11.1 12.9 %all-to-all-start = ((s32[8,1,128]{2,1,0:T(1,128)}), s32[8,1,128]{2,1,0:T(1,128)S(1)}, u32[]{:S(2)}, u32[]{:S(2)}) async-start(s32[8,1,128]{2,1,0:T(1,128)} %bitcast.2), calls=%async_computation | async-start | bytes 8192 | tf_op jit(solution)/shard_map/all_to_all | solution.py:427
  27.4 18.7 %collective-permute-start.8 = (f32[1024,128]{1,0:T(8,128)S(1)}, f32[1024,128]{1,0:T(8,128)S(1)}, u32[]{:S(2)}, u32[]{:S(2)}) collective-permute-start(f32[1024,128]{1,0:T(8,128)S(1)} %pad_maximum_fusion.4), channel_id=1, source_target_pairs={{0,16},{16,32},{32,48},{48,0},{1,17},{17,33},{33,49},{49,1},{2,18}... | collective-permute-start | bytes 1572872 | tf_op jit(solution)/shard_map/ppermute | solution.py:282
  28.8 18.3 %collective-permute-start.9 = (f32[1024,128]{1,0:T(8,128)S(1)}, f32[1024,128]{1,0:T(8,128)S(1)}, u32[]{:S(2)}, u32[]{:S(2)}) collective-permute-start(f32[1024,128]{1,0:T(8,128)S(1)} %pad_maximum_fusion.4), channel_id=1, source_target_pairs={{0,48},{16,0},{32,16},{48,32},{1,49},{17,1},{33,17},{49,33},{2,50}... | collective-permute-start | bytes 1572872 | tf_op jit(solution)/shard_map/ppermute | solution.py:282
  33.3 10.1 %collective-permute-start.2 = (f32[256,128]{1,0:T(8,128)S(1)}, f32[256,128]{1,0:T(8,128)S(1)}, u32[]{:S(2)}, u32[]{:S(2)}) collective-permute-start(f32[256,128]{1,0:T(8,128)S(1)} %slice.517), channel_id=1, source_target_pairs={{0,16},{16,32},{32,48},{48,0},{1,17},{17,33},{33,49},{49,1},{2,18}... | collective-permute-start | bytes 393224 | tf_op jit(solution)/shard_map/ppermute | solution.py:282
  33.5 9.9 %collective-permute-start.3 = (f32[256,128]{1,0:T(8,128)S(1)}, f32[256,128]{1,0:T(8,128)S(1)}, u32[]{:S(2)}, u32[]{:S(2)}) collective-permute-start(f32[256,128]{1,0:T(8,128)S(1)} %slice.518), channel_id=1, source_target_pairs={{0,48},{16,0},{32,16},{48,32},{1,49},{17,1},{33,17},{49,33},{2,50}... | collective-permute-start | bytes 393224 | tf_op jit(solution)/shard_map/ppermute | solution.py:282
  37.2 13.5 %collective-permute-start.4 = (f32[1024,128]{1,0:T(8,128)S(1)}, f32[1024,128]{1,0:T(8,128)S(1)}, u32[]{:S(2)}, u32[]{:S(2)}) collective-permute-start(f32[1024,128]{1,0:T(8,128)S(1)} %pad_maximum_fusion.2), channel_id=1, source_target_pairs={{0,64},{64,2},{2,66},{66,0},{1,65},{65,3},{3,67},{67,1},{4,68},{68... | collective-permute-start | bytes 1572872 | tf_op jit(solution)/shard_map/ppermute | solution.py:282
  43.4 15.4 %collective-permute-start.5 = (f32[1024,128]{1,0:T(8,128)S(1)}, f32[1024,128]{1,0:T(8,128)S(1)}, u32[]{:S(2)}, u32[]{:S(2)}) collective-permute-start(f32[1024,128]{1,0:T(8,128)S(1)} %pad_maximum_fusion.3), channel_id=1, source_target_pairs={{0,66},{64,0},{2,64},{66,2},{1,67},{65,1},{3,65},{67,3},{4,70},{68... | collective-permute-start | bytes 1572872 | tf_op jit(solution)/shard_map/ppermute | solution.py:282
  54.1 22.0 %collective-permute-start.13 = (f32[4096,128]{1,0:T(8,128)}, f32[4096,128]{1,0:T(8,128)}, u32[]{:S(2)}, u32[]{:S(2)}) collective-permute-start(f32[4096,128]{1,0:T(8,128)} %constant_dynamic-update-slice_fusion.7.refs_2_), channel_id=1, source_target_pairs={{0,1},{1,0},{2,3},{3,2},{4,5},{5,4},{6,7},{7,6},{8,9},{9,8},{10,11... | collective-permute-start | bytes 6291464 | tf_op jit(solution)/shard_map/ppermute | solution.py:282
  59.7 16.4 %collective-permute-start.12 = (f32[4096,128]{1,0:T(8,128)}, f32[4096,128]{1,0:T(8,128)}, u32[]{:S(2)}, u32[]{:S(2)}) collective-permute-start(f32[4096,128]{1,0:T(8,128)} %constant_dynamic-update-slice_fusion.refs_1_), channel_id=1, source_target_pairs={{0,1},{1,0},{2,3},{3,2},{4,5},{5,4},{6,7},{7,6},{8,9},{9,8},{10,11... | collective-permute-start | bytes 6291464 | tf_op jit(solution)/shard_map/ppermute | solution.py:282
  60.3 13.2 %all-to-all-start.1 = ((s32[16,4,128]{2,1,0:T(4,128)}), s32[16,4,128]{2,1,0:T(4,128)S(1)}, u32[]{:S(2)}, u32[]{:S(2)}) async-start(s32[16,4,128]{2,1,0:T(4,128)} %broadcast_in_dim.38), calls=%async_computation.1 | async-start | bytes 65536 | tf_op jit(solution)/shard_map/all_to_all | solution.py:430
  286.6 116.5 %collective-permute-start.58 = (f32[4096,128]{1,0:T(8,128)}, f32[4096,128]{1,0:T(8,128)}, u32[]{:S(2)}, u32[]{:S(2)}) collective-permute-start(f32[4096,128]{1,0:T(8,128)} %slice.448), channel_id=1, source_target_pairs={{0,1},{1,0},{2,3},{3,2},{4,5},{5,4},{6,7},{7,6},{8,9},{9,8},{10,11... | collective-permute-start | bytes 6291464 | tf_op jit(solution)/shard_map/ppermute | solution.py:282
  287.4 13.4 %collective-permute-start.69 = (f32[2048,128]{1,0:T(8,128)}, f32[2048,128]{1,0:T(8,128)}, u32[]{:S(2)}, u32[]{:S(2)}) collective-permute-start(f32[2048,128]{1,0:T(8,128)} %slice.468), channel_id=1, source_target_pairs={{0,1},{1,0},{2,3},{3,2},{4,5},{5,4},{6,7},{7,6},{8,9},{9,8},{10,11... | collective-permute-start | bytes 3145736 | tf_op jit(solution)/shard_map/ppermute | solution.py:282
  291.0 14.6 %collective-permute-start.36 = (f32[512,512]{1,0:T(8,128)}, f32[512,512]{1,0:T(8,128)}, u32[]{:S(2)}, u32[]{:S(2)}) collective-permute-start(f32[512,512]{1,0:T(8,128)} %slice_bitcast_fusion.3), channel_id=1, source_target_pairs={{0,1},{1,0},{2,3},{3,2},{4,5},{5,4},{6,7},{7,6},{8,9},{9,8},{10,11... | collective-permute-start | bytes 3145736 | tf_op jit(solution)/shard_map/ppermute | solution.py:282
  300.6 7.5 %collective-permute-start.14 = (f32[512,512]{1,0:T(8,128)S(1)}, f32[512,512]{1,0:T(8,128)S(1)}, u32[]{:S(2)}, u32[]{:S(2)}) collective-permute-start(f32[512,512]{1,0:T(8,128)S(1)} %slice_bitcast_fusion.6), channel_id=1, source_target_pairs={{0,1},{1,0},{2,3},{3,2},{4,5},{5,4},{6,7},{7,6},{8,9},{9,8},{10,11... | collective-permute-start | bytes 3145736 | tf_op jit(solution)/shard_map/ppermute | solution.py:282
  302.9 8.8 %collective-permute-start.71 = (f32[512,128]{1,0:T(8,128)S(1)}, f32[512,128]{1,0:T(8,128)S(1)}, u32[]{:S(2)}, u32[]{:S(2)}) collective-permute-start(f32[512,128]{1,0:T(8,128)S(1)} %get-tuple-element.65), channel_id=1, source_target_pairs={{0,4},{4,8},{8,12},{12,0},{1,5},{5,9},{9,13},{13,1},{2,6},{6,10},{... | collective-permute-start | bytes 786440 | tf_op jit(solution)/shard_map/ppermute | solution.py:282
  303.2 16.3 %collective-permute-start.70 = (f32[512,128]{1,0:T(8,128)S(1)}, f32[512,128]{1,0:T(8,128)S(1)}, u32[]{:S(2)}, u32[]{:S(2)}) collective-permute-start(f32[512,128]{1,0:T(8,128)S(1)} %get-tuple-element.66), channel_id=1, source_target_pairs={{0,12},{4,0},{8,4},{12,8},{1,13},{5,1},{9,5},{13,9},{2,14},{6,2},{... | collective-permute-start | bytes 786440 | tf_op jit(solution)/shard_map/ppermute | solution.py:282
  305.6 93.4 %collective-permute-start.80 = (f32[2048,128]{1,0:T(8,128)S(1)}, f32[2048,128]{1,0:T(8,128)S(1)}, u32[]{:S(2)}, u32[]{:S(2)}) collective-permute-start(f32[2048,128]{1,0:T(8,128)S(1)} %get-tuple-element.46), channel_id=1, source_target_pairs={{0,1},{1,0},{2,3},{3,2},{4,5},{5,4},{6,7},{7,6},{8,9},{9,8},{10,11... | collective-permute-start | bytes 3145736 | tf_op jit(solution)/shard_map/ppermute | solution.py:282
  308.1 9.0 %collective-permute-start.38 = (f32[128,512]{1,0:T(8,128)S(1)}, f32[128,512]{1,0:T(8,128)S(1)}, u32[]{:S(2)}, u32[]{:S(2)}) collective-permute-start(f32[128,512]{1,0:T(8,128)S(1)} %get-tuple-element.69), channel_id=1, source_target_pairs={{0,16},{16,32},{32,48},{48,0},{1,17},{17,33},{33,49},{49,1},{2,18}... | collective-permute-start | bytes 786440 | tf_op jit(solution)/shard_map/ppermute | solution.py:282
  311.7 7.8 %collective-permute-start.16 = (f32[128,512]{1,0:T(8,128)S(1)}, f32[128,512]{1,0:T(8,128)S(1)}, u32[]{:S(2)}, u32[]{:S(2)}) collective-permute-start(f32[128,512]{1,0:T(8,128)S(1)} %get-tuple-element.71), channel_id=1, source_target_pairs={{0,4},{4,8},{8,12},{12,0},{1,5},{5,9},{9,13},{13,1},{2,6},{6,10},{... | collective-permute-start | bytes 786440 | tf_op jit(solution)/shard_map/ppermute | solution.py:282
  317.1 8.0 %collective-permute-start.37 = (f32[128,512]{1,0:T(8,128)S(1)}, f32[128,512]{1,0:T(8,128)S(1)}, u32[]{:S(2)}, u32[]{:S(2)}) collective-permute-start(f32[128,512]{1,0:T(8,128)S(1)} %get-tuple-element.70), channel_id=1, source_target_pairs={{0,48},{16,0},{32,16},{48,32},{1,49},{17,1},{33,17},{49,33},{2,50}... | collective-permute-start | bytes 786440 | tf_op jit(solution)/shard_map/ppermute | solution.py:282
  319.5 10.1 %collective-permute-start.15 = (f32[128,512]{1,0:T(8,128)S(1)}, f32[128,512]{1,0:T(8,128)S(1)}, u32[]{:S(2)}, u32[]{:S(2)}) collective-permute-start(f32[128,512]{1,0:T(8,128)S(1)} %get-tuple-element.72), channel_id=1, source_target_pairs={{0,12},{4,0},{8,4},{12,8},{1,13},{5,1},{9,5},{13,9},{2,14},{6,2},{... | collective-permute-start | bytes 786440 | tf_op jit(solution)/shard_map/ppermute | solution.py:282
  329.6 9.2 %collective-permute-start.73 = (f32[128,128]{1,0:T(8,128)S(1)}, f32[128,128]{1,0:T(8,128)S(1)}, u32[]{:S(2)}, u32[]{:S(2)}) collective-permute-start(f32[128,128]{1,0:T(8,128)S(1)} %slice.594), channel_id=1, source_target_pairs={{0,64},{64,2},{2,66},{66,0},{1,65},{65,3},{3,67},{67,1},{4,68},{68... | collective-permute-start | bytes 196616 | tf_op jit(solution)/shard_map/ppermute | solution.py:282
  365.6 16.5 %collective-permute-start.77 = (f32[32,128]{1,0:T(8,128)S(1)}, f32[32,128]{1,0:T(8,128)S(1)}, u32[]{:S(2)}, u32[]{:S(2)}) collective-permute-start(f32[32,128]{1,0:T(8,128)S(1)} %get-tuple-element.112), channel_id=1, source_target_pairs={{0,16},{16,32},{32,48},{48,0},{1,17},{17,33},{33,49},{49,1},{2,18}... | collective-permute-start | bytes 49160 | tf_op jit(solution)/shard_map/ppermute | solution.py:282
  377.9 13.3 %collective-permute-start.54 = (f32[128,512]{1,0:T(8,128)S(1)}, f32[128,512]{1,0:T(8,128)S(1)}, u32[]{:S(2)}, u32[]{:S(2)}) collective-permute-start(f32[128,512]{1,0:T(8,128)S(1)} %get-tuple-element.120), channel_id=1, source_target_pairs={{0,16},{16,32},{32,48},{48,0},{1,17},{17,33},{33,49},{49,1},{2,18}... | collective-permute-start | bytes 786440 | tf_op jit(solution)/shard_map/ppermute | solution.py:282
  389.8 8.4 %collective-permute-start.31 = (f32[128,512]{1,0:T(8,128)S(1)}, f32[128,512]{1,0:T(8,128)S(1)}, u32[]{:S(2)}, u32[]{:S(2)}) collective-permute-start(f32[128,512]{1,0:T(8,128)S(1)} %get-tuple-element.132), channel_id=1, source_target_pairs={{0,12},{4,0},{8,4},{12,8},{1,13},{5,1},{9,5},{13,9},{2,14},{6,2},{... | collective-permute-start | bytes 786440 | tf_op jit(solution)/shard_map/ppermute | solution.py:282
  391.3 6.7 %collective-permute-start.32 = (f32[128,512]{1,0:T(8,128)S(1)}, f32[128,512]{1,0:T(8,128)S(1)}, u32[]{:S(2)}, u32[]{:S(2)}) collective-permute-start(f32[128,512]{1,0:T(8,128)S(1)} %get-tuple-element.132), channel_id=1, source_target_pairs={{0,4},{4,8},{8,12},{12,0},{1,5},{5,9},{9,13},{13,1},{2,6},{6,10},{... | collective-permute-start | bytes 786440 | tf_op jit(solution)/shard_map/ppermute | solution.py:282
  393.6 12.9 %collective-permute-start.55 = (f32[64,512]{1,0:T(8,128)S(1)}, f32[64,512]{1,0:T(8,128)S(1)}, u32[]{:S(2)}, u32[]{:S(2)}) collective-permute-start(f32[64,512]{1,0:T(8,128)S(1)} %slice.564), channel_id=1, source_target_pairs={{0,16},{16,32},{32,48},{48,0},{1,17},{17,33},{33,49},{49,1},{2,18}... | collective-permute-start | bytes 393224 | tf_op jit(solution)/shard_map/ppermute | solution.py:282
  398.0 12.4 %collective-permute-start.56 = (f32[64,512]{1,0:T(8,128)S(1)}, f32[64,512]{1,0:T(8,128)S(1)}, u32[]{:S(2)}, u32[]{:S(2)}) collective-permute-start(f32[64,512]{1,0:T(8,128)S(1)} %slice.565), channel_id=1, source_target_pairs={{0,48},{16,0},{32,16},{48,32},{1,49},{17,1},{33,17},{49,33},{2,50}... | collective-permute-start | bytes 393224 | tf_op jit(solution)/shard_map/ppermute | solution.py:282
  398.1 43.1 %collective-permute-start.33 = (f32[64,512]{1,0:T(8,128)S(1)}, f32[64,512]{1,0:T(8,128)S(1)}, u32[]{:S(2)}, u32[]{:S(2)}) collective-permute-start(f32[64,512]{1,0:T(8,128)S(1)} %slice.541), channel_id=1, source_target_pairs={{0,4},{4,8},{8,12},{12,0},{1,5},{5,9},{9,13},{13,1},{2,6},{6,10},{... | collective-permute-start | bytes 393224 | tf_op jit(solution)/shard_map/ppermute | solution.py:282
  399.0 43.8 %collective-permute-start.34 = (f32[64,512]{1,0:T(8,128)S(1)}, f32[64,512]{1,0:T(8,128)S(1)}, u32[]{:S(2)}, u32[]{:S(2)}) collective-permute-start(f32[64,512]{1,0:T(8,128)S(1)} %slice.542), channel_id=1, source_target_pairs={{0,12},{4,0},{8,4},{12,8},{1,13},{5,1},{9,5},{13,9},{2,14},{6,2},{... | collective-permute-start | bytes 393224 | tf_op jit(solution)/shard_map/ppermute | solution.py:282
  403.1 6.7 %collective-permute-start.82 = (f32[512,128]{1,0:T(8,128)S(1)}, f32[512,128]{1,0:T(8,128)S(1)}, u32[]{:S(2)}, u32[]{:S(2)}) collective-permute-start(f32[512,128]{1,0:T(8,128)S(1)} %get-tuple-element.67), channel_id=1, source_target_pairs={{0,64},{64,2},{2,66},{66,0},{1,65},{65,3},{3,67},{67,1},{4,68},{68... | collective-permute-start | bytes 786440 | tf_op jit(solution)/shard_map/ppermute | solution.py:282
  406.4 40.1 %collective-permute-start.60 = (f32[1024,128]{1,0:T(8,128)S(1)}, f32[1024,128]{1,0:T(8,128)S(1)}, u32[]{:S(2)}, u32[]{:S(2)}) collective-permute-start(f32[1024,128]{1,0:T(8,128)S(1)} %get-tuple-element.49), channel_id=1, source_target_pairs={{0,16},{16,32},{32,48},{48,0},{1,17},{17,33},{33,49},{49,1},{2,18}... | collective-permute-start | bytes 1572872 | tf_op jit(solution)/shard_map/ppermute | solution.py:282
  410.5 7.3 %collective-permute-start.83 = (f32[256,128]{1,0:T(8,128)S(1)}, f32[256,128]{1,0:T(8,128)S(1)}, u32[]{:S(2)}, u32[]{:S(2)}) collective-permute-start(f32[256,128]{1,0:T(8,128)S(1)} %slice_add_fusion.9), channel_id=1, source_target_pairs={{0,64},{64,2},{2,66},{66,0},{1,65},{65,3},{3,67},{67,1},{4,68},{68... | collective-permute-start | bytes 393224 | tf_op jit(solution)/shard_map/ppermute | solution.py:282
  415.1 38.9 %collective-permute-start.59 = (f32[1024,128]{1,0:T(8,128)S(1)}, f32[1024,128]{1,0:T(8,128)S(1)}, u32[]{:S(2)}, u32[]{:S(2)}) collective-permute-start(f32[1024,128]{1,0:T(8,128)S(1)} %get-tuple-element.50), channel_id=1, source_target_pairs={{0,48},{16,0},{32,16},{48,32},{1,49},{17,1},{33,17},{49,33},{2,50}... | collective-permute-start | bytes 1572872 | tf_op jit(solution)/shard_map/ppermute | solution.py:282
  417.8 48.4 %collective-permute-start.57 = (f32[512,512]{1,0:T(8,128)S(1)}, f32[512,512]{1,0:T(8,128)S(1)}, u32[]{:S(2)}, u32[]{:S(2)}) collective-permute-start(f32[512,512]{1,0:T(8,128)S(1)} %get-tuple-element.85), channel_id=1, source_target_pairs={{0,1},{1,0},{2,3},{3,2},{4,5},{5,4},{6,7},{7,6},{8,9},{9,8},{10,11... | collective-permute-start | bytes 3145736 | tf_op jit(solution)/shard_map/ppermute | solution.py:282
  448.2 8.9 %collective-permute-start.61 = (f32[512,128]{1,0:T(8,128)S(1)}, f32[512,128]{1,0:T(8,128)S(1)}, u32[]{:S(2)}, u32[]{:S(2)}) collective-permute-start(f32[512,128]{1,0:T(8,128)S(1)} %slice_add_fusion.5), channel_id=1, source_target_pairs={{0,16},{16,32},{32,48},{48,0},{1,17},{17,33},{33,49},{49,1},{2,18}... | collective-permute-start | bytes 786440 | tf_op jit(solution)/shard_map/ppermute | solution.py:282
  451.3 6.7 %collective-permute-start.88 = (f32[32,128]{1,0:T(8,128)S(1)}, f32[32,128]{1,0:T(8,128)S(1)}, u32[]{:S(2)}, u32[]{:S(2)}) collective-permute-start(f32[32,128]{1,0:T(8,128)S(1)} %get-tuple-element.115), channel_id=1, source_target_pairs={{0,4},{4,8},{8,12},{12,0},{1,5},{5,9},{9,13},{13,1},{2,6},{6,10},{... | collective-permute-start | bytes 49160 | tf_op jit(solution)/shard_map/ppermute | solution.py:282
  451.4 9.0 %collective-permute-start.89 = (f32[32,128]{1,0:T(8,128)S(1)}, f32[32,128]{1,0:T(8,128)S(1)}, u32[]{:S(2)}, u32[]{:S(2)}) collective-permute-start(f32[32,128]{1,0:T(8,128)S(1)} %get-tuple-element.117), channel_id=1, source_target_pairs={{0,12},{4,0},{8,4},{12,8},{1,13},{5,1},{9,5},{13,9},{2,14},{6,2},{... | collective-permute-start | bytes 49160 | tf_op jit(solution)/shard_map/ppermute | solution.py:282
  458.0 13.5 %collective-permute-start.35 = (f32[512,512]{1,0:T(8,128)}, f32[512,512]{1,0:T(8,128)}, u32[]{:S(2)}, u32[]{:S(2)}) collective-permute-start(f32[512,512]{1,0:T(8,128)} %get-tuple-element.89), channel_id=1, source_target_pairs={{0,1},{1,0},{2,3},{3,2},{4,5},{5,4},{6,7},{7,6},{8,9},{9,8},{10,11... | collective-permute-start | bytes 3145736 | tf_op jit(solution)/shard_map/ppermute | solution.py:282
  461.7 15.7 %collective-permute-start.62 = (f32[256,128]{1,0:T(8,128)}, f32[256,128]{1,0:T(8,128)S(1)}, u32[]{:S(2)}, u32[]{:S(2)}) collective-permute-start(f32[256,128]{1,0:T(8,128)} %slice.576), channel_id=1, source_target_pairs={{0,4},{4,8},{8,12},{12,0},{1,5},{5,9},{9,13},{13,1},{2,6},{6,10},{... | collective-permute-start | bytes 393224 | tf_op jit(solution)/shard_map/ppermute | solution.py:282
  464.2 13.3 %collective-permute-start.64 = (f32[256,128]{1,0:T(8,128)}, f32[256,128]{1,0:T(8,128)}, u32[]{:S(2)}, u32[]{:S(2)}) collective-permute-start(f32[256,128]{1,0:T(8,128)} %get-tuple-element.83), channel_id=1, source_target_pairs={{0,12},{4,0},{8,4},{12,8},{1,13},{5,1},{9,5},{13,9},{2,14},{6,2},{... | collective-permute-start | bytes 393224 | tf_op jit(solution)/shard_map/ppermute | solution.py:282
  465.1 13.0 %collective-permute-start.65 = (f32[256,128]{1,0:T(8,128)}, f32[256,128]{1,0:T(8,128)}, u32[]{:S(2)}, u32[]{:S(2)}) collective-permute-start(f32[256,128]{1,0:T(8,128)} %get-tuple-element.84), channel_id=1, source_target_pairs={{0,8},{4,12},{8,0},{12,4},{1,9},{5,13},{9,1},{13,5},{2,10},{6,14},... | collective-permute-start | bytes 393224 | tf_op jit(solution)/shard_map/ppermute | solution.py:282
  479.2 8.8 %collective-permute-start.66 = (f32[64,128]{1,0:T(8,128)S(1)}, f32[64,128]{1,0:T(8,128)S(1)}, u32[]{:S(2)}, u32[]{:S(2)}) collective-permute-start(f32[64,128]{1,0:T(8,128)S(1)} %get-tuple-element.93), channel_id=1, source_target_pairs={{0,64},{64,2},{2,66},{66,0},{1,65},{65,3},{3,67},{67,1},{4,68},{68... | collective-permute-start | bytes 98312 | tf_op jit(solution)/shard_map/ppermute | solution.py:282
  479.2 8.7 %collective-permute-start.67 = (f32[64,128]{1,0:T(8,128)S(1)}, f32[64,128]{1,0:T(8,128)S(1)}, u32[]{:S(2)}, u32[]{:S(2)}) collective-permute-start(f32[64,128]{1,0:T(8,128)S(1)} %get-tuple-element.95), channel_id=1, source_target_pairs={{0,66},{64,0},{2,64},{66,2},{1,67},{65,1},{3,65},{67,3},{4,70},{68... | collective-permute-start | bytes 98312 | tf_op jit(solution)/shard_map/ppermute | solution.py:282
  (72 other events, 523.2 us)

commit v3 on v2

--- a/solution.py
+++ b/solution.py
@@ -145,7 +145,8 @@
                 pltpu.VMEM((rows, 256), BF),
                 pltpu.VMEM((rows, 256), BF),
             ],
-            compiler_params=pltpu.CompilerParams(vmem_limit_bytes=56 * 1024 * 1024),
+            compiler_params=pltpu.CompilerParams(vmem_limit_bytes=56 * MIB),
+            cost_estimate=pl.CostEstimate(flops=90_000_000_000, bytes_accessed=32 * MIB, transcendentals=8 * MIB),
         )(bias, qt4, qs2, dot_, kv, kv)
     return call
 
@@ -167,7 +168,7 @@
     return bias, qt4, qs2, dot_
 
 
-def front(pieces, slots, w_hi, w_lo, rows, span=512, unroll=8):
+def front(pieces, slots, w_hi, w_lo, rows, span=512, unroll=32):
     width = 512
     n = len(pieces)
     count = sum(p.shape[0] for p in pieces)
@@ -211,17 +212,17 @@
         out_shape=[jax.ShapeDtypeStruct((rows, width), F32), jax.ShapeDtypeStruct((rows, 2 * width), F32)],
         scratch_shapes=[pltpu.VMEM((count, 128), F32), pltpu.VMEM((span * 4, 128), F32), pltpu.SemaphoreType.DMA((n,))],
         compiler_params=pltpu.CompilerParams(vmem_limit_bytes=56 * MIB),
+        cost_estimate=pl.CostEstimate(flops=40_000_000_000, bytes_accessed=32 * MIB, transcendentals=0),
     )(slots, *pieces, w_hi, w_lo)
 
-def back(slots, own, dk, dv, x, wt_hi, wt_lo, qx, count, span=512, unroll=8, chains=4):
-    rows, width = x.shape
-    def kernel(idx, own_ref, dk_ref, dv_ref, x_ref, wh, wl, qx_ref, acc, w_ref, *more):
+def back(slots, own, dk, dv, wt_hi, wt_lo, qx, count, span=512, unroll=32, chains=4):
+    rows, width = dk.shape
+    def kernel(idx, own_ref, dk_ref, dv_ref, wh, wl, qx_ref, acc, *more):
         *others, dx, flat = more
         accs = [acc, *others]
         step = pl.program_id(0)
         @pl.when(step == 0)
         def _():
-            w_ref[...] = jnp.zeros_like(w_ref)
             def clear(i, c):
                 at = pl.ds(pl.multiple_of(i * 512, 512), 512)
                 for a in accs:
@@ -233,8 +234,6 @@
         hi = jnp.concatenate([khi, vhi], axis=1)
         lo = jnp.concatenate([klo, vlo], axis=1)
         dx[...] = dot_nn(hi, wh[...]) + dot_nn(hi, wl[...]) + dot_nn(lo, wh[...])
-        xhi, xlo = halves(x_ref[...])
-        w_ref[...] += dot_tn(hi, xhi) + dot_tn(hi, xlo) + dot_tn(lo, xhi)
         @pl.when(own_ref[0] // 2 == step)
         def _():
             at = pl.ds(pl.multiple_of(own_ref[0] % 2 * 256, 256), 256)
@@ -263,23 +262,57 @@
         kernel,
         grid=(rows // span,),
         in_specs=[pl.BlockSpec(memory_space=pltpu.SMEM)] * 2
-        + [pl.BlockSpec((span, width), lambda i: (i, 0))] * 3
+        + [pl.BlockSpec((span, width), lambda i: (i, 0))] * 2
         + [pl.BlockSpec((2 * width, width), lambda i: (0, 0))] * 2
         + [pl.BlockSpec(qx.shape, lambda i: (0, 0))],
-        out_specs=[pl.BlockSpec((count * 4, 128), lambda i: (0, 0), pipeline_mode=pl.Buffered(1)), pl.BlockSpec((2 * width, width), lambda i: (0, 0), pipeline_mode=pl.Buffered(1))],
-        out_shape=[jax.ShapeDtypeStruct((count * 4, 128), F32), jax.ShapeDtypeStruct((2 * width, width), F32)],
+        out_specs=[pl.BlockSpec((count * 4, 128), lambda i: (0, 0), pipeline_mode=pl.Buffered(1))],
+        out_shape=[jax.ShapeDtypeStruct((count * 4, 128), F32)],
         scratch_shapes=[pltpu.VMEM((count * 4, 128), F32)] * (chains - 1) + [pltpu.VMEM((span, width), F32), pltpu.VMEM((span * 4, 128), F32)],
         compiler_params=pltpu.CompilerParams(vmem_limit_bytes=56 * MIB),
-    )(slots, own, dk, dv, x, wt_hi, wt_lo, qx)
+        cost_estimate=pl.CostEstimate(flops=40_000_000_000, bytes_accessed=24 * MIB, transcendentals=0),
+    )(slots, own, dk, dv, wt_hi, wt_lo, qx)[0]
+
+
+def both_weights(dk, dv, x, span=512):
+    rows, width = x.shape
+
+    def kernel(dk_ref, dv_ref, x_ref, w_ref):
+        @pl.when(pl.program_id(0) == 0)
+        def _():
+            w_ref[...] = jnp.zeros_like(w_ref)
+
+        xhi, xlo = halves(x_ref[...])
+        for j, ref in enumerate((dk_ref, dv_ref)):
+            hi, lo = halves(ref[...])
+            w_ref[:, j * width:(j + 1) * width] += dot_tn(xhi, hi) + dot_tn(xhi, lo) + dot_tn(xlo, hi)
+
+    return pl.pallas_call(
+        kernel,
+        grid=(rows // span,),
+        in_specs=[pl.BlockSpec((span, width), lambda i: (i, 0))] * 3,
+        out_specs=pl.BlockSpec((width, 2 * width), lambda i: (0, 0)),
+        out_shape=jax.ShapeDtypeStruct((width, 2 * width), F32),
+        compiler_params=pltpu.CompilerParams(vmem_limit_bytes=56 * MIB),
+        cost_estimate=pl.CostEstimate(flops=20_000_000_000, bytes_accessed=26 * MIB, transcendentals=0),
+    )(dk, dv, x)
 
 
 Z = ("zl", "zh")
 SIZES = {"x": 4, "y": 4, Z: 4, "c": 2}
 
+
+def place(axis, i):
+    return i % 2 * 2 + i // 2 if axis == Z else i
+
+
+def move(v, axis, to):
+    n = SIZES[axis]
+    return lax.ppermute(v, axis, [(place(axis, i), place(axis, to(i))) for i in range(n)])
+
+
 def shift(v, axis, s):
-    n = SIZES[axis]
-    place = (lambda z: z % 2 * 2 + z // 2) if axis == Z else (lambda i: i)
-    return lax.ppermute(v, axis, [(place(i), place((i + s) % n)) for i in range(n)])
+    return move(v, axis, lambda i: (i + s) % SIZES[axis])
+
 
 def ring_gather(v, axis):
     n = v.shape[0] // 2
@@ -288,6 +321,7 @@
     far_a = shift(before[:n], axis, 1)
     far_b = shift(after[n:], axis, -1)
     return [v, before, after, far_a, far_b]
+
 
 def table_gather(shard):
     c = lax.axis_index("c")
@@ -308,50 +342,38 @@
     other_second = shift(second, "c", 1)
     return first, second, other_first, other_second
 
-def ring_scatter(v, axis):
-    m = v.shape[0] // 4
-    h = m // 2
-    up = shift(v[m + h:2 * m + h], axis, 1)
-    down = shift(v[2 * m + h:3 * m + h], axis, -1)
-    up2 = shift(v[m:m + h] + up[h:], axis, 1)
-    down2 = shift(v[3 * m + h:] + down[:h], axis, -1)
-    top = v[:h] + down[h:] + up2
-    low = v[h:m] + up[:h] + down2
-    return jnp.concatenate([top, low], 0)
-
-def direct_scatter(v, axis):
-    m = v.shape[0] // 4
-    a = shift(v[m:2 * m], axis, 1)
-    b = shift(v[3 * m:], axis, -1)
-    d = shift(v[2 * m:3 * m], axis, 2)
-    return v[:m] + a + b + d
-
-def scatter_parts(parts, orders, direct=True):
+
+SIDES = (lambda i: i ^ 1, lambda i: 3 - i)
+GROUPS = (
+    ((("x", 0), ("x", 1)), (("y", 0), ("y", 1), (Z, 0), (Z, 1))),
+    ((("y", 0), ("y", 1)), ((Z, 0), (Z, 1), ("x", 0), ("x", 1))),
+)
+
+
+def side_bit(bit, at):
+    axis, side = bit
+    return (at[axis] + 1) // 2 % 2 if side == 0 else at[axis] // 2
+
+
+def halve(v, dim, bit):
+    keep = lax.index_in_dim(v, 0, dim, keepdims=False)
+    send = lax.index_in_dim(v, 1, dim, keepdims=False)
+    if bit == "c":
+        return keep + shift(send, "c", 1)
+    return keep + move(send, bit[0], SIDES[bit[1]])
+
+
+def scatter_table(terms):
     out = []
-    for v, order in zip(parts, orders):
-        half = v.shape[0] // 2
-        v = v[:half] + shift(v[half:], "c", 1)
-        v = ring_scatter(v, order[0])
-        for ax in order[1:]:
-            v = direct_scatter(v, ax) if direct else ring_scatter(v, ax)
-        out.append(v)
-    return out
-
-def direct_gather(v, axis):
-    return jnp.concatenate([v, shift(v, axis, -1), shift(v, axis, 2), shift(v, axis, 1)], 0)
-
-def ring_gather4(v, axis):
-    own, before, after, fa, fb = ring_gather(v, axis)
-    return jnp.concatenate([own, after, fa, fb, before], 0)
-
-def gather_parts(parts, orders):
-    out = []
-    for v, order in zip(parts, orders):
-        for ax in order[:0:-1]:
-            v = direct_gather(v, ax)
-        v = ring_gather4(v, order[0])
-        out.append(jnp.concatenate([v, shift(v, "c", 1)], 0))
-    return out
+    for v, (first, rest) in zip(terms.reshape(2, *[2] * 8, -1, 128), GROUPS):
+        v = halve(v, 0, "c")
+        a = halve(halve(v[0], 0, first[0]), 0, first[1])
+        b = halve(halve(v[1], 0, first[1]), 0, first[0])
+        w = jnp.stack([a, b])
+        for bit in rest:
+            w = halve(w, 1, bit)
+        out.append(w)
+    return jnp.stack(out).reshape(-1, 128)
 
 
 def coordinates():
@@ -370,40 +392,24 @@
     return jnp.where(half != me["c"], 2048, 0) + jnp.where(part == 0, first, second)
 
 
-PARTS = (("x", "y", Z), ("y", Z, "x"), (Z, "x", "y"))
-PART_ROWS = (16, 8, 8)
-
-
 def scatter_place(row, me):
     owner, local = row // 512, row % 512
     seq, within = local // 32, local % 32
     at = {"x": owner % 4, "y": seq // 4, Z: seq // 2 % 2 * 2 + owner // 4, "c": seq % 2}
-    turn = {k: (v - me[k]) % SIZES[k] for k, v in at.items()}
-    result, base, low = jnp.zeros_like(row), 0, 0
-    for order, n in zip(PARTS, PART_ROWS):
-        block = turn["c"]
-        for axis in order:
-            block = block * 4 + turn[axis]
-        place = base + block * n + within - low
-        result = jnp.where((within >= low) & (within < low + n), place, result)
-        base, low = base + 128 * n, low + n
-    return result
-
-
-def turned(order, me, back):
-    ids = jnp.arange(128, dtype=jnp.int32)
-    digits = [("c", ids // 64, 2), (order[0], ids // 16 % 4, 4), (order[1], ids // 4 % 4, 4), (order[2], ids % 4, 4)]
-    out = jnp.zeros_like(ids)
-    for axis, digit, n in digits:
-        out = out * n + ((digit - me[axis]) if back else (digit + me[axis])) % n
-    return out
-
-
-def sum_everywhere(arrays, me):
-    orders = PARTS[:2]
-    sent = [v.reshape(128, 8, 512)[turned(o, me, False)].reshape(1024, 512) for v, o in zip(arrays, orders)]
-    got = gather_parts(scatter_parts(sent, orders), orders)
-    return [v.reshape(128, 8, 512)[turned(o, me, True)].reshape(1024, 512) for v, o in zip(got, orders)]
+    group, sub, inner = within // 16, within // 8 % 2, within % 8
+
+    def chain(bits):
+        out = 0
+        for bit in bits:
+            out = out * 2 + (side_bit(bit, at) ^ side_bit(bit, me))
+        return out
+
+    spots = []
+    for first, rest in GROUPS:
+        lead = jnp.where(sub == 0, chain(first), chain(first[::-1]))
+        spots.append(lead * 16 + chain(rest))
+    spot = jnp.where(group == 0, *spots)
+    return (((group * 2 + (at["c"] ^ me["c"])) * 2 + sub) * 64 + spot) * 8 + inner
 
 
 DP = ("zl", "x")
@@ -449,17 +455,17 @@
     grad_out_w = product(context_t, cotangent)
     grad_query_w = product(inputs.T, grad_queries)
     query_terms = product(grad_queries, w_query.T)
-    terms, grad_both_w = back(
-        scatter_place(rows, me), seq.reshape(1), grad_keys, grad_values, history, w_hi.T, w_lo.T, query_terms, 4096
+    grad_both_w = both_weights(grad_keys, grad_values, history)
+    local_w = (grad_query_w, grad_both_w, grad_out_w)
+    grad_keys, grad_values, local_w = lax.optimization_barrier((grad_keys, grad_values, local_w))
+    sums = lax.psum(local_w, DP + SEQ)
+    terms = back(
+        scatter_place(rows, me), seq.reshape(1), grad_keys, grad_values, w_hi.T, w_lo.T, query_terms, 4096
     )
-    sums = sum_everywhere([grad_both_w, jnp.concatenate([grad_query_w, grad_out_w], axis=0)], me)
-    grad_key_w, grad_value_w = sums[0][:512].T, sums[0][512:].T
-    grad_query_w, grad_out_w = sums[1][:512], sums[1][512:]
-    cuts, at = [], 0
-    for n in PART_ROWS:
-        cuts.append(terms[at * 512:(at + n) * 512])
-        at += n
-    grad_table = jnp.concatenate(scatter_parts(cuts, PARTS), axis=0).reshape(32, 512)
+    grad_table = scatter_table(terms).reshape(32, 512)
+    sums, grad_table = lax.optimization_barrier((sums, grad_table))
+    grad_query_w, grad_both_w, grad_out_w = sums
+    grad_key_w, grad_value_w = grad_both_w[:, :512], grad_both_w[:, 512:]
     return (attended[None], grad_query_w, grad_key_w, grad_value_w, grad_out_w, grad_table)
 
 

time: 497 us -> 476 us (0.958); the launches traced: 489 us -> 476 us
  waiting for transfers between devices: 58.3 us -> 154 us
  starting transfers between devices: 131 us -> 45.5 us
  local copies, waits for them, and re-layouts: 68.6 us -> 41.5 us
  between operations: 1.93 us -> 14.6 us
  other arithmetic: 27 us -> 15.8 us
    psum x0 -> x1, waiting for transfers between devices: none -> 104 us  [on_device(): sums = lax.psum(local_w, DP + SEQ)]
    ppermute x91 -> x32, starting transfers between devices: 122 us -> 35 us  [move(): lax.ppermute(v, axis, [(place(axis, i), place(axis, to(i))) for i in rang...]
    pallas_call x0 -> x1, Pallas kernels: none -> 18.2 us  [both_weights(): pl.pallas_call(kernel, grid=(rows // span,), in_specs=[pl.BlockSpec((span...]
    pallas_call x1, Pallas kernels: 57.2 us -> 40.4 us  [back(): pl.pallas_call(kernel, grid=(rows // span,), in_specs=[pl.BlockSpec(memor...]
    unnamed x91 -> x49, local copies, waits for them, and re-layouts: 27.6 us -> 16.6 us
    gather x4 -> x0, local copies, waits for them, and re-layouts: 10.9 us -> none  [the longest x2 6.08 us: sum_everywhere(): v.reshape(128, 8, 512)[turned(o, me, False)].reshape(1024, 512)]
    ppermute x91 -> x32, waiting for transfers between devices: 55.1 us -> 49 us  [move(): lax.ppermute(v, axis, [(place(axis, i), place(axis, to(i))) for i in rang...]
    slice x25 -> x2, local copies, waits for them, and re-layouts: 10.8 us -> 9.15 us  [the longest x1 6.04 us: halve(): send = lax.index_in_dim(v, 1, dim, keepdims=False)]
  transfers between devices with their start and end apart: 93 -> 35, of which waited for: 32 -> 17; matrix products, arithmetic and copies ran while one was open for 16% -> 8% of each run, Pallas kernels for 0% -> 0%
where the time goes in v3:
time: 476 us
  Pallas kernels  189 us (40%)
  waiting for transfers between devices  154 us (32%)
  starting transfers between devices  45.5 us (10%)
  local copies, waits for them, and re-layouts  41.5 us (9%)
  other arithmetic  15.8 us (3%)
  matrix products  14.6 us (3%)
  between operations  14.6 us (3%)
    psum x1, waiting for transfers between devices, on_device(): sums = lax.psum(local_w, DP + SEQ)  104 us
    pallas_call x1, Pallas kernels, call(): pl.pallas_call(kernel, grid=(pairs,), in_specs=[pl.BlockSpec(bias.shape,...  93.8 us
    ppermute x32, waiting for transfers between devices, move(): lax.ppermute(v, axis, [(place(axis, i), place(axis, to(i))) for i in rang...  49 us
    pallas_call x1, Pallas kernels, back(): pl.pallas_call(kernel, grid=(rows // span,), in_specs=[pl.BlockSpec(memor...  40.4 us
    pallas_call x1, Pallas kernels, front(): pl.pallas_call(kernel, grid=(rows // span,), in_specs=[pl.BlockSpec(memor...  37 us
    ppermute x32, starting transfers between devices, move(): lax.ppermute(v, axis, [(place(axis, i), place(axis, to(i))) for i in rang...  35 us
    pallas_call x1, Pallas kernels, both_weights(): pl.pallas_call(kernel, grid=(rows // span,), in_specs=[pl.BlockSpec((span...  18.2 us
    unnamed x49, local copies, waits for them, and re-layouts  16.6 us
  transfers between devices with their start and end apart: 35, of which 17 were waited for; matrix products, arithmetic and copies ran while one was open for 8% of the time, Pallas kernels for 0%

profile of v3, /device:TPU:1, one launch (start us, length us, event | category | flops | bytes accessed | tf_op | source)
XLA Modules:
  0.0 475.5 jit_solution(3627804053539283448)
XLA Ops:
  7.2 1.4 reshape.143
  9.5 3.3 collective-permute-start.1
  12.8 5.3 %all-to-all-start = ((s32[8,1,128]{2,1,0:T(1,128)}), s32[8,1,128]{2,1,0:T(1,128)S(1)}, u32[]{:S(2)}, u32[]{:S(2)}) async-start(s32[8,1,128]{2,1,0:T(1,128)} %bitcast.2), calls=%async_computation | async-start | bytes 8192 | tf_op jit(solution)/shard_map/all_to_all | solution.py:433
  18.9 3.6 collective-permute-start.7
  22.5 1.4 fusion.7.dot_
  25.9 2.6 copy.41
  28.5 2.3 gather_fusion
  31.8 2.5 collective-permute-start.9
  34.2 1.6 constant_dynamic-update-slice_fusion.12
  36.5 2.7 collective-permute-start.3
  40.9 5.3 %collective-permute-done.3 = f32[256,128]{1,0:T(8,128)S(1)} collective-permute-done((f32[256,128]{1,0:T(8,128)S(1)}, f32[256,128]{1,0:T(8,128)S(1)}, u32[]{:S(2)}, u32[]{:S(2)}) %collective-permute-start.3) | collective-permute-done | bytes 131104 | tf_op jit(solution)/shard_map/ppermute | solution.py:310
  46.2 3.1 collective-permute-done.2
  49.4 2.5 collective-permute-start.5
  57.3 2.7 collective-permute-done.10
  61.5 5.0 %collective-permute-start.13 = (f32[4096,128]{1,0:T(8,128)}, f32[4096,128]{1,0:T(8,128)}, u32[]{:S(2)}, u32[]{:S(2)}) collective-permute-start(f32[4096,128]{1,0:T(8,128)} %constant_dynamic-update-slice_fusion.7.refs_2_), channel_id=1, source_target_pairs={{0,1},{1,0},{2,3},{3,2},{4,5},{5,4},{6,7},{7,6},{8,9},{9,8},{10,11... | collective-permute-start | bytes 6291464 | tf_op jit(solution)/shard_map/ppermute | solution.py:310
  67.9 5.0 %all-to-all-start.1 = ((s32[16,4,128]{2,1,0:T(4,128)}), s32[16,4,128]{2,1,0:T(4,128)S(1)}, u32[]{:S(2)}, u32[]{:S(2)}) async-start(s32[16,4,128]{2,1,0:T(4,128)} %broadcast_in_dim.34), calls=%async_computation.1 | async-start | bytes 65536 | tf_op jit(solution)/shard_map/all_to_all | solution.py:436
  73.2 1.9 fusion
  78.9 1.4 all-to-all-done.1
  80.3 2.1 fusion.45
  83.5 37.0 %shard_map.136 = (f32[4096,512]{1,0:T(8,128)}, f32[4096,1024]{1,0:T(8,128)}) custom-call(s32[2,4096]{1,0:T(2,128)} %fusion.40.refs_0_, f32[4096,128]{1,0:T(8,128)} %constant_dynamic-update-slice_fusion.refs_1_, f32[4096,128]{1,0:T(8,128)} %constant_dynamic-update-slice_fusion.7.refs_2_, f32[4096,128]{1,0:T(8,128)} %collective-permute-done.12.refs_3_, ...), custom_call_target="tpu_custom_call" | custom-call | flops 40000000000 | bytes 33554432 | tf_op jit(solution)/shard_map/pallas_call | solution.py:205
  120.5 2.9 broadcast_multiply_fusion
  124.4 1.4 copy.46
  127.0 2.1 copy.44
  132.4 93.8 %shard_map.137 = (f32[512,256]{1,0:T(8,128)}, f32[512,256]{1,0:T(8,128)}, f32[4096,512]{1,0:T(8,128)}, f32[4096,512]{1,0:T(8,128)}) custom-call(f32[32,256]{1,0:T(8,128)} %bitcast.194, bf16[8,256,256]{2,1,0:T(8,128)(2,1)} %pad_maximum_fusion.1.qt4, bf16[8,256,128]{2,1,0:T(8,128)(2,1)} %pad_maximum_fusion.5.qs2, f32[8,64,256]{2,1,0:T(8,128)} %fusion.7.dot_, ...), custom_call_target="tpu_custom_call" | custom-call | flops 89999998976 | bytes 33554432 | tf_op jit(solution)/shard_map/pallas_call | solution.py:118
  226.2 3.0 fusion.11.qx_ref
  229.2 3.1 fusion.13
  232.3 1.6 fusion.9
  233.8 18.2 %shard_map.138 = f32[512,1024]{1,0:T(8,128)} custom-call(f32[4096,512]{1,0:T(8,128)} %get-tuple-element.30.dk_ref, f32[4096,512]{1,0:T(8,128)} %get-tuple-element.31.dv_ref, f32[4096,512]{1,0:T(8,128)} %get-tuple-element.21.x_ref), custom_call_target="tpu_custom_call" | custom-call | flops 20000000000 | bytes 27262976 | tf_op jit(solution)/shard_map/pallas_call | solution.py:289
  252.1 40.4 %shard_map.139 = f32[16384,128]{1,0:T(8,128)} custom-call(s32[2,4096]{1,0:T(2,128)} %get-tuple-element.39.idx, s32[1]{0:T(128)} %bitcast.17.own_ref, f32[4096,512]{1,0:T(8,128)} %get-tuple-element.30.dk_ref, f32[4096,512]{1,0:T(8,128)} %get-tuple-element.31.dv_ref, bf16[1024,512]{1,0:T(8,128)(2,1)} %bitcast.187, bf16[1024,512]{1,0:T(8,128)(2,1)} %bitcast.186, ...), custom_call_target="tpu_custom_call" | custom-call | flops 40000000000 | bytes 25165824 | tf_op jit(solution)/shard_map/pallas_call | solution.py:261
  292.5 6.0 %fusion.71 = (f32[4096,128]{1,0:T(8,128)}, f32[4096,128]{1,0:T(8,128)S(1)}, f32[4096,128]{1,0:T(8,128)S(1)}, f32[4096,128]{1,0:T(8,128)}) fusion(f32[16384,128]{1,0:T(8,128)} %shard_map.139), kind=kLoop, calls=%fused_computation.246 | loop fusion | bytes 16777216 | tf_op jit(solution)/shard_map/slice | solution.py:360
  299.0 5.5 %collective-permute-done.23 = f32[2,2,2,2,2,2,2,32,128]{8,7,6,5,4,3,2,1,0:T(8,128)S(1)} collective-permute-done((f32[2,2,2,2,2,2,2,32,128]{8,7,6,5,4,3,2,1,0:T(8,128)S(1)}, f32[2,2,2,2,2,2,2,32,128]{8,7,6,5,4,3,2,1,0:T(8,128)S(1)}, u32[]{:S(2)}, u32[]{:S(2)}) %collective-permute-start.23) | collective-permute-done | bytes 2097184 | tf_op jit(solution)/shard_map/ppermute | solution.py:310
  307.4 2.6 convolution_bitcast_fusion
  310.0 2.1 add.355
  312.9 7.6 %collective-permute-done.24 = f32[2,2,2,2,2,32,128]{6,5,4,3,2,1,0:T(8,128)} collective-permute-done((f32[2,2,2,2,2,32,128]{6,5,4,3,2,1,0:T(8,128)}, f32[2,2,2,2,2,32,128]{6,5,4,3,2,1,0:T(8,128)}, u32[]{:S(2)}, u32[]{:S(2)}) %collective-permute-start.24) | collective-permute-done | bytes 524320 | tf_op jit(solution)/shard_map/ppermute | solution.py:310
  320.5 1.6 collective-permute-done.26
  322.1 1.4 fusion.4
  324.7 3.7 collective-permute-done.15
  328.3 2.0 collective-permute-done.17
  333.4 5.7 %collective-permute-done.18 = f32[2,2,2,2,32,128]{5,4,3,2,1,0:T(8,128)S(1)} collective-permute-done((f32[2,2,2,2,32,128]{5,4,3,2,1,0:T(8,128)S(1)}, f32[2,2,2,2,32,128]{5,4,3,2,1,0:T(8,128)S(1)}, u32[]{:S(2)}, u32[]{:S(2)}) %collective-permute-start.18) | collective-permute-done | bytes 262176 | tf_op jit(solution)/shard_map/ppermute | solution.py:310
  340.1 2.8 collective-permute-start.29
  342.9 2.3 collective-permute-done.19
  345.3 1.4 collective-permute-start.20
  346.9 3.5 collective-permute-done.20
  352.0 2.1 collective-permute-done.21
  354.1 2.5 collective-permute-start.22
  356.6 2.0 collective-permute-done.22
  359.2 103.7 %all-reduce.3.cloned.1.call-done = (f32[512,512]{1,0:T(8,128)}, f32[512,1024]{1,0:T(8,128)}, f32[512,512]{1,0:T(8,128)}) async-done(((f32[512,512]{1,0:T(8,128)}, f32[512,1024]{1,0:T(8,128)}, f32[512,512]{1,0:T(8,128)}), (f32[512,512]{1,0:T(8,128)}, f32[512,1024]{1,0:T(8,128)}, f32[512,512]{1,0:T(8,128)})) %all-reduce.3.cloned.1.call-update) | async-done | bytes 4194320 | tf_op jit(solution)/shard_map/psum | solution.py:461
  463.0 3.1 fusion.72
  (149 shorter events, 40.1 us)
Async XLA Ops:
  7.2 15.3 %copy-start = (f32[512,512]{1,0:T(8,128)S(1)}, f32[512,512]{1,0:T(8,128)}, u32[]{:S(2)}) copy-start(f32[512,512]{1,0:T(8,128)} %param.16) | copy-start | bytes 3145732
  7.2 15.3 %copy-start.15 = (s32[1,2,256]{2,1,0:T(2,128)S(1)}, s32[1,2,256]{2,1,0:T(2,128)}, u32[]{:S(2)}) copy-start(s32[1,2,256]{2,1,0:T(2,128)} %param.11) | copy-start | bytes 6148
  7.2 15.3 %copy-start.8 = (f32[1,256,512]{2,1,0:T(8,128)S(1)}, f32[1,256,512]{2,1,0:T(8,128)}, u32[]{:S(2)}) copy-start(f32[1,256,512]{2,1,0:T(8,128)} %param.17) | copy-start | bytes 1572868
  9.5 26.9 %collective-permute-start.1 = (f32[512,128]{1,0:T(8,128)S(1)}, f32[512,128]{1,0:T(8,128)S(1)}, u32[]{:S(2)}, u32[]{:S(2)}) collective-permute-start(f32[512,128]{1,0:T(8,128)S(1)} %get-tuple-element.67), channel_id=1, source_target_pairs={{0,48},{16,0},{32,16},{48,32},{1,49},{17,1},{33,17},{49,33},{2,50}... | collective-permute-start | bytes 786440 | tf_op jit(solution)/shard_map/ppermute | solution.py:310
  12.8 26.4 %collective-permute-start = (f32[512,128]{1,0:T(8,128)S(1)}, f32[512,128]{1,0:T(8,128)S(1)}, u32[]{:S(2)}, u32[]{:S(2)}) collective-permute-start(f32[512,128]{1,0:T(8,128)S(1)} %get-tuple-element.67), channel_id=1, source_target_pairs={{0,16},{16,32},{32,48},{48,0},{1,17},{17,33},{33,49},{49,1},{2,18}... | collective-permute-start | bytes 786440 | tf_op jit(solution)/shard_map/ppermute | solution.py:310
  12.8 15.7 %all-to-all-start = ((s32[8,1,128]{2,1,0:T(1,128)}), s32[8,1,128]{2,1,0:T(1,128)S(1)}, u32[]{:S(2)}, u32[]{:S(2)}) async-start(s32[8,1,128]{2,1,0:T(1,128)} %bitcast.2), calls=%async_computation | async-start | bytes 8192 | tf_op jit(solution)/shard_map/all_to_all | solution.py:433
  18.9 5.8 %copy-start.11 = (f32[512,512]{1,0:T(8,128)S(1)}, f32[512,512]{1,0:T(8,128)}, u32[]{:S(2)}) copy-start(f32[512,512]{1,0:T(8,128)} %param.14) | copy-start | bytes 3145732
  18.9 11.9 %collective-permute-start.7 = (f32[256,128]{1,0:T(8,128)}, f32[256,128]{1,0:T(8,128)S(1)}, u32[]{:S(2)}, u32[]{:S(2)}) collective-permute-start(f32[256,128]{1,0:T(8,128)} %get-tuple-element.64), channel_id=1, source_target_pairs={{0,66},{64,0},{2,64},{66,2},{1,67},{65,1},{3,65},{67,3},{4,70},{68... | collective-permute-start | bytes 393224 | tf_op jit(solution)/shard_map/ppermute | solution.py:310
  22.4 8.4 %collective-permute-start.6 = (f32[256,128]{1,0:T(8,128)}, f32[256,128]{1,0:T(8,128)}, u32[]{:S(2)}, u32[]{:S(2)}) collective-permute-start(f32[256,128]{1,0:T(8,128)} %get-tuple-element.65), channel_id=1, source_target_pairs={{0,64},{64,2},{2,66},{66,0},{1,65},{65,3},{3,67},{67,1},{4,68},{68... | collective-permute-start | bytes 393224 | tf_op jit(solution)/shard_map/ppermute | solution.py:310
  25.9 4.9 %copy-start.14 = (f32[512,128]{1,0:T(8,128)S(1)}, f32[512,128]{1,0:T(8,128)}, u32[]{:S(2)}) copy-start(f32[512,128]{1,0:T(8,128)} %get-tuple-element.43) | copy-start | bytes 786436
  31.8 21.4 %collective-permute-start.9 = (f32[1024,128]{1,0:T(8,128)S(1)}, f32[1024,128]{1,0:T(8,128)S(1)}, u32[]{:S(2)}, u32[]{:S(2)}) collective-permute-start(f32[1024,128]{1,0:T(8,128)S(1)} %pad_maximum_fusion.4), channel_id=1, source_target_pairs={{0,48},{16,0},{32,16},{48,32},{1,49},{17,1},{33,17},{49,33},{2,50}... | collective-permute-start | bytes 1572872 | tf_op jit(solution)/shard_map/ppermute | solution.py:310
  34.2 19.3 %collective-permute-start.8 = (f32[1024,128]{1,0:T(8,128)S(1)}, f32[1024,128]{1,0:T(8,128)S(1)}, u32[]{:S(2)}, u32[]{:S(2)}) collective-permute-start(f32[1024,128]{1,0:T(8,128)S(1)} %pad_maximum_fusion.4), channel_id=1, source_target_pairs={{0,16},{16,32},{32,48},{48,0},{1,17},{17,33},{33,49},{49,1},{2,18}... | collective-permute-start | bytes 1572872 | tf_op jit(solution)/shard_map/ppermute | solution.py:310
  36.5 9.7 %collective-permute-start.3 = (f32[256,128]{1,0:T(8,128)S(1)}, f32[256,128]{1,0:T(8,128)S(1)}, u32[]{:S(2)}, u32[]{:S(2)}) collective-permute-start(f32[256,128]{1,0:T(8,128)S(1)} %slice.219), channel_id=1, source_target_pairs={{0,48},{16,0},{32,16},{48,32},{1,49},{17,1},{33,17},{49,33},{2,50}... | collective-permute-start | bytes 393224 | tf_op jit(solution)/shard_map/ppermute | solution.py:310
  39.2 10.1 %collective-permute-start.2 = (f32[256,128]{1,0:T(8,128)S(1)}, f32[256,128]{1,0:T(8,128)S(1)}, u32[]{:S(2)}, u32[]{:S(2)}) collective-permute-start(f32[256,128]{1,0:T(8,128)S(1)} %slice.218), channel_id=1, source_target_pairs={{0,16},{16,32},{32,48},{48,0},{1,17},{17,33},{33,49},{49,1},{2,18}... | collective-permute-start | bytes 393224 | tf_op jit(solution)/shard_map/ppermute | solution.py:310
  39.3 17.1 %collective-permute-start.4 = (f32[1024,128]{1,0:T(8,128)S(1)}, f32[1024,128]{1,0:T(8,128)S(1)}, u32[]{:S(2)}, u32[]{:S(2)}) collective-permute-start(f32[1024,128]{1,0:T(8,128)S(1)} %pad_maximum_fusion.2), channel_id=1, source_target_pairs={{0,64},{64,2},{2,66},{66,0},{1,65},{65,3},{3,67},{67,1},{4,68},{68... | collective-permute-start | bytes 1572872 | tf_op jit(solution)/shard_map/ppermute | solution.py:310
  49.4 17.1 %collective-permute-start.5 = (f32[1024,128]{1,0:T(8,128)S(1)}, f32[1024,128]{1,0:T(8,128)S(1)}, u32[]{:S(2)}, u32[]{:S(2)}) collective-permute-start(f32[1024,128]{1,0:T(8,128)S(1)} %pad_maximum_fusion.3), channel_id=1, source_target_pairs={{0,66},{64,0},{2,64},{66,2},{1,67},{65,1},{3,65},{67,3},{4,70},{68... | collective-permute-start | bytes 1572872 | tf_op jit(solution)/shard_map/ppermute | solution.py:310
  53.2 7.6 %collective-permute-start.11 = (f32[512,128]{1,0:T(8,128)S(1)}, f32[512,128]{1,0:T(8,128)S(1)}, u32[]{:S(2)}, u32[]{:S(2)}) collective-permute-start(f32[512,128]{1,0:T(8,128)S(1)} %slice.221), channel_id=1, source_target_pairs={{0,48},{16,0},{32,16},{48,32},{1,49},{17,1},{33,17},{49,33},{2,50}... | collective-permute-start | bytes 786440 | tf_op jit(solution)/shard_map/ppermute | solution.py:310
  53.5 6.5 %collective-permute-start.10 = (f32[512,128]{1,0:T(8,128)S(1)}, f32[512,128]{1,0:T(8,128)S(1)}, u32[]{:S(2)}, u32[]{:S(2)}) collective-permute-start(f32[512,128]{1,0:T(8,128)S(1)} %slice.220), channel_id=1, source_target_pairs={{0,16},{16,32},{32,48},{48,0},{1,17},{17,33},{33,49},{49,1},{2,18}... | collective-permute-start | bytes 786440 | tf_op jit(solution)/shard_map/ppermute | solution.py:310
  61.5 22.0 %collective-permute-start.13 = (f32[4096,128]{1,0:T(8,128)}, f32[4096,128]{1,0:T(8,128)}, u32[]{:S(2)}, u32[]{:S(2)}) collective-permute-start(f32[4096,128]{1,0:T(8,128)} %constant_dynamic-update-slice_fusion.7.refs_2_), channel_id=1, source_target_pairs={{0,1},{1,0},{2,3},{3,2},{4,5},{5,4},{6,7},{7,6},{8,9},{9,8},{10,11... | collective-permute-start | bytes 6291464 | tf_op jit(solution)/shard_map/ppermute | solution.py:310
  67.3 16.2 %collective-permute-start.12 = (f32[4096,128]{1,0:T(8,128)}, f32[4096,128]{1,0:T(8,128)}, u32[]{:S(2)}, u32[]{:S(2)}) collective-permute-start(f32[4096,128]{1,0:T(8,128)} %constant_dynamic-update-slice_fusion.refs_1_), channel_id=1, source_target_pairs={{0,1},{1,0},{2,3},{3,2},{4,5},{5,4},{6,7},{7,6},{8,9},{9,8},{10,11... | collective-permute-start | bytes 6291464 | tf_op jit(solution)/shard_map/ppermute | solution.py:310
  67.9 12.3 %all-to-all-start.1 = ((s32[16,4,128]{2,1,0:T(4,128)}), s32[16,4,128]{2,1,0:T(4,128)S(1)}, u32[]{:S(2)}, u32[]{:S(2)}) async-start(s32[16,4,128]{2,1,0:T(4,128)} %broadcast_in_dim.34), calls=%async_computation.1 | async-start | bytes 65536 | tf_op jit(solution)/shard_map/all_to_all | solution.py:436
  72.9 390.1 %all-reduce.3.cloned.1.call-start = ((), (), s32[]{:S(2)}) async-start(), calls=%async_computation.2 | async-start | bytes 8388608 | tf_op jit(solution)/shard_map/psum | solution.py:461
  75.0 3.9 copy-start.3
  75.0 3.8 copy-start.4
  83.5 37.0 %copy-start.2 = (f32[512,512]{1,0:T(8,128)S(1)}, f32[512,512]{1,0:T(8,128)}, u32[]{:S(2)}) copy-start(f32[512,512]{1,0:T(8,128)} %param.13) | copy-start | bytes 3145732
  127.0 3.3 copy-start.6
  127.0 3.3 copy-start.7
  226.2 6.1 %copy-start.9 = (f32[1,256,512]{2,1,0:T(8,128)S(1)}, f32[1,256,512]{2,1,0:T(8,128)}, u32[]{:S(2)}) copy-start(f32[1,256,512]{2,1,0:T(8,128)} %param.17) | copy-start | bytes 1572868
  226.2 6.1 %copy-start.10 = (f32[512,256]{1,0:T(8,128)S(1)}, f32[512,256]{1,0:T(8,128)}, u32[]{:S(2)}) copy-start(f32[512,256]{1,0:T(8,128)} %get-tuple-element.23) | copy-start | bytes 1572868
  298.5 6.0 %collective-permute-start.23 = (f32[2,2,2,2,2,2,2,32,128]{8,7,6,5,4,3,2,1,0:T(8,128)S(1)}, f32[2,2,2,2,2,2,2,32,128]{8,7,6,5,4,3,2,1,0:T(8,128)S(1)}, u32[]{:S(2)}, u32[]{:S(2)}) collective-permute-start(f32[2,2,2,2,2,2,2,32,128]{8,7,6,5,4,3,2,1,0:T(8,128)S(1)} %bitcast.190), channel_id=1, source_target_pairs={{0,1},{1,0},{2,3},{3,2},{4,5},{5,4},{6,7},{7,6},{8,9},{9,8},{10,11... | collective-permute-start | bytes 6291464 | tf_op jit(solution)/shard_map/ppermute | solution.py:310
  298.9 11.1 %collective-permute-start.14 = (f32[2,2,2,2,2,2,2,32,128]{8,7,6,5,4,3,2,1,0:T(8,128)}, f32[2,2,2,2,2,2,2,32,128]{8,7,6,5,4,3,2,1,0:T(8,128)}, u32[]{:S(2)}, u32[]{:S(2)}) collective-permute-start(f32[2,2,2,2,2,2,2,32,128]{8,7,6,5,4,3,2,1,0:T(8,128)} %bitcast.21), channel_id=1, source_target_pairs={{0,1},{1,0},{2,3},{3,2},{4,5},{5,4},{6,7},{7,6},{8,9},{9,8},{10,11... | collective-permute-start | bytes 6291464 | tf_op jit(solution)/shard_map/ppermute | solution.py:310
  306.1 14.5 %collective-permute-start.24 = (f32[2,2,2,2,2,32,128]{6,5,4,3,2,1,0:T(8,128)}, f32[2,2,2,2,2,32,128]{6,5,4,3,2,1,0:T(8,128)}, u32[]{:S(2)}, u32[]{:S(2)}) collective-permute-start(f32[2,2,2,2,2,32,128]{6,5,4,3,2,1,0:T(8,128)} %get-tuple-element.58), channel_id=1, source_target_pairs={{0,4},{4,0},{8,12},{12,8},{1,5},{5,1},{9,13},{13,9},{2,6},{6,2},{1... | collective-permute-start | bytes 1572872 | tf_op jit(solution)/shard_map/ppermute | solution.py:310
  306.3 15.8 %collective-permute-start.26 = (f32[2,2,2,2,2,32,128]{6,5,4,3,2,1,0:T(8,128)}, f32[2,2,2,2,2,32,128]{6,5,4,3,2,1,0:T(8,128)}, u32[]{:S(2)}, u32[]{:S(2)}) collective-permute-start(f32[2,2,2,2,2,32,128]{6,5,4,3,2,1,0:T(8,128)} %get-tuple-element.59), channel_id=1, source_target_pairs={{0,12},{4,8},{8,4},{12,0},{1,13},{5,9},{9,5},{13,1},{2,14},{6,10},... | collective-permute-start | bytes 1572872 | tf_op jit(solution)/shard_map/ppermute | solution.py:310
  312.2 16.1 %collective-permute-start.15 = (f32[2,2,2,2,2,32,128]{6,5,4,3,2,1,0:T(8,128)S(1)}, f32[2,2,2,2,2,32,128]{6,5,4,3,2,1,0:T(8,128)S(1)}, u32[]{:S(2)}, u32[]{:S(2)}) collective-permute-start(f32[2,2,2,2,2,32,128]{6,5,4,3,2,1,0:T(8,128)S(1)} %get-tuple-element.54), channel_id=1, source_target_pairs={{0,16},{16,0},{32,48},{48,32},{1,17},{17,1},{33,49},{49,33},{2,18}... | collective-permute-start | bytes 1572872 | tf_op jit(solution)/shard_map/ppermute | solution.py:310
  312.6 17.7 %collective-permute-start.17 = (f32[2,2,2,2,2,32,128]{6,5,4,3,2,1,0:T(8,128)S(1)}, f32[2,2,2,2,2,32,128]{6,5,4,3,2,1,0:T(8,128)S(1)}, u32[]{:S(2)}, u32[]{:S(2)}) collective-permute-start(f32[2,2,2,2,2,32,128]{6,5,4,3,2,1,0:T(8,128)S(1)} %get-tuple-element.55), channel_id=1, source_target_pairs={{0,48},{16,32},{32,16},{48,0},{1,49},{17,33},{33,17},{49,1},{2,50}... | collective-permute-start | bytes 1572872 | tf_op jit(solution)/shard_map/ppermute | solution.py:310
  323.6 7.6 %collective-permute-start.27 = (f32[2,2,2,2,32,128]{5,4,3,2,1,0:T(8,128)S(1)}, f32[2,2,2,2,32,128]{5,4,3,2,1,0:T(8,128)S(1)}, u32[]{:S(2)}, u32[]{:S(2)}) collective-permute-start(f32[2,2,2,2,32,128]{5,4,3,2,1,0:T(8,128)S(1)} %slice_bitcast_fusion.8), channel_id=1, source_target_pairs={{0,4},{4,0},{8,12},{12,8},{1,5},{5,1},{9,13},{13,9},{2,6},{6,2},{1... | collective-permute-start | bytes 786440 | tf_op jit(solution)/shard_map/ppermute | solution.py:310
  323.7 8.6 %collective-permute-start.25 = (f32[2,2,2,2,32,128]{5,4,3,2,1,0:T(8,128)S(1)}, f32[2,2,2,2,32,128]{5,4,3,2,1,0:T(8,128)S(1)}, u32[]{:S(2)}, u32[]{:S(2)}) collective-permute-start(f32[2,2,2,2,32,128]{5,4,3,2,1,0:T(8,128)S(1)} %slice_bitcast_fusion.10), channel_id=1, source_target_pairs={{0,12},{4,8},{8,4},{12,0},{1,13},{5,9},{9,5},{13,1},{2,14},{6,10},... | collective-permute-start | bytes 786440 | tf_op jit(solution)/shard_map/ppermute | solution.py:310
  330.6 8.5 %collective-permute-start.18 = (f32[2,2,2,2,32,128]{5,4,3,2,1,0:T(8,128)S(1)}, f32[2,2,2,2,32,128]{5,4,3,2,1,0:T(8,128)S(1)}, u32[]{:S(2)}, u32[]{:S(2)}) collective-permute-start(f32[2,2,2,2,32,128]{5,4,3,2,1,0:T(8,128)S(1)} %slice_bitcast_fusion.12), channel_id=1, source_target_pairs={{0,16},{16,0},{32,48},{48,32},{1,17},{17,1},{33,49},{49,33},{2,18}... | collective-permute-start | bytes 786440 | tf_op jit(solution)/shard_map/ppermute | solution.py:310
  330.7 9.2 %collective-permute-start.16 = (f32[2,2,2,2,32,128]{5,4,3,2,1,0:T(8,128)S(1)}, f32[2,2,2,2,32,128]{5,4,3,2,1,0:T(8,128)S(1)}, u32[]{:S(2)}, u32[]{:S(2)}) collective-permute-start(f32[2,2,2,2,32,128]{5,4,3,2,1,0:T(8,128)S(1)} %slice_bitcast_fusion.14), channel_id=1, source_target_pairs={{0,48},{16,32},{32,16},{48,0},{1,49},{17,33},{33,17},{49,1},{2,50}... | collective-permute-start | bytes 786440 | tf_op jit(solution)/shard_map/ppermute | solution.py:310
  332.4 7.7 %collective-permute-start.28 = (f32[2,2,2,2,32,128]{5,4,3,2,1,0:T(8,128)S(1)}, f32[2,2,2,2,32,128]{5,4,3,2,1,0:T(8,128)S(1)}, u32[]{:S(2)}, u32[]{:S(2)}) collective-permute-start(f32[2,2,2,2,32,128]{5,4,3,2,1,0:T(8,128)S(1)} %fusion.24), channel_id=1, source_target_pairs={{0,64},{64,0},{2,66},{66,2},{1,65},{65,1},{3,67},{67,3},{4,68},{68... | collective-permute-start | bytes 786440 | tf_op jit(solution)/shard_map/ppermute | solution.py:310
  339.9 5.3 %collective-permute-start.19 = (f32[2,2,2,2,32,128]{5,4,0,3,2,1:T(8,128)S(1)}, f32[2,2,2,2,32,128]{5,4,0,3,2,1:T(8,128)S(1)}, u32[]{:S(2)}, u32[]{:S(2)}) collective-permute-start(f32[2,2,2,2,32,128]{5,4,0,3,2,1:T(8,128)S(1)} %fusion.29), channel_id=1, source_target_pairs={{0,4},{4,0},{8,12},{12,8},{1,5},{5,1},{9,13},{13,9},{2,6},{6,2},{1... | collective-permute-start | bytes 786440 | tf_op jit(solution)/shard_map/ppermute | solution.py:310
  340.1 6.6 %collective-permute-start.29 = (f32[2,2,2,32,128]{4,3,2,1,0:T(8,128)S(1)}, f32[2,2,2,32,128]{4,3,2,1,0:T(8,128)S(1)}, u32[]{:S(2)}, u32[]{:S(2)}) collective-permute-start(f32[2,2,2,32,128]{4,3,2,1,0:T(8,128)S(1)} %slice_bitcast_fusion.16), channel_id=1, source_target_pairs={{0,66},{64,2},{2,64},{66,0},{1,67},{65,3},{3,65},{67,1},{4,70},{68... | collective-permute-start | bytes 393224 | tf_op jit(solution)/shard_map/ppermute | solution.py:310
  345.3 5.1 %collective-permute-start.20 = (f32[2,2,2,32,128]{4,3,0,2,1:T(8,128)S(1)}, f32[2,2,2,32,128]{4,3,0,2,1:T(8,128)S(1)}, u32[]{:S(2)}, u32[]{:S(2)}) collective-permute-start(f32[2,2,2,32,128]{4,3,0,2,1:T(8,128)S(1)} %slice_bitcast_fusion.18), channel_id=1, source_target_pairs={{0,12},{4,8},{8,4},{12,0},{1,13},{5,9},{9,5},{13,1},{2,14},{6,10},... | collective-permute-start | bytes 393224 | tf_op jit(solution)/shard_map/ppermute | solution.py:310
  346.8 3.9 collective-permute-start.30
  350.4 3.6 collective-permute-start.21
  350.7 5.9 %collective-permute-start.31 = (f32[2,32,128]{2,1,0:T(8,128)S(1)}, f32[2,32,128]{2,1,0:T(8,128)S(1)}, u32[]{:S(2)}, u32[]{:S(2)}) collective-permute-start(f32[2,32,128]{2,1,0:T(8,128)S(1)} %slice_bitcast_fusion.24), channel_id=1, source_target_pairs={{0,48},{16,32},{32,16},{48,0},{1,49},{17,33},{33,17},{49,1},{2,50}... | collective-permute-start | bytes 98312 | tf_op jit(solution)/shard_map/ppermute | solution.py:310
  354.1 4.5 collective-permute-start.22
  463.0 3.1 copy-start.13
  (3 other events, 7.3 us)
Sparse Core Ops, SparseCore 0:
  307.5 155.4 all-reduce.2

commit v4 on v3

--- a/solution.py
+++ b/solution.py
@@ -8,7 +8,7 @@
 HEADS = 8
 HEAD_DIM = 64
 TILE = 128
-SPAN = 512
+SPAN = 1024
 MIB = 1024 * 1024
 BF = jnp.bfloat16
 F32 = jnp.float32
@@ -30,7 +30,7 @@
     lo = (x - hi.astype(F32)).astype(BF)
     return hi, lo
 
-def make(span):
+def make(span, un):
     def kernel(bias, qt4, qs2, dot_, k_ref, v_ref, ctx_ref, dq_ref, dk_ref, dv_ref, k2, v2, s_ref, ph, plo):
         rows = k_ref.shape[0]
         nb = rows // span
@@ -62,7 +62,7 @@
                     s_ref[pl.ds(pl.multiple_of(i * span + t * 128, 128), 128), :] = st
                     peak = jnp.maximum(peak, jnp.max(st.reshape(16, 8, 256), axis=0))
                 return peak
-            peak = lax.fori_loop(0, nb, score, jnp.full((8, 256), -3e38, F32))
+            peak = lax.fori_loop(0, nb, score, jnp.full((8, 256), -3e38, F32), unroll=un)
             peak = jnp.max(peak, axis=0, keepdims=True)
 
             def weigh(i, carry):
@@ -76,7 +76,7 @@
                 v = v2[at, :]
                 acc = acc + dot_tn(v, hi) + dot_tn(v, lo)
                 return total, acc
-            total, acc = lax.fori_loop(0, nb, weigh, (jnp.zeros((8, 256), F32), jnp.zeros((128, 256), F32)))
+            total, acc = lax.fori_loop(0, nb, weigh, (jnp.zeros((8, 256), F32), jnp.zeros((128, 256), F32)), unroll=un)
             share = 1.0 / jnp.sum(total, axis=0, keepdims=True)
             ctx = (acc[:64] + acc[64:]) * share
             ctx_ref[head * 64:(head + 1) * 64, :] = ctx
@@ -109,7 +109,7 @@
                     dv_ref[at, :] = jnp.where(low, dv_ref[at, :], dv)
                     dk_ref[at, :] = jnp.where(low, dk_ref[at, :], dk)
                 return acc + dot_tn(k, shi) + dot_tn(k, slo)
-            acc = lax.fori_loop(0, nb, back, jnp.zeros((128, 256), F32))
+            acc = lax.fori_loop(0, nb, back, jnp.zeros((128, 256), F32), unroll=un)
             dq_ref[head * 64:(head + 1) * 64, :] = acc[:64] + acc[64:]
 
     def call(bias, qt4, qs2, dot_, kv):
@@ -273,10 +273,11 @@
     )(slots, own, dk, dv, wt_hi, wt_lo, qx)[0]
 
 
-def both_weights(dk, dv, x, span=512):
+def weight_blocks(places, dq_w, do_w, dk, dv, x, span=512):
     rows, width = x.shape
-
-    def kernel(dk_ref, dv_ref, x_ref, w_ref):
+    steps = rows // span
+
+    def kernel(at_ref, q_ref, o_ref, dk_ref, dv_ref, x_ref, out_ref, w_ref):
         @pl.when(pl.program_id(0) == 0)
         def _():
             w_ref[...] = jnp.zeros_like(w_ref)
@@ -286,15 +287,65 @@
             hi, lo = halves(ref[...])
             w_ref[:, j * width:(j + 1) * width] += dot_tn(xhi, hi) + dot_tn(xhi, lo) + dot_tn(xlo, hi)
 
+        @pl.when(pl.program_id(0) == steps - 1)
+        def _():
+            def copy(i, c):
+                cut = pl.ds(pl.multiple_of(i * 16, 16), 16)
+                for j in range(16):
+                    ref, k = ((w_ref, j), (q_ref, j - 8), (o_ref, j - 12))[(j >= 8) + (j >= 12)]
+                    to = pl.ds(pl.multiple_of(at_ref[i * 16 + j] * 16, 16), 16)
+                    out_ref[to, :] = ref[cut, k * 128:(k + 1) * 128]
+                return c
+
+            lax.fori_loop(0, 32, copy, 0)
+
+    whole = pl.BlockSpec((width, width), lambda i: (0, 0))
     return pl.pallas_call(
         kernel,
-        grid=(rows // span,),
-        in_specs=[pl.BlockSpec((span, width), lambda i: (i, 0))] * 3,
-        out_specs=pl.BlockSpec((width, 2 * width), lambda i: (0, 0)),
-        out_shape=jax.ShapeDtypeStruct((width, 2 * width), F32),
+        grid=(steps,),
+        in_specs=[pl.BlockSpec(memory_space=pltpu.SMEM), whole, whole]
+        + [pl.BlockSpec((span, width), lambda i: (i, 0))] * 3,
+        out_specs=pl.BlockSpec((16 * width, 128), lambda i: (0, 0)),
+        out_shape=jax.ShapeDtypeStruct((16 * width, 128), F32),
+        scratch_shapes=[pltpu.VMEM((width, 2 * width), F32)],
         compiler_params=pltpu.CompilerParams(vmem_limit_bytes=56 * MIB),
-        cost_estimate=pl.CostEstimate(flops=20_000_000_000, bytes_accessed=26 * MIB, transcendentals=0),
-    )(dk, dv, x)
+        cost_estimate=pl.CostEstimate(flops=20_000_000_000, bytes_accessed=28 * MIB, transcendentals=0),
+    )(places, dq_w, do_w, dk, dv, x)
+
+
+def weights_of(places, pieces):
+    width = 512
+    n = len(pieces)
+
+    def kernel(at_ref, *refs):
+        parts, outs, all_ref, sem = refs[:n], refs[n:n + 4], refs[n + 4], refs[n + 5]
+        copies, base = [], 0
+        for j, p in enumerate(parts):
+            copies.append(pltpu.make_async_copy(p, all_ref.at[pl.ds(base, p.shape[0])], sem.at[j]))
+            base += p.shape[0]
+        for c in copies:
+            c.start()
+        for c in copies:
+            c.wait()
+
+        def copy(i, c):
+            cut = pl.ds(pl.multiple_of(i * 16, 16), 16)
+            for j in range(16):
+                k = j % 4
+                at = pl.ds(pl.multiple_of(at_ref[i * 16 + j] * 16, 16), 16)
+                outs[j // 4][cut, k * 128:(k + 1) * 128] = all_ref[at, :]
+            return c
+
+        lax.fori_loop(0, 32, copy, 0)
+
+    return pl.pallas_call(
+        kernel,
+        in_specs=[pl.BlockSpec(memory_space=pltpu.SMEM)] + [pl.BlockSpec(memory_space=pl.ANY)] * n,
+        out_specs=[pl.BlockSpec(memory_space=pltpu.VMEM)] * 4,
+        out_shape=[jax.ShapeDtypeStruct((width, width), F32)] * 4,
+        scratch_shapes=[pltpu.VMEM((16 * width, 128), F32), pltpu.SemaphoreType.DMA((n,))],
+        compiler_params=pltpu.CompilerParams(vmem_limit_bytes=56 * MIB),
+    )(places, *pieces)
 
 
 Z = ("zl", "zh")
@@ -323,7 +374,7 @@
     return [v, before, after, far_a, far_b]
 
 
-def table_gather(shard):
+def table_gather(shard, extra):
     c = lax.axis_index("c")
     half = shard.shape[0] // 2
     mine = lax.dynamic_slice_in_dim(shard, c * half, half, 0)
@@ -333,6 +384,7 @@
     zb = shift(a2[q:], Z, -1)
     s1 = ring_gather(a1, "x")
     v2 = jnp.concatenate([a2, za, zb], 0)
+    v2, extra = lax.optimization_barrier((v2, extra))
     s2 = ring_gather(v2, "x")
     z1 = shift(jnp.concatenate(s1[:2], 0), Z, 1)
     z2 = shift(jnp.concatenate(s1[2:], 0), Z, -1)
@@ -340,7 +392,7 @@
     other_first = shift(first, "c", 1)
     second = jnp.concatenate(s2, 0)
     other_second = shift(second, "c", 1)
-    return first, second, other_first, other_second
+    return (first, second, other_first, other_second), extra
 
 
 SIDES = (lambda i: i ^ 1, lambda i: 3 - i)
@@ -355,25 +407,42 @@
     return (at[axis] + 1) // 2 % 2 if side == 0 else at[axis] // 2
 
 
+def across(v, bit):
+    return move(v, bit[0], SIDES[bit[1]])
+
+
 def halve(v, dim, bit):
     keep = lax.index_in_dim(v, 0, dim, keepdims=False)
     send = lax.index_in_dim(v, 1, dim, keepdims=False)
-    if bit == "c":
-        return keep + shift(send, "c", 1)
-    return keep + move(send, bit[0], SIDES[bit[1]])
-
-
-def scatter_table(terms):
-    out = []
-    for v, (first, rest) in zip(terms.reshape(2, *[2] * 8, -1, 128), GROUPS):
-        v = halve(v, 0, "c")
+    return keep + across(send, bit)
+
+
+def sum_over_devices(terms, blocks):
+    bits = [2] * 6
+    terms = terms.reshape(2, 2, 2, *bits, -1, 128)
+    blocks = blocks.reshape(2, 2, 2, *bits, -1, 128)
+    n = terms.shape[-2]
+    mine, pieces = [], []
+    for g, (first, rest) in enumerate(GROUPS):
+        sent = shift(jnp.concatenate([terms[g, 1], blocks[g, 1]], axis=-2), "c", 1)
+        v = jnp.concatenate([terms[g, 0], blocks[g, 0]], axis=-2) + sent
         a = halve(halve(v[0], 0, first[0]), 0, first[1])
         b = halve(halve(v[1], 0, first[1]), 0, first[0])
         w = jnp.stack([a, b])
         for bit in rest:
             w = halve(w, 1, bit)
-        out.append(w)
-    return jnp.stack(out).reshape(-1, 128)
+        mine.append(w[:, :n])
+        w = w[:, n:]
+        for bit in rest[::-1]:
+            w = jnp.stack([w, across(w, bit)], axis=1)
+        a, b = w[0], w[1]
+        for bit in first[::-1]:
+            a = jnp.stack([a, across(a, bit)])
+        for bit in first:
+            b = jnp.stack([b, across(b, bit)])
+        w = jnp.stack([a, b]).reshape(-1, 128)
+        pieces += [w, shift(w, "c", 1)]
+    return jnp.stack(mine).reshape(-1, 128), pieces
 
 
 def coordinates():
@@ -410,6 +479,23 @@
         spots.append(lead * 16 + chain(rest))
     spot = jnp.where(group == 0, *spots)
     return (((group * 2 + (at["c"] ^ me["c"])) * 2 + sub) * 64 + spot) * 8 + inner
+
+
+def block_place(me):
+    ids = jnp.arange(512, dtype=jnp.int32)
+    group, sub = ids // 256, ids // 64 % 2
+
+    def chain(bits):
+        out = 0
+        for bit in bits:
+            out = out * 2 + side_bit(bit, me)
+        return out
+
+    spots = []
+    for first, rest in GROUPS:
+        lead = jnp.where(sub == 0, chain(first), chain(first[::-1]))
+        spots.append(lead * 16 + chain(rest))
+    return ids ^ (jnp.where(group == 0, *spots) + me["c"] * 128)
 
 
 DP = ("zl", "x")
@@ -429,13 +515,13 @@
 ):
     me = coordinates()
     seq = lax.axis_index(SEQ)
-    pieces = table_gather(item_table.reshape(-1, 128))
     lists = lax.all_to_all(serve_lists[0, :, 0, :], DP, split_axis=0, concat_axis=0, tiled=True)
     slots = event_slots[0]
     rows = slots // TILE * 512 + lists.reshape(-1)[slots]
     rows = lax.all_to_all(
         jnp.broadcast_to(rows.reshape(1, 4, 128), (16, 4, 128)), SEQ, split_axis=0, concat_axis=0, tiled=True
     )
+    pieces, rows = table_gather(item_table.reshape(-1, 128), rows)
     rows = rows.reshape(16, 2, 256).transpose(1, 0, 2).reshape(2, 4096)
     w_both = jnp.concatenate([w_key, w_value], axis=1)
     w_hi, w_lo = split_xla(w_both)
@@ -446,7 +532,7 @@
     scale = HEAD_DIM ** (-0.5)
     queries = product(inputs, w_query, EXACT) * scale
     grad_context = product(cotangent, w_out.T)
-    context_t, grad_queries_t, grad_keys, grad_values = make(SPAN)(
+    context_t, grad_queries_t, grad_keys, grad_values = make(SPAN, 2)(
         *operands(queries, grad_context, session_tiles[0]), both
     )
     context = context_t.T
@@ -455,17 +541,14 @@
     grad_out_w = product(context_t, cotangent)
     grad_query_w = product(inputs.T, grad_queries)
     query_terms = product(grad_queries, w_query.T)
-    grad_both_w = both_weights(grad_keys, grad_values, history)
-    local_w = (grad_query_w, grad_both_w, grad_out_w)
-    grad_keys, grad_values, local_w = lax.optimization_barrier((grad_keys, grad_values, local_w))
-    sums = lax.psum(local_w, DP + SEQ)
+    places = block_place(me)
+    blocks = weight_blocks(places, grad_query_w, grad_out_w, grad_keys, grad_values, history)
     terms = back(
         scatter_place(rows, me), seq.reshape(1), grad_keys, grad_values, w_hi.T, w_lo.T, query_terms, 4096
     )
-    grad_table = scatter_table(terms).reshape(32, 512)
-    sums, grad_table = lax.optimization_barrier((sums, grad_table))
-    grad_query_w, grad_both_w, grad_out_w = sums
-    grad_key_w, grad_value_w = grad_both_w[:, :512], grad_both_w[:, 512:]
+    grad_table, pieces = sum_over_devices(terms, blocks)
+    grad_key_w, grad_value_w, grad_query_w, grad_out_w = weights_of(places, pieces)
+    grad_table = grad_table.reshape(32, 512)
     return (attended[None], grad_query_w, grad_key_w, grad_value_w, grad_out_w, grad_table)
 
 

time: 476 us -> 392 us (0.82); the launches traced: 476 us -> 386 us
  waiting for transfers between devices: 154 us -> 82.2 us
  starting transfers between devices: 45.5 us -> 66 us
  Pallas kernels: 189 us -> 169 us
  between operations: 14.6 us -> 2 us
    psum x1 -> x0, waiting for transfers between devices: 104 us -> none  [on_device(): sums = lax.psum(local_w, DP + SEQ)]
    pallas_call x1, Pallas kernels: 93.8 us -> 65.1 us  [call(): pl.pallas_call(kernel, grid=(pairs,), in_specs=[pl.BlockSpec(bias.shape,...]
    ppermute x32 -> x50, waiting for transfers between devices: 49 us -> 76.8 us  [move(): lax.ppermute(v, axis, [(place(axis, i), place(axis, to(i))) for i in rang...]
    ppermute x32 -> x50, starting transfers between devices: 35 us -> 53.2 us  [move(): lax.ppermute(v, axis, [(place(axis, i), place(axis, to(i))) for i in rang...]
    slice x3 -> x1, local copies, waits for them, and re-layouts: 9.86 us -> 0.7 us  [table_gather(): za = shift(a2[:q], Z, 1)]
    pallas_call x1 -> x2, Pallas kernels: 18.2 us -> 26.4 us  [the longest x1 20.8 us: weight_blocks(): pl.pallas_call(kernel, grid=(steps,), in_specs=[pl.BlockSpec(memory_space...]
    squeeze x0 -> x2, local copies, waits for them, and re-layouts: none -> 7.53 us  [sum_over_devices(): v = jnp.concatenate([terms[g, 0], blocks[g, 0]], axis=-2) + sent]
    unnamed x49 -> x46, local copies, waits for them, and re-layouts: 16.6 us -> 13.2 us
  transfers between devices with their start and end apart: 35 -> 52, of which waited for: 17 -> 30; matrix products, arithmetic and copies ran while one was open for 8% -> 10% of each run, Pallas kernels for 0% -> 0%
where the time goes in v4:
time: 392 us; the launch traced here: 386 us
  Pallas kernels  169 us (43%)
  waiting for transfers between devices  82.2 us (21%)
  starting transfers between devices  66 us (17%)
  local copies, waits for them, and re-layouts  36.8 us (9%)
  other arithmetic  16.5 us (4%)
  matrix products  13.4 us (3%)
    ppermute x50, waiting for transfers between devices, move(): lax.ppermute(v, axis, [(place(axis, i), place(axis, to(i))) for i in rang...  76.8 us
    pallas_call x1, Pallas kernels, call(): pl.pallas_call(kernel, grid=(pairs,), in_specs=[pl.BlockSpec(bias.shape,...  65.1 us
    ppermute x50, starting transfers between devices, move(): lax.ppermute(v, axis, [(place(axis, i), place(axis, to(i))) for i in rang...  53.2 us
    pallas_call x1, Pallas kernels, back(): pl.pallas_call(kernel, grid=(rows // span,), in_specs=[pl.BlockSpec(memor...  40.7 us
    pallas_call x1, Pallas kernels, front(): pl.pallas_call(kernel, grid=(rows // span,), in_specs=[pl.BlockSpec(memor...  37 us
    pallas_call x1, Pallas kernels, weight_blocks(): pl.pallas_call(kernel, grid=(steps,), in_specs=[pl.BlockSpec(memory_space...  20.8 us
    dot_general x6, matrix products, product(): return jnp.dot(left, right, precision=precision, preferred_element_type=F32)  13.4 us
    unnamed x46, local copies, waits for them, and re-layouts  13.2 us
  transfers between devices with their start and end apart: 52, of which 30 were waited for; matrix products, arithmetic and copies ran while one was open for 10% of the time, Pallas kernels for 0%

profile of v4, /device:TPU:1, one launch (start us, length us, event | category | flops | bytes accessed | tf_op | source)
XLA Modules:
  0.0 386.1 jit_solution(3383987745210571362)
XLA Ops:
  3.1 3.3 collective-permute-start.3
  6.4 5.3 %all-to-all-start = ((s32[8,1,128]{2,1,0:T(1,128)}), s32[8,1,128]{2,1,0:T(1,128)S(1)}, u32[]{:S(2)}, u32[]{:S(2)}) async-start(s32[8,1,128]{2,1,0:T(1,128)} %bitcast.2), calls=%async_computation | async-start | bytes 8192 | tf_op jit(solution)/shard_map/all_to_all | solution.py:518
  13.9 2.1 collective-permute-start.1
  18.7 1.9 fusion
  20.7 2.3 gather_fusion
  23.6 7.5 %all-to-all-start.1 = ((s32[16,4,128]{2,1,0:T(4,128)}), s32[16,4,128]{2,1,0:T(4,128)S(1)}, u32[]{:S(2)}, u32[]{:S(2)}) async-start(s32[16,4,128]{2,1,0:T(4,128)} %broadcast_in_dim.48), calls=%async_computation.1 | async-start | bytes 65536 | tf_op jit(solution)/shard_map/all_to_all | solution.py:521
  31.1 1.9 pad_maximum_fusion.6
  33.0 5.4 %all-to-all-done.1 = s32[16,4,128]{2,1,0:T(4,128)S(1)} async-done(((s32[16,4,128]{2,1,0:T(4,128)}), s32[16,4,128]{2,1,0:T(4,128)S(1)}, u32[]{:S(2)}, u32[]{:S(2)}) %all-to-all-start.1) | async-done | bytes 32800 | tf_op jit(solution)/shard_map/all_to_all | solution.py:521
  38.4 2.9 collective-permute-start.9
  41.4 1.9 constant_dynamic-update-slice_fusion.11
  43.3 2.7 collective-permute-start.5
  48.7 1.7 constant_dynamic-update-slice_fusion.5
  51.1 4.1 %collective-permute-done.5 = f32[256,128]{1,0:T(8,128)S(1)} collective-permute-done((f32[256,128]{1,0:T(8,128)S(1)}, f32[256,128]{1,0:T(8,128)S(1)}, u32[]{:S(2)}, u32[]{:S(2)}) %collective-permute-start.5) | collective-permute-done | bytes 131104 | tf_op jit(solution)/shard_map/ppermute | solution.py:361
  55.3 3.1 collective-permute-done.4
  64.3 3.5 collective-permute-done.10
  69.3 2.7 collective-permute-start.13
  79.3 2.1 fusion.49
  82.5 37.0 %shard_map.136 = (f32[4096,512]{1,0:T(8,128)}, f32[4096,1024]{1,0:T(8,128)}) custom-call(s32[2,4096]{1,0:T(2,128)} %fusion.44.refs_0_, f32[4096,128]{1,0:T(8,128)} %constant_dynamic-update-slice_fusion.refs_1_, f32[4096,128]{1,0:T(8,128)} %constant_dynamic-update-slice_fusion.7.refs_2_, f32[4096,128]{1,0:T(8,128)} %collective-permute-done.12.refs_3_, ...), custom_call_target="tpu_custom_call" | custom-call | flops 40000000000 | bytes 33554432 | tf_op jit(solution)/shard_map/pallas_call | solution.py:205
  119.5 2.9 broadcast_multiply_fusion
  126.0 2.1 copy.56
  131.4 65.1 %shard_map.137 = (f32[512,256]{1,0:T(8,128)}, f32[512,256]{1,0:T(8,128)}, f32[4096,512]{1,0:T(8,128)}, f32[4096,512]{1,0:T(8,128)}) custom-call(f32[32,256]{1,0:T(8,128)} %bitcast.287, bf16[8,256,256]{2,1,0:T(8,128)(2,1)} %pad_maximum_fusion.3.qt4, bf16[8,256,128]{2,1,0:T(8,128)(2,1)} %pad_maximum_fusion.9.qs2, f32[8,64,256]{2,1,0:T(8,128)} %fusion.7.dot_, ...), custom_call_target="tpu_custom_call" | custom-call | flops 89999998976 | bytes 33554432 | tf_op jit(solution)/shard_map/pallas_call | solution.py:118
  196.6 3.0 fusion.13.qx_ref
  199.6 3.1 fusion.11.q_ref
  204.2 20.8 %shard_map.139 = f32[8192,128]{1,0:T(8,128)} custom-call(s32[512]{0:T(512)} %add_xor_fusion.at_ref, f32[512,512]{1,0:T(8,128)} %fusion.11.q_ref, f32[512,512]{1,0:T(8,128)} %fusion.9.o_ref, f32[4096,512]{1,0:T(8,128)} %get-tuple-element.23.dk_ref, f32[4096,512]{1,0:T(8,128)} %get-tuple-element.24.dv_ref, f32[4096,512]{1,0:T(8,128)} %get-tuple-element.20.x_ref), custom_call_target="tpu_custom_call" | custom-call | flops 20000000000 | bytes 29360128 | tf_op jit(solution)/shard_map/pallas_call | solution.py:303
  225.0 3.0 slice_bitcast_fusion.5
  228.0 40.7 %shard_map.138 = f32[16384,128]{1,0:T(8,128)} custom-call(s32[2,4096]{1,0:T(2,128)} %get-tuple-element.30.idx, s32[1]{0:T(128)} %bitcast.17.own_ref, f32[4096,512]{1,0:T(8,128)} %get-tuple-element.23.dk_ref, f32[4096,512]{1,0:T(8,128)} %get-tuple-element.24.dv_ref, bf16[1024,512]{1,0:T(8,128)(2,1)} %bitcast.261, bf16[1024,512]{1,0:T(8,128)(2,1)} %bitcast.260, ...), custom_call_target="tpu_custom_call" | custom-call | flops 40000000000 | bytes 25165824 | tf_op jit(solution)/shard_map/pallas_call | solution.py:261
  268.7 4.5 %slice_bitcast_fusion.1 = (f32[2,2,2,2,2,2,2,32,128]{8,7,6,5,4,3,2,1,0:T(8,128)S(1)}, f32[2,2,2,2,2,2,2,32,128]{8,7,6,5,4,3,2,1,0:T(8,128)S(1)}, f32[2,2,2,2,2,2...) fusion(f32[2,2,2,2,2,2,2,2,2,32,128]{10,9,8,7,6,5,4,3,2,1,0:T(8,128)} %bitcast.258), kind=kLoop, calls=%fused_computation.9 | loop fusion | bytes 16777216 | tf_op jit(solution)/shard_map/squeeze | solution.py:428
  274.5 4.8 %collective-permute-done.14 = f32[2,2,2,2,2,2,2,48,128]{8,7,6,5,4,3,2,1,0:T(8,128)S(1)} collective-permute-done((f32[2,2,2,2,2,2,2,48,128]{8,7,6,5,4,3,2,1,0:T(8,128)S(1)}, f32[2,2,2,2,2,2,2,48,128]{8,7,6,5,4,3,2,1,0:T(8,128)S(1)}, u32[]{:S(2)}, u32[]{:S(2)}) %collective-permute-start.14) | collective-permute-done | bytes 3145760 | tf_op jit(solution)/shard_map/ppermute | solution.py:361
  280.6 3.2 collective-permute-done.32
  285.8 13.3 %collective-permute-done.15 = f32[2,2,2,2,2,48,128]{6,5,4,3,2,1,0:T(8,128)S(1)} collective-permute-done((f32[2,2,2,2,2,48,128]{6,5,4,3,2,1,0:T(8,128)S(1)}, f32[2,2,2,2,2,48,128]{6,5,4,3,2,1,0:T(8,128)S(1)}, u32[]{:S(2)}, u32[]{:S(2)}) %collective-permute-start.15) | collective-permute-done | bytes 786464 | tf_op jit(solution)/shard_map/ppermute | solution.py:361
  301.6 2.0 collective-permute-done.33
  306.2 4.3 %collective-permute-done.18 = f32[2,2,2,2,48,128]{5,4,3,2,1,0:T(8,128)S(1)} collective-permute-done((f32[2,2,2,2,48,128]{5,4,3,2,1,0:T(8,128)S(1)}, f32[2,2,2,2,48,128]{5,4,3,2,1,0:T(8,128)S(1)}, u32[]{:S(2)}, u32[]{:S(2)}) %collective-permute-start.18) | collective-permute-done | bytes 393248 | tf_op jit(solution)/shard_map/ppermute | solution.py:361
  311.8 2.7 collective-permute-done.36
  316.1 6.8 %collective-permute-done.19 = f32[2,2,2,2,48,128]{5,4,0,3,2,1:T(8,128)S(1)} collective-permute-done((f32[2,2,2,2,48,128]{5,4,0,3,2,1:T(8,128)S(1)}, f32[2,2,2,2,48,128]{5,4,0,3,2,1:T(8,128)S(1)}, u32[]{:S(2)}, u32[]{:S(2)}) %collective-permute-start.19) | collective-permute-done | bytes 393248 | tf_op jit(solution)/shard_map/ppermute | solution.py:361
  324.0 1.6 collective-permute-start.38
  325.6 3.1 collective-permute-done.20
  330.3 2.4 collective-permute-done.21
  332.7 1.6 collective-permute-start.22
  335.1 1.8 collective-permute-done.22
  336.9 1.6 collective-permute-start.23
  340.8 1.6 collective-permute-done.41
  345.2 1.6 collective-permute-start.43
  346.8 1.8 collective-permute-done.25
  349.7 3.1 collective-permute-done.26
  359.8 3.4 collective-permute-done.30
  364.0 11.6 %collective-permute-start.31 = (f32[2048,128]{1,0:T(8,128)S(1)}, f32[2048,128]{1,0:T(8,128)}, u32[]{:S(2)}, u32[]{:S(2)}) collective-permute-start(f32[2048,128]{1,0:T(8,128)S(1)} %bitcast.262), channel_id=1, source_target_pairs={{0,1},{1,0},{2,3},{3,2},{4,5},{5,4},{6,7},{7,6},{8,9},{9,8},{10,11... | collective-permute-start | bytes 3145736 | tf_op jit(solution)/shard_map/ppermute | solution.py:361
  375.8 1.7 collective-permute-start.49
  380.0 5.6 %shard_map.140 = (f32[512,512]{1,0:T(8,128)}, f32[512,512]{1,0:T(8,128)}, f32[512,512]{1,0:T(8,128)}, f32[512,512]{1,0:T(8,128)}) custom-call(s32[512]{0:T(512)} %add_xor_fusion.at_ref, f32[2048,128]{1,0:T(8,128)} %bitcast.263, f32[2048,128]{1,0:T(8,128)} %collective-permute-done.31.refs_1_, f32[2048,128]{1,0:T(8,128)} %bitcast.265, ...), custom_call_target="tpu_custom_call" | custom-call | tf_op jit(solution)/shard_map/pallas_call | solution.py:341
  (206 shorter events, 67.9 us)
Async XLA Ops:
  3.1 40.2 %collective-permute-start.3 = (f32[512,128]{1,0:T(8,128)}, f32[512,128]{1,0:T(8,128)S(1)}, u32[]{:S(2)}, u32[]{:S(2)}) collective-permute-start(f32[512,128]{1,0:T(8,128)} %get-tuple-element.34), channel_id=1, source_target_pairs={{0,48},{16,0},{32,16},{48,32},{1,49},{17,1},{33,17},{49,33},{2,50}... | collective-permute-start | bytes 786440 | tf_op jit(solution)/shard_map/ppermute | solution.py:361
  6.4 39.6 %collective-permute-start.2 = (f32[512,128]{1,0:T(8,128)}, f32[512,128]{1,0:T(8,128)}, u32[]{:S(2)}, u32[]{:S(2)}) collective-permute-start(f32[512,128]{1,0:T(8,128)} %get-tuple-element.34), channel_id=1, source_target_pairs={{0,16},{16,32},{32,48},{48,0},{1,17},{17,33},{33,49},{49,1},{2,18}... | collective-permute-start | bytes 786440 | tf_op jit(solution)/shard_map/ppermute | solution.py:361
  6.4 14.3 %all-to-all-start = ((s32[8,1,128]{2,1,0:T(1,128)}), s32[8,1,128]{2,1,0:T(1,128)S(1)}, u32[]{:S(2)}, u32[]{:S(2)}) async-start(s32[8,1,128]{2,1,0:T(1,128)} %bitcast.2), calls=%async_computation | async-start | bytes 8192 | tf_op jit(solution)/shard_map/all_to_all | solution.py:518
  12.4 18.7 %collective-permute-start = (f32[256,128]{1,0:T(8,128)}, f32[256,128]{1,0:T(8,128)}, u32[]{:S(2)}, u32[]{:S(2)}) collective-permute-start(f32[256,128]{1,0:T(8,128)} %get-tuple-element.56), channel_id=1, source_target_pairs={{0,64},{64,2},{2,66},{66,0},{1,65},{65,3},{3,67},{67,1},{4,68},{68... | collective-permute-start | bytes 393224 | tf_op jit(solution)/shard_map/ppermute | solution.py:361
  13.9 17.2 %collective-permute-start.1 = (f32[256,128]{1,0:T(8,128)}, f32[256,128]{1,0:T(8,128)}, u32[]{:S(2)}, u32[]{:S(2)}) collective-permute-start(f32[256,128]{1,0:T(8,128)} %get-tuple-element.57), channel_id=1, source_target_pairs={{0,66},{64,0},{2,64},{66,2},{1,67},{65,1},{3,65},{67,3},{4,70},{68... | collective-permute-start | bytes 393224 | tf_op jit(solution)/shard_map/ppermute | solution.py:361
  23.6 14.8 %all-to-all-start.1 = ((s32[16,4,128]{2,1,0:T(4,128)}), s32[16,4,128]{2,1,0:T(4,128)S(1)}, u32[]{:S(2)}, u32[]{:S(2)}) async-start(s32[16,4,128]{2,1,0:T(4,128)} %broadcast_in_dim.48), calls=%async_computation.1 | async-start | bytes 65536 | tf_op jit(solution)/shard_map/all_to_all | solution.py:521
  38.4 21.7 %collective-permute-start.9 = (f32[1024,128]{1,0:T(8,128)}, f32[1024,128]{1,0:T(8,128)S(1)}, u32[]{:S(2)}, u32[]{:S(2)}) collective-permute-start(f32[1024,128]{1,0:T(8,128)} %pad_maximum_fusion.6), channel_id=1, source_target_pairs={{0,48},{16,0},{32,16},{48,32},{1,49},{17,1},{33,17},{49,33},{2,50}... | collective-permute-start | bytes 1572872 | tf_op jit(solution)/shard_map/ppermute | solution.py:361
  41.3 19.2 %collective-permute-start.8 = (f32[1024,128]{1,0:T(8,128)}, f32[1024,128]{1,0:T(8,128)S(1)}, u32[]{:S(2)}, u32[]{:S(2)}) collective-permute-start(f32[1024,128]{1,0:T(8,128)} %pad_maximum_fusion.6), channel_id=1, source_target_pairs={{0,16},{16,32},{32,48},{48,0},{1,17},{17,33},{33,49},{49,1},{2,18}... | collective-permute-start | bytes 1572872 | tf_op jit(solution)/shard_map/ppermute | solution.py:361
  43.3 12.0 %collective-permute-start.5 = (f32[256,128]{1,0:T(8,128)S(1)}, f32[256,128]{1,0:T(8,128)S(1)}, u32[]{:S(2)}, u32[]{:S(2)}) collective-permute-start(f32[256,128]{1,0:T(8,128)S(1)} %slice.249), channel_id=1, source_target_pairs={{0,48},{16,0},{32,16},{48,32},{1,49},{17,1},{33,17},{49,33},{2,50}... | collective-permute-start | bytes 393224 | tf_op jit(solution)/shard_map/ppermute | solution.py:361
  46.9 11.4 %collective-permute-start.4 = (f32[256,128]{1,0:T(8,128)S(1)}, f32[256,128]{1,0:T(8,128)S(1)}, u32[]{:S(2)}, u32[]{:S(2)}) collective-permute-start(f32[256,128]{1,0:T(8,128)S(1)} %slice.248), channel_id=1, source_target_pairs={{0,16},{16,32},{32,48},{48,0},{1,17},{17,33},{33,49},{49,1},{2,18}... | collective-permute-start | bytes 393224 | tf_op jit(solution)/shard_map/ppermute | solution.py:361
  48.1 15.4 %collective-permute-start.6 = (f32[1024,128]{1,0:T(8,128)S(1)}, f32[1024,128]{1,0:T(8,128)S(1)}, u32[]{:S(2)}, u32[]{:S(2)}) collective-permute-start(f32[1024,128]{1,0:T(8,128)S(1)} %pad_maximum_fusion.7), channel_id=1, source_target_pairs={{0,64},{64,2},{2,66},{66,0},{1,65},{65,3},{3,67},{67,1},{4,68},{68... | collective-permute-start | bytes 1572872 | tf_op jit(solution)/shard_map/ppermute | solution.py:361
  58.4 13.6 %collective-permute-start.7 = (f32[1024,128]{1,0:T(8,128)S(1)}, f32[1024,128]{1,0:T(8,128)S(1)}, u32[]{:S(2)}, u32[]{:S(2)}) collective-permute-start(f32[1024,128]{1,0:T(8,128)S(1)} %pad_maximum_fusion.8), channel_id=1, source_target_pairs={{0,66},{64,0},{2,64},{66,2},{1,67},{65,1},{3,65},{67,3},{4,70},{68... | collective-permute-start | bytes 1572872 | tf_op jit(solution)/shard_map/ppermute | solution.py:361
  60.1 8.4 %collective-permute-start.11 = (f32[512,128]{1,0:T(8,128)S(1)}, f32[512,128]{1,0:T(8,128)S(1)}, u32[]{:S(2)}, u32[]{:S(2)}) collective-permute-start(f32[512,128]{1,0:T(8,128)S(1)} %slice.251), channel_id=1, source_target_pairs={{0,48},{16,0},{32,16},{48,32},{1,49},{17,1},{33,17},{49,33},{2,50}... | collective-permute-start | bytes 786440 | tf_op jit(solution)/shard_map/ppermute | solution.py:361
  60.6 7.3 %collective-permute-start.10 = (f32[512,128]{1,0:T(8,128)S(1)}, f32[512,128]{1,0:T(8,128)S(1)}, u32[]{:S(2)}, u32[]{:S(2)}) collective-permute-start(f32[512,128]{1,0:T(8,128)S(1)} %slice.250), channel_id=1, source_target_pairs={{0,16},{16,32},{32,48},{48,0},{1,17},{17,33},{33,49},{49,1},{2,18}... | collective-permute-start | bytes 786440 | tf_op jit(solution)/shard_map/ppermute | solution.py:361
  69.3 13.2 %collective-permute-start.13 = (f32[4096,128]{1,0:T(8,128)}, f32[4096,128]{1,0:T(8,128)}, u32[]{:S(2)}, u32[]{:S(2)}) collective-permute-start(f32[4096,128]{1,0:T(8,128)} %constant_dynamic-update-slice_fusion.7.refs_2_), channel_id=1, source_target_pairs={{0,1},{1,0},{2,3},{3,2},{4,5},{5,4},{6,7},{7,6},{8,9},{9,8},{10,11... | collective-permute-start | bytes 6291464 | tf_op jit(solution)/shard_map/ppermute | solution.py:361
  72.8 9.7 %collective-permute-start.12 = (f32[4096,128]{1,0:T(8,128)}, f32[4096,128]{1,0:T(8,128)}, u32[]{:S(2)}, u32[]{:S(2)}) collective-permute-start(f32[4096,128]{1,0:T(8,128)} %constant_dynamic-update-slice_fusion.refs_1_), channel_id=1, source_target_pairs={{0,1},{1,0},{2,3},{3,2},{4,5},{5,4},{6,7},{7,6},{8,9},{9,8},{10,11... | collective-permute-start | bytes 6291464 | tf_op jit(solution)/shard_map/ppermute | solution.py:361
  273.6 5.7 %collective-permute-start.14 = (f32[2,2,2,2,2,2,2,48,128]{8,7,6,5,4,3,2,1,0:T(8,128)S(1)}, f32[2,2,2,2,2,2,2,48,128]{8,7,6,5,4,3,2,1,0:T(8,128)S(1)}, u32[]{:S(2)}, u32[]{:S(2)}) collective-permute-start(f32[2,2,2,2,2,2,2,48,128]{8,7,6,5,4,3,2,1,0:T(8,128)S(1)} %pad_maximum_fusion), channel_id=1, source_target_pairs={{0,1},{1,0},{2,3},{3,2},{4,5},{5,4},{6,7},{7,6},{8,9},{9,8},{10,11... | collective-permute-start | bytes 9437192 | tf_op jit(solution)/shard_map/ppermute | solution.py:361
  274.0 9.8 %collective-permute-start.32 = (f32[2,2,2,2,2,2,2,48,128]{8,7,6,5,4,3,2,1,0:T(8,128)S(1)}, f32[2,2,2,2,2,2,2,48,128]{8,7,6,5,4,3,2,1,0:T(8,128)S(1)}, u32[]{:S(2)}, u32[]{:S(2)}) collective-permute-start(f32[2,2,2,2,2,2,2,48,128]{8,7,6,5,4,3,2,1,0:T(8,128)S(1)} %pad_maximum_fusion.1), channel_id=1, source_target_pairs={{0,1},{1,0},{2,3},{3,2},{4,5},{5,4},{6,7},{7,6},{8,9},{9,8},{10,11... | collective-permute-start | bytes 9437192 | tf_op jit(solution)/shard_map/ppermute | solution.py:361
  280.1 19.1 %collective-permute-start.15 = (f32[2,2,2,2,2,48,128]{6,5,4,3,2,1,0:T(8,128)S(1)}, f32[2,2,2,2,2,48,128]{6,5,4,3,2,1,0:T(8,128)S(1)}, u32[]{:S(2)}, u32[]{:S(2)}) collective-permute-start(f32[2,2,2,2,2,48,128]{6,5,4,3,2,1,0:T(8,128)S(1)} %get-tuple-element.49), channel_id=1, source_target_pairs={{0,16},{16,0},{32,48},{48,32},{1,17},{17,1},{33,49},{49,33},{2,18}... | collective-permute-start | bytes 2359304 | tf_op jit(solution)/shard_map/ppermute | solution.py:361
  280.1 20.3 %collective-permute-start.17 = (f32[2,2,2,2,2,48,128]{6,5,4,3,2,1,0:T(8,128)S(1)}, f32[2,2,2,2,2,48,128]{6,5,4,3,2,1,0:T(8,128)S(1)}, u32[]{:S(2)}, u32[]{:S(2)}) collective-permute-start(f32[2,2,2,2,2,48,128]{6,5,4,3,2,1,0:T(8,128)S(1)} %get-tuple-element.50), channel_id=1, source_target_pairs={{0,48},{16,32},{32,16},{48,0},{1,49},{17,33},{33,17},{49,1},{2,50}... | collective-permute-start | bytes 2359304 | tf_op jit(solution)/shard_map/ppermute | solution.py:361
  284.5 19.1 %collective-permute-start.33 = (f32[2,2,2,2,2,48,128]{6,5,4,3,2,1,0:T(8,128)S(1)}, f32[2,2,2,2,2,48,128]{6,5,4,3,2,1,0:T(8,128)S(1)}, u32[]{:S(2)}, u32[]{:S(2)}) collective-permute-start(f32[2,2,2,2,2,48,128]{6,5,4,3,2,1,0:T(8,128)S(1)} %get-tuple-element.45), channel_id=1, source_target_pairs={{0,4},{4,0},{8,12},{12,8},{1,5},{5,1},{9,13},{13,9},{2,6},{6,2},{1... | collective-permute-start | bytes 2359304 | tf_op jit(solution)/shard_map/ppermute | solution.py:361
  284.9 19.9 %collective-permute-start.35 = (f32[2,2,2,2,2,48,128]{6,5,4,3,2,1,0:T(8,128)S(1)}, f32[2,2,2,2,2,48,128]{6,5,4,3,2,1,0:T(8,128)S(1)}, u32[]{:S(2)}, u32[]{:S(2)}) collective-permute-start(f32[2,2,2,2,2,48,128]{6,5,4,3,2,1,0:T(8,128)S(1)} %get-tuple-element.46), channel_id=1, source_target_pairs={{0,12},{4,8},{8,4},{12,0},{1,13},{5,9},{9,5},{13,1},{2,14},{6,10},... | collective-permute-start | bytes 2359304 | tf_op jit(solution)/shard_map/ppermute | solution.py:361
  300.7 9.7 %collective-permute-start.18 = (f32[2,2,2,2,48,128]{5,4,3,2,1,0:T(8,128)S(1)}, f32[2,2,2,2,48,128]{5,4,3,2,1,0:T(8,128)S(1)}, u32[]{:S(2)}, u32[]{:S(2)}) collective-permute-start(f32[2,2,2,2,48,128]{5,4,3,2,1,0:T(8,128)S(1)} %slice_bitcast_fusion.20), channel_id=1, source_target_pairs={{0,16},{16,0},{32,48},{48,32},{1,17},{17,1},{33,49},{49,33},{2,18}... | collective-permute-start | bytes 1179656 | tf_op jit(solution)/shard_map/ppermute | solution.py:361
  300.8 10.5 %collective-permute-start.16 = (f32[2,2,2,2,48,128]{5,4,3,2,1,0:T(8,128)S(1)}, f32[2,2,2,2,48,128]{5,4,3,2,1,0:T(8,128)S(1)}, u32[]{:S(2)}, u32[]{:S(2)}) collective-permute-start(f32[2,2,2,2,48,128]{5,4,3,2,1,0:T(8,128)S(1)} %slice_bitcast_fusion.22), channel_id=1, source_target_pairs={{0,48},{16,32},{32,16},{48,0},{1,49},{17,33},{33,17},{49,1},{2,50}... | collective-permute-start | bytes 1179656 | tf_op jit(solution)/shard_map/ppermute | solution.py:361
  305.0 9.4 %collective-permute-start.36 = (f32[2,2,2,2,48,128]{5,4,3,2,1,0:T(8,128)S(1)}, f32[2,2,2,2,48,128]{5,4,3,2,1,0:T(8,128)S(1)}, u32[]{:S(2)}, u32[]{:S(2)}) collective-permute-start(f32[2,2,2,2,48,128]{5,4,3,2,1,0:T(8,128)S(1)} %slice_bitcast_fusion.16), channel_id=1, source_target_pairs={{0,4},{4,0},{8,12},{12,8},{1,5},{5,1},{9,13},{13,9},{2,6},{6,2},{1... | collective-permute-start | bytes 1179656 | tf_op jit(solution)/shard_map/ppermute | solution.py:361
  305.2 10.4 %collective-permute-start.34 = (f32[2,2,2,2,48,128]{5,4,3,2,1,0:T(8,128)S(1)}, f32[2,2,2,2,48,128]{5,4,3,2,1,0:T(8,128)S(1)}, u32[]{:S(2)}, u32[]{:S(2)}) collective-permute-start(f32[2,2,2,2,48,128]{5,4,3,2,1,0:T(8,128)S(1)} %slice_bitcast_fusion.18), channel_id=1, source_target_pairs={{0,12},{4,8},{8,4},{12,0},{1,13},{5,9},{9,5},{13,1},{2,14},{6,10},... | collective-permute-start | bytes 1179656 | tf_op jit(solution)/shard_map/ppermute | solution.py:361
  311.4 11.4 %collective-permute-start.19 = (f32[2,2,2,2,48,128]{5,4,0,3,2,1:T(8,128)S(1)}, f32[2,2,2,2,48,128]{5,4,0,3,2,1:T(8,128)S(1)}, u32[]{:S(2)}, u32[]{:S(2)}) collective-permute-start(f32[2,2,2,2,48,128]{5,4,0,3,2,1:T(8,128)S(1)} %fusion.29), channel_id=1, source_target_pairs={{0,4},{4,0},{8,12},{12,8},{1,5},{5,1},{9,13},{13,9},{2,6},{6,2},{1... | collective-permute-start | bytes 1179656 | tf_op jit(solution)/shard_map/ppermute | solution.py:361
  315.6 8.3 %collective-permute-start.37 = (f32[2,2,2,2,48,128]{5,4,3,2,1,0:T(8,128)S(1)}, f32[2,2,2,2,48,128]{5,4,3,2,1,0:T(8,128)S(1)}, u32[]{:S(2)}, u32[]{:S(2)}) collective-permute-start(f32[2,2,2,2,48,128]{5,4,3,2,1,0:T(8,128)S(1)} %fusion.24), channel_id=1, source_target_pairs={{0,64},{64,0},{2,66},{66,2},{1,65},{65,1},{3,67},{67,3},{4,68},{68... | collective-permute-start | bytes 1179656 | tf_op jit(solution)/shard_map/ppermute | solution.py:361
  322.9 5.8 %collective-permute-start.20 = (f32[2,2,2,48,128]{4,3,0,2,1:T(8,128)S(1)}, f32[2,2,2,48,128]{4,3,0,2,1:T(8,128)S(1)}, u32[]{:S(2)}, u32[]{:S(2)}) collective-permute-start(f32[2,2,2,48,128]{4,3,0,2,1:T(8,128)S(1)} %slice_bitcast_fusion.26), channel_id=1, source_target_pairs={{0,12},{4,8},{8,4},{12,0},{1,13},{5,9},{9,5},{13,1},{2,14},{6,10},... | collective-permute-start | bytes 589832 | tf_op jit(solution)/shard_map/ppermute | solution.py:361
  324.0 6.1 %collective-permute-start.38 = (f32[2,2,2,48,128]{4,3,2,1,0:T(8,128)S(1)}, f32[2,2,2,48,128]{4,3,2,1,0:T(8,128)S(1)}, u32[]{:S(2)}, u32[]{:S(2)}) collective-permute-start(f32[2,2,2,48,128]{4,3,2,1,0:T(8,128)S(1)} %slice_bitcast_fusion.24), channel_id=1, source_target_pairs={{0,66},{64,2},{2,64},{66,0},{1,67},{65,3},{3,65},{67,1},{4,70},{68... | collective-permute-start | bytes 589832 | tf_op jit(solution)/shard_map/ppermute | solution.py:361
  330.2 4.1 %collective-permute-start.39 = (f32[2,2,48,128]{3,2,1,0:T(8,128)S(1)}, f32[2,2,48,128]{3,2,1,0:T(8,128)S(1)}, u32[]{:S(2)}, u32[]{:S(2)}) collective-permute-start(f32[2,2,48,128]{3,2,1,0:T(8,128)S(1)} %slice_bitcast_fusion.28), channel_id=1, source_target_pairs={{0,16},{16,0},{32,48},{48,32},{1,17},{17,1},{33,49},{49,33},{2,18}... | collective-permute-start | bytes 294920 | tf_op jit(solution)/shard_map/ppermute | solution.py:361
  332.7 4.2 %collective-permute-start.22 = (f32[2,48,128]{2,1,0:T(8,128)S(1)}, f32[2,48,128]{2,1,0:T(8,128)S(1)}, u32[]{:S(2)}, u32[]{:S(2)}) collective-permute-start(f32[2,48,128]{2,1,0:T(8,128)S(1)} %slice_bitcast_fusion.34), channel_id=1, source_target_pairs={{0,66},{64,2},{2,64},{66,0},{1,67},{65,3},{3,65},{67,1},{4,70},{68... | collective-permute-start | bytes 147464 | tf_op jit(solution)/shard_map/ppermute | solution.py:361
  334.3 4.2 %collective-permute-start.40 = (f32[2,48,128]{2,1,0:T(8,128)S(1)}, f32[2,48,128]{2,1,0:T(8,128)S(1)}, u32[]{:S(2)}, u32[]{:S(2)}) collective-permute-start(f32[2,48,128]{2,1,0:T(8,128)S(1)} %slice_bitcast_fusion.32), channel_id=1, source_target_pairs={{0,48},{16,32},{32,16},{48,0},{1,49},{17,33},{33,17},{49,1},{2,50}... | collective-permute-start | bytes 147464 | tf_op jit(solution)/shard_map/ppermute | solution.py:361
  336.9 3.9 %collective-permute-start.23 = (f32[2,16,128]{2,1,0:T(8,128)S(1)}, f32[2,16,128]{2,1,0:T(8,128)S(1)}, u32[]{:S(2)}, u32[]{:S(2)}) collective-permute-start(f32[2,16,128]{2,1,0:T(8,128)S(1)} %get-tuple-element.85), channel_id=1, source_target_pairs={{0,66},{64,2},{2,64},{66,0},{1,67},{65,3},{3,65},{67,1},{4,70},{68... | collective-permute-start | bytes 49160 | tf_op jit(solution)/shard_map/ppermute | solution.py:361
  343.9 4.7 %collective-permute-start.25 = (f32[2,2,2,16,128]{4,3,0,2,1:T(8,128)S(1)}, f32[2,2,2,16,128]{4,3,0,2,1:T(8,128)S(1)}, u32[]{:S(2)}, u32[]{:S(2)}) collective-permute-start(f32[2,2,2,16,128]{4,3,0,2,1:T(8,128)S(1)} %get-tuple-element.81), channel_id=1, source_target_pairs={{0,12},{4,8},{8,4},{12,0},{1,13},{5,9},{9,5},{13,1},{2,14},{6,10},... | collective-permute-start | bytes 196616 | tf_op jit(solution)/shard_map/ppermute | solution.py:361
  345.2 4.4 %collective-permute-start.43 = (f32[2,2,2,16,128]{4,3,2,1,0:T(8,128)S(1)}, f32[2,2,2,16,128]{4,3,2,1,0:T(8,128)S(1)}, u32[]{:S(2)}, u32[]{:S(2)}) collective-permute-start(f32[2,2,2,16,128]{4,3,2,1,0:T(8,128)S(1)} %get-tuple-element.79), channel_id=1, source_target_pairs={{0,66},{64,2},{2,64},{66,0},{1,67},{65,3},{3,65},{67,1},{4,70},{68... | collective-permute-start | bytes 196616 | tf_op jit(solution)/shard_map/ppermute | solution.py:361
  348.6 4.2 %collective-permute-start.26 = (f32[2,2,2,2,16,128]{5,4,0,3,2,1:T(8,128)S(1)}, f32[2,2,2,2,16,128]{5,4,0,3,2,1:T(8,128)S(1)}, u32[]{:S(2)}, u32[]{:S(2)}) collective-permute-start(f32[2,2,2,2,16,128]{5,4,0,3,2,1:T(8,128)S(1)} %get-tuple-element.77), channel_id=1, source_target_pairs={{0,4},{4,0},{8,12},{12,8},{1,5},{5,1},{9,13},{13,9},{2,6},{6,2},{1... | collective-permute-start | bytes 393224 | tf_op jit(solution)/shard_map/ppermute | solution.py:361
  349.6 4.0 %collective-permute-start.44 = (f32[2,2,2,2,16,128]{5,4,3,2,1,0:T(8,128)S(1)}, f32[2,2,2,2,16,128]{5,4,3,2,1,0:T(8,128)S(1)}, u32[]{:S(2)}, u32[]{:S(2)}) collective-permute-start(f32[2,2,2,2,16,128]{5,4,3,2,1,0:T(8,128)S(1)} %get-tuple-element.75), channel_id=1, source_target_pairs={{0,64},{64,0},{2,66},{66,2},{1,65},{65,1},{3,67},{67,3},{4,68},{68... | collective-permute-start | bytes 393224 | tf_op jit(solution)/shard_map/ppermute | solution.py:361
  352.8 3.9 %collective-permute-start.29 = (f32[2,2,2,2,16,128]{5,4,3,2,1,0:T(8,128)S(1)}, f32[2,2,2,2,16,128]{5,4,3,2,1,0:T(8,128)S(1)}, u32[]{:S(2)}, u32[]{:S(2)}) collective-permute-start(f32[2,2,2,2,16,128]{5,4,3,2,1,0:T(8,128)S(1)} %bitcast.271), channel_id=1, source_target_pairs={{0,16},{16,0},{32,48},{48,32},{1,17},{17,1},{33,49},{49,33},{2,18}... | collective-permute-start | bytes 393224 | tf_op jit(solution)/shard_map/ppermute | solution.py:361
  352.9 5.4 %collective-permute-start.27 = (f32[2,2,2,2,16,128]{5,4,3,2,1,0:T(8,128)S(1)}, f32[2,2,2,2,16,128]{5,4,3,2,1,0:T(8,128)S(1)}, u32[]{:S(2)}, u32[]{:S(2)}) collective-permute-start(f32[2,2,2,2,16,128]{5,4,3,2,1,0:T(8,128)S(1)} %bitcast.269), channel_id=1, source_target_pairs={{0,48},{16,32},{32,16},{48,0},{1,49},{17,33},{33,17},{49,1},{2,50}... | collective-permute-start | bytes 393224 | tf_op jit(solution)/shard_map/ppermute | solution.py:361
  353.6 4.8 %collective-permute-start.47 = (f32[2,2,2,2,16,128]{5,4,3,2,1,0:T(8,128)S(1)}, f32[2,2,2,2,16,128]{5,4,3,2,1,0:T(8,128)S(1)}, u32[]{:S(2)}, u32[]{:S(2)}) collective-permute-start(f32[2,2,2,2,16,128]{5,4,3,2,1,0:T(8,128)S(1)} %bitcast.270), channel_id=1, source_target_pairs={{0,4},{4,0},{8,12},{12,8},{1,5},{5,1},{9,13},{13,9},{2,6},{6,2},{1... | collective-permute-start | bytes 393224 | tf_op jit(solution)/shard_map/ppermute | solution.py:361
  354.4 5.3 %collective-permute-start.45 = (f32[2,2,2,2,16,128]{5,4,3,2,1,0:T(8,128)S(1)}, f32[2,2,2,2,16,128]{5,4,3,2,1,0:T(8,128)S(1)}, u32[]{:S(2)}, u32[]{:S(2)}) collective-permute-start(f32[2,2,2,2,16,128]{5,4,3,2,1,0:T(8,128)S(1)} %bitcast.268), channel_id=1, source_target_pairs={{0,12},{4,8},{8,4},{12,0},{1,13},{5,9},{9,5},{13,1},{2,14},{6,10},... | collective-permute-start | bytes 393224 | tf_op jit(solution)/shard_map/ppermute | solution.py:361
  356.8 6.5 %collective-permute-start.30 = (f32[2,2,2,2,2,16,128]{6,5,0,4,3,2,1:T(8,128)S(1)}, f32[2,2,2,2,2,16,128]{6,5,0,4,3,2,1:T(8,128)S(1)}, u32[]{:S(2)}, u32[]{:S(2)}) collective-permute-start(f32[2,2,2,2,2,16,128]{6,5,0,4,3,2,1:T(8,128)S(1)} %get-tuple-element.73), channel_id=1, source_target_pairs={{0,48},{16,32},{32,16},{48,0},{1,49},{17,33},{33,17},{49,1},{2,50}... | collective-permute-start | bytes 786440 | tf_op jit(solution)/shard_map/ppermute | solution.py:361
  358.4 5.3 %collective-permute-start.28 = (f32[2,2,2,2,2,16,128]{6,5,0,4,3,2,1:T(8,128)S(1)}, f32[2,2,2,2,2,16,128]{6,5,0,4,3,2,1:T(8,128)S(1)}, u32[]{:S(2)}, u32[]{:S(2)}) collective-permute-start(f32[2,2,2,2,2,16,128]{6,5,0,4,3,2,1:T(8,128)S(1)} %get-tuple-element.69), channel_id=1, source_target_pairs={{0,16},{16,0},{32,48},{48,32},{1,17},{17,1},{33,49},{49,33},{2,18}... | collective-permute-start | bytes 786440 | tf_op jit(solution)/shard_map/ppermute | solution.py:361
  358.5 17.1 %collective-permute-start.48 = (f32[2,2,2,2,2,16,128]{6,5,4,3,2,1,0:T(8,128)S(1)}, f32[2,2,2,2,2,16,128]{6,5,4,3,2,1,0:T(8,128)S(1)}, u32[]{:S(2)}, u32[]{:S(2)}) collective-permute-start(f32[2,2,2,2,2,16,128]{6,5,4,3,2,1,0:T(8,128)S(1)} %get-tuple-element.67), channel_id=1, source_target_pairs={{0,12},{4,8},{8,4},{12,0},{1,13},{5,9},{9,5},{13,1},{2,14},{6,10},... | collective-permute-start | bytes 786440 | tf_op jit(solution)/shard_map/ppermute | solution.py:361
  359.7 15.9 %collective-permute-start.46 = (f32[2,2,2,2,2,16,128]{6,5,4,3,2,1,0:T(8,128)S(1)}, f32[2,2,2,2,2,16,128]{6,5,4,3,2,1,0:T(8,128)S(1)}, u32[]{:S(2)}, u32[]{:S(2)}) collective-permute-start(f32[2,2,2,2,2,16,128]{6,5,4,3,2,1,0:T(8,128)S(1)} %get-tuple-element.63), channel_id=1, source_target_pairs={{0,4},{4,0},{8,12},{12,8},{1,5},{5,1},{9,13},{13,9},{2,6},{6,2},{1... | collective-permute-start | bytes 786440 | tf_op jit(solution)/shard_map/ppermute | solution.py:361
  364.0 15.6 %collective-permute-start.31 = (f32[2048,128]{1,0:T(8,128)S(1)}, f32[2048,128]{1,0:T(8,128)}, u32[]{:S(2)}, u32[]{:S(2)}) collective-permute-start(f32[2048,128]{1,0:T(8,128)S(1)} %bitcast.262), channel_id=1, source_target_pairs={{0,1},{1,0},{2,3},{3,2},{4,5},{5,4},{6,7},{7,6},{8,9},{9,8},{10,11... | collective-permute-start | bytes 3145736 | tf_op jit(solution)/shard_map/ppermute | solution.py:361
  375.8 4.1 %collective-permute-start.49 = (f32[2048,128]{1,0:T(8,128)S(1)}, f32[2048,128]{1,0:T(8,128)}, u32[]{:S(2)}, u32[]{:S(2)}) collective-permute-start(f32[2048,128]{1,0:T(8,128)S(1)} %bitcast.264), channel_id=1, source_target_pairs={{0,1},{1,0},{2,3},{3,2},{4,5},{5,4},{6,7},{7,6},{8,9},{9,8},{10,11... | collective-permute-start | bytes 3145736 | tf_op jit(solution)/shard_map/ppermute | solution.py:361
  (20 other events, 328.4 us)
